TPU v7x, 32 devices: a whole 2x2x4 slice. The times are simulated.
32 devices in a mesh: dp: 2 (over y), expert: 16 (over z, x, core).
Axes of the slice: x: 2, y: 2, z: 4, core: 2. Of those that a mesh axis runs over, the one named last changes fastest.
Arguments:
- tokens: bfloat16 [4096, 2048], P(('dp', 'expert')), may hold values from -6 to 6
- attn_gain: bfloat16 [2048], P(('dp', 'expert')), may hold values from 0.25 to 1.75
- q_gain: bfloat16 [2048], P(('dp', 'expert')), may hold values from 0.25 to 1.75
- k_gain: bfloat16 [2048], P(('dp', 'expert')), may hold values from 0.25 to 1.75
- ffn_gain: bfloat16 [2048], P(('dp', 'expert')), may hold values from 0.25 to 1.75
- w_query: bfloat16 [2048, 2048], P(('dp', 'expert')), may hold values from -0.125 to 0.125
- w_key: bfloat16 [2048, 2048], P(('dp', 'expert')), may hold values from -0.125 to 0.125
- w_value: bfloat16 [2048, 2048], P(('dp', 'expert')), may hold values from -0.125 to 0.125
- w_out: bfloat16 [2048, 2048], P(('dp', 'expert')), may hold values from -5 to 5
- router: bfloat16 [2048, 16], P(('dp', 'expert')), may hold values from -0.0625 to 0.0625
- w_gate: bfloat16 [16, 2048, 1024], P('expert', 'dp'), may hold values from -0.125 to 0.125
- w_up: bfloat16 [16, 2048, 1024], P('expert', 'dp'), may hold values from -0.125 to 0.125
- w_down: bfloat16 [16, 1024, 2048], P('expert', 'dp'), may hold values from -4 to 4
- cotangent: bfloat16 [4096, 2048], P(('dp', 'expert')), may hold values from -6 to 6
- routes: int32 [4096, 8], P(('dp', 'expert')), may hold values from 0 to 15, all different within a row; in each aligned block of 128 rows (0 to 127, 128 to 255, ...) at most 96 rows name the same one
- parents: int32 [32], replicated, may hold values from -1 to 30, as said below
Outputs:
- output: bfloat16 [4096, 2048], P(('dp', 'expert'))
- grad_tokens: float32 [4096, 2048], P(('dp', 'expert'))
- grad_attn_gain: float32 [2048], P(('dp', 'expert'))
- grad_q_gain: float32 [2048], P(('dp', 'expert'))
- grad_k_gain: float32 [2048], P(('dp', 'expert'))
- grad_ffn_gain: float32 [2048], P(('dp', 'expert'))
- grad_w_query: float32 [2048, 2048], P(('dp', 'expert'))
- grad_w_key: float32 [2048, 2048], P(('dp', 'expert'))
- grad_w_value: float32 [2048, 2048], P(('dp', 'expert'))
- grad_w_out: float32 [2048, 2048], P(('dp', 'expert'))
- grad_router: float32 [2048, 16], P(('dp', 'expert'))
- grad_w_gate: float32 [16, 2048, 1024], P('expert', 'dp')
- grad_w_up: float32 [16, 2048, 1024], P('expert', 'dp')
- grad_w_down: float32 [16, 1024, 2048], P('expert', 'dp')
Inputs may be any that keep to these rules, and one draw needn't show every extreme that they name: `routes`: no expert is named by more than 96 of the 128 rows of one device, and 96 is reached. Segments come in runs of 16, one tree a run. parents[s] is -1 where s is a multiple of 16; the last segment of a run has parent s - 1; otherwise it is one of s - 1, s - 2, s - 3 that is not before the run's first segment.
All inputs are finite; a program needn't handle non-finite values.
Results may differ from a plain program's by a relative error of at most 0.04.
Values may be sent and summed in bfloat16 or wider, within the bound.
A program may use at most 384 MiB of HBM per device.

v0:
```python
import math

import jax
import jax.numpy as jnp
from jax import lax
from jax.sharding import PartitionSpec as P

HEAD_DIM = 128


EPSILON = 1e-05
THETA = 10000.0
NEGATIVE = -1e30
HIGHEST = lax.Precision.HIGHEST


def times_transposed(matrix_left, matrix_right):
    return lax.dot_general(
        matrix_left, matrix_right, (((1,), (1,)), ((), ())), preferred_element_type=jnp.float32
    )


def transposed_times(matrix_left, matrix_right):
    return lax.dot_general(
        matrix_left, matrix_right, (((0,), (0,)), ((), ())), preferred_element_type=jnp.float32
    )


def inverse_rms(values):
    return lax.rsqrt(jnp.mean(values * values, axis=-1, keepdims=True) + EPSILON)


def norm_backward(values, scale_inv, gain_values, upstream):
    weighted = upstream * gain_values
    gain_grad = jnp.sum(upstream * values * scale_inv, axis=0)
    input_grad = scale_inv * weighted - values * scale_inv**3 * jnp.mean(
        weighted * values, axis=-1, keepdims=True
    )
    return (input_grad, gain_grad)


def rotate(values, positions, direction):
    row_count, model_width = values.shape
    head_count = model_width // HEAD_DIM
    half_dim = HEAD_DIM // 2
    frequencies = THETA ** (-2.0 * jnp.arange(half_dim, dtype=jnp.float32) / HEAD_DIM)
    angles = positions[:, None] * frequencies[None, :]
    cosine = jnp.cos(angles)[:, None, :]
    sine = direction * jnp.sin(angles)[:, None, :]
    split_heads = values.reshape(row_count, head_count, HEAD_DIM)
    first_half = split_heads[..., :half_dim]
    second_half = split_heads[..., half_dim:]
    turned = jnp.concatenate(
        [first_half * cosine - second_half * sine, second_half * cosine + first_half * sine],
        axis=-1,
    )
    return turned.reshape(row_count, model_width)


def ancestry(parents):
    segment_count = parents.shape[0]
    labels = jnp.arange(segment_count, dtype=jnp.int32)
    reach_table = (parents[:, None] == labels[None, :]).astype(jnp.float32)
    for doubling in range(segment_count.bit_length()):
        product = jnp.dot(
            reach_table, reach_table, precision=HIGHEST, preferred_element_type=jnp.float32
        )
        reach_table = jnp.minimum(reach_table + product, 1.0)
    return reach_table


def blockwise(block_step, carried, arrays):
    piece_rows = arrays[0].shape[0]
    block_rows = math.gcd(piece_rows, 512)

    def block_turn(block_index, running):
        offset = block_index * block_rows
        block_parts = tuple(
            (lax.dynamic_slice_in_dim(member, offset, block_rows, 0) for member in arrays)
        )
        return block_step(running, block_parts, offset)

    return lax.fori_loop(0, piece_rows // block_rows, block_turn, carried)


def per_device(
    tokens,
    attn_gain,
    q_gain,
    k_gain,
    ffn_gain,
    w_query,
    w_key,
    w_value,
    w_out,
    router,
    w_gate,
    w_up,
    w_down,
    cotangent,
    routes,
    parents,
):
    row_count, model_width = tokens.shape
    head_count = model_width // HEAD_DIM
    score_scale = HEAD_DIM ** (-0.5)
    group_size = lax.axis_size("expert")
    dp_offset = lax.axis_index("dp") * group_size
    my_segment = dp_offset + lax.axis_index("expert")
    segment_count = parents.shape[0]
    labels = jnp.arange(segment_count, dtype=jnp.int32)
    reach_table = ancestry(parents)
    seen_table = reach_table + jnp.eye(segment_count, dtype=jnp.float32)
    own_pick = (labels == my_segment).astype(jnp.float32)
    seen_row = jnp.sum(own_pick[:, None] * seen_table, axis=0)
    seen_column = jnp.sum(seen_table * own_pick[None, :], axis=1)
    seg_depth = jnp.sum(own_pick[:, None] * reach_table)
    offsets = jnp.arange(row_count, dtype=jnp.int32)
    positions = seg_depth * row_count + offsets.astype(jnp.float32)

    def lookup(lookup_table, segment_ids):
        hits = jnp.where(segment_ids[:, None] == labels[None, :], lookup_table[None, :], 0.0)
        return jnp.sum(hits, axis=1) > 0.5

    def key_mask(first_row, piece_rows):
        row_index = first_row + jnp.arange(piece_rows, dtype=jnp.int32)
        key_segment = dp_offset + row_index // row_count
        causal = (key_segment[None, :] != my_segment) | (
            (row_index % row_count)[None, :] <= offsets[:, None]
        )
        return lookup(seen_row, key_segment)[None, :] & causal

    def query_mask(first_row, piece_rows):
        row_index = first_row + jnp.arange(piece_rows, dtype=jnp.int32)
        query_segment = dp_offset + row_index // row_count
        causal = (query_segment[:, None] != my_segment) | (
            offsets[None, :] <= (row_index % row_count)[:, None]
        )
        return lookup(seen_column, query_segment)[:, None] & causal

    query_w, key_w, value_w, out_w, router_w, attn_g, query_g, key_g, ffn_g = (
        lax.all_gather(w_query, ("dp", "expert"), axis=0, tiled=True),
        lax.all_gather(w_key, ("dp", "expert"), axis=0, tiled=True),
        lax.all_gather(w_value, ("dp", "expert"), axis=0, tiled=True),
        lax.all_gather(w_out, ("dp", "expert"), axis=0, tiled=True),
        lax.all_gather(router, ("dp", "expert"), axis=0, tiled=True),
        lax.all_gather(attn_gain, ("dp", "expert"), axis=0, tiled=True),
        lax.all_gather(q_gain, ("dp", "expert"), axis=0, tiled=True),
        lax.all_gather(k_gain, ("dp", "expert"), axis=0, tiled=True),
        lax.all_gather(ffn_gain, ("dp", "expert"), axis=0, tiled=True),
    )
    attn_gf = attn_g.astype(jnp.float32)
    query_gf = query_g.astype(jnp.float32)
    key_gf = key_g.astype(jnp.float32)
    ffn_gf = ffn_g.astype(jnp.float32)
    gate_full, up_full, down_full = (
        lax.all_gather(w_gate, "dp", axis=1, tiled=True),
        lax.all_gather(w_up, "dp", axis=1, tiled=True),
        lax.all_gather(w_down, "dp", axis=1, tiled=True),
    )
    token_f = tokens.astype(jnp.float32)
    first_scale = inverse_rms(token_f)
    normed = (token_f * first_scale * attn_gf).astype(jnp.bfloat16)
    query_pre = jnp.dot(normed, query_w, preferred_element_type=jnp.float32)
    key_pre = jnp.dot(normed, key_w, preferred_element_type=jnp.float32)
    value_rows = jnp.dot(normed, value_w, preferred_element_type=jnp.float32).astype(jnp.bfloat16)
    query_scale = inverse_rms(query_pre)
    key_scale = inverse_rms(key_pre)
    queries = rotate(query_pre * query_scale * query_gf, positions, 1.0).astype(jnp.bfloat16)
    key_rows = rotate(key_pre * key_scale * key_gf, positions, 1.0).astype(jnp.bfloat16)
    query_heads = queries.reshape(row_count, head_count, HEAD_DIM)
    key_heads = key_rows.reshape(row_count, head_count, HEAD_DIM)
    value_heads = value_rows.reshape(row_count, head_count, HEAD_DIM)

    def forward_block(carried, block_parts, first_row):
        key_block, value_block = block_parts
        piece_rows = key_block.shape[0]
        allowed = key_mask(first_row, piece_rows)
        running_max, running_sum, running_out = carried
        raw_scores = (
            jnp.einsum(
                "qhd,khd->hqk",
                query_heads,
                key_block.reshape(piece_rows, head_count, HEAD_DIM),
                preferred_element_type=jnp.float32,
            )
            * score_scale
        )
        scores = jnp.where(allowed[None], raw_scores, NEGATIVE)
        new_max = jnp.maximum(running_max, jnp.max(scores, axis=-1))
        factor = jnp.exp(running_max - new_max)
        weights = jnp.where(allowed[None], jnp.exp(scores - new_max[:, :, None]), 0.0)
        weights_low = weights.astype(jnp.bfloat16)
        value_part = value_block.reshape(piece_rows, head_count, HEAD_DIM)
        running_out = running_out * factor.T[:, :, None] + jnp.einsum(
            "hqk,khd->qhd", weights_low, value_part, preferred_element_type=jnp.float32
        )
        return (new_max, running_sum * factor + jnp.sum(weights, axis=-1), running_out)

    start_state = (
        jnp.full((head_count, row_count), NEGATIVE, jnp.float32),
        jnp.zeros((head_count, row_count), jnp.float32),
        jnp.zeros((row_count, head_count, HEAD_DIM), jnp.float32),
    )
    running_max, running_sum, running_out = blockwise(
        forward_block,
        start_state,
        (
            lax.all_gather(key_rows, "expert", axis=0, tiled=True),
            lax.all_gather(value_rows, "expert", axis=0, tiled=True),
        ),
    )
    log_total = running_max + jnp.log(running_sum)
    attn_out = (running_out / running_sum.T[:, :, None]).reshape(row_count, model_width)
    mixed = attn_out.astype(jnp.bfloat16)
    residual = token_f + jnp.dot(mixed, out_w, preferred_element_type=jnp.float32)
    second_scale = inverse_rms(residual)
    normed_two = (residual * second_scale * ffn_gf).astype(jnp.bfloat16)
    logits = jnp.dot(normed_two, router_w, preferred_element_type=jnp.float32)
    router_probs = jax.nn.softmax(logits, axis=-1)
    expert_count = router_w.shape[1]
    top_count = routes.shape[1]
    local_experts = gate_full.shape[0]
    capacity = 3 * row_count * top_count // (2 * expert_count)
    expert_labels = jnp.arange(expert_count, dtype=jnp.int32)
    picked = (routes[:, :, None] == expert_labels[None, None, :]).astype(jnp.int32)
    flat_pick = picked.reshape(row_count * top_count, expert_count)
    slot_rank = jnp.sum((jnp.cumsum(flat_pick, axis=0) - 1) * flat_pick, axis=1)
    place = routes.reshape(-1) * capacity + slot_rank
    slot_labels = jnp.arange(expert_count * capacity, dtype=jnp.int32)
    matches = place[None, :] == slot_labels[:, None]
    filled = jnp.any(matches, axis=1)
    pair_labels = jnp.arange(row_count * top_count, dtype=jnp.int32)
    pair_index = jnp.sum(jnp.where(matches, pair_labels[None, :], 0), axis=1)
    gates = jnp.sum(picked.astype(jnp.float32) * router_probs[:, None, :], axis=-1)
    empty_value = jnp.zeros((), jnp.bfloat16)
    send_rows = jnp.where(
        filled[:, None], jnp.take(normed_two, pair_index // top_count, axis=0), empty_value
    ).reshape(expert_count, capacity, model_width)
    received = lax.all_to_all(send_rows, "expert", split_axis=0, concat_axis=0, tiled=True)
    slot_count = received.shape[1]
    grouped = received.reshape(group_size, local_experts, slot_count, model_width)
    gate_pre = jnp.einsum("secd,edf->secf", grouped, gate_full, preferred_element_type=jnp.float32)
    up_pre = jnp.einsum("secd,edf->secf", grouped, up_full, preferred_element_type=jnp.float32)
    hidden = (jax.nn.silu(gate_pre) * up_pre).astype(jnp.bfloat16)
    expert_out = jnp.einsum(
        "secf,efd->secd", hidden, down_full, preferred_element_type=jnp.float32
    ).astype(jnp.bfloat16)
    returned = lax.all_to_all(
        expert_out.reshape(group_size * local_experts, slot_count, model_width),
        "expert",
        split_axis=0,
        concat_axis=0,
        tiled=True,
    )
    hidden_width = gate_pre.shape[-1]
    returned, kept_rows, kept_gate, kept_up = (
        returned,
        received,
        gate_pre.reshape(group_size * local_experts, slot_count, hidden_width),
        up_pre.reshape(group_size * local_experts, slot_count, hidden_width),
    )
    pair_out = (
        jnp.take(returned.reshape(expert_count * capacity, model_width), place, axis=0)
        .reshape(row_count, top_count, model_width)
        .astype(jnp.float32)
    )
    layer_out = residual + jnp.sum(gates[:, :, None] * pair_out, axis=1)
    output = layer_out.astype(jnp.bfloat16)
    query_back, key_back, value_back, out_back, router_back = (
        lax.all_gather(w_query, ("dp", "expert"), axis=0, tiled=True),
        lax.all_gather(w_key, ("dp", "expert"), axis=0, tiled=True),
        lax.all_gather(w_value, ("dp", "expert"), axis=0, tiled=True),
        lax.all_gather(w_out, ("dp", "expert"), axis=0, tiled=True),
        lax.all_gather(router, ("dp", "expert"), axis=0, tiled=True),
    )
    out_grad = cotangent.astype(jnp.float32)
    gate_grad = jnp.sum(out_grad[:, None, :] * pair_out, axis=-1)
    pair_grad = (
        (gates[:, :, None] * out_grad[:, None, :])
        .astype(jnp.bfloat16)
        .reshape(row_count * top_count, model_width)
    )
    send_grads = jnp.where(
        filled[:, None], jnp.take(pair_grad, pair_index, axis=0), empty_value
    ).reshape(expert_count, capacity, model_width)
    received_grads = lax.all_to_all(send_grads, "expert", split_axis=0, concat_axis=0, tiled=True)
    grads_in = received_grads.reshape(group_size, local_experts, capacity, model_width)
    rows_in = kept_rows.reshape(group_size, local_experts, capacity, model_width)
    gate_in = kept_gate.reshape(group_size, local_experts, capacity, -1)
    up_in = kept_up.reshape(group_size, local_experts, capacity, -1)
    hidden_low = jnp.einsum(
        "secd,efd->secf", grads_in, down_full, preferred_element_type=jnp.float32
    ).astype(jnp.bfloat16)
    hidden_grad = lax.optimization_barrier(hidden_low).astype(jnp.float32)
    sigmoid_gate = jax.nn.sigmoid(gate_in)
    silu_gate = jax.nn.silu(gate_in)
    gate_pre_grad = (
        hidden_grad * up_in * sigmoid_gate * (1.0 + gate_in * (1.0 - sigmoid_gate))
    ).astype(jnp.bfloat16)
    up_pre_grad = (hidden_grad * silu_gate).astype(jnp.bfloat16)
    hidden_again = (silu_gate * up_in).astype(jnp.bfloat16)
    down_w_grad = jnp.einsum(
        "secf,secd->efd", hidden_again, grads_in, preferred_element_type=jnp.float32
    )
    gate_w_grad = jnp.einsum(
        "secd,secf->edf", rows_in, gate_pre_grad, preferred_element_type=jnp.float32
    )
    up_w_grad = jnp.einsum(
        "secd,secf->edf", rows_in, up_pre_grad, preferred_element_type=jnp.float32
    )
    row_grad = jnp.einsum(
        "secf,edf->secd", gate_pre_grad, gate_full, preferred_element_type=jnp.float32
    )
    row_grad = (
        row_grad
        + jnp.einsum("secf,edf->secd", up_pre_grad, up_full, preferred_element_type=jnp.float32)
    ).astype(jnp.bfloat16)
    returned_grads = lax.all_to_all(
        row_grad.reshape(group_size * local_experts, capacity, model_width),
        "expert",
        split_axis=0,
        concat_axis=0,
        tiled=True,
    )
    pair_input_grad = (
        jnp.take(returned_grads.reshape(expert_count * capacity, model_width), place, axis=0)
        .reshape(row_count, top_count, model_width)
        .astype(jnp.float32)
    )
    expert_input_grad = jnp.sum(pair_input_grad, axis=1)
    prob_grad = jnp.sum(picked.astype(jnp.float32) * gate_grad[:, :, None], axis=1)
    logit_grad = (
        router_probs * (prob_grad - jnp.sum(router_probs * prob_grad, axis=-1, keepdims=True))
    ).astype(jnp.bfloat16)
    router_grad = transposed_times(normed_two, logit_grad)
    normed_two_grad = expert_input_grad + times_transposed(logit_grad, router_back)
    residual_norm_grad, ffn_gain_grad = norm_backward(
        residual, second_scale, ffn_gf, normed_two_grad
    )
    residual_grad = out_grad + residual_norm_grad
    proj_grad = residual_grad.astype(jnp.bfloat16)
    out_w_grad = transposed_times(mixed, proj_grad)
    mixed_grad = times_transposed(proj_grad, out_back).astype(jnp.bfloat16)
    dout_heads = mixed_grad.reshape(row_count, head_count, HEAD_DIM)
    row_delta = jnp.sum(
        dout_heads.astype(jnp.float32) * attn_out.reshape(row_count, head_count, HEAD_DIM), axis=-1
    )
    own_delta = row_delta.T
    lse_rows = log_total.T
    lse_all, delta_all = (
        lax.all_gather(lse_rows, "expert", axis=0, tiled=True),
        lax.all_gather(row_delta, "expert", axis=0, tiled=True),
    )

    def backward_block(carried, block_parts, first_row):
        key_block, value_block, query_block, dout_block = block_parts
        piece_rows = key_block.shape[0]
        lse_block = lax.dynamic_slice_in_dim(lse_all, first_row, piece_rows, 0)
        delta_block = lax.dynamic_slice_in_dim(delta_all, first_row, piece_rows, 0)
        key_part = key_block.reshape(piece_rows, head_count, HEAD_DIM)
        value_part = value_block.reshape(piece_rows, head_count, HEAD_DIM)
        query_part = query_block.reshape(piece_rows, head_count, HEAD_DIM)
        dout_part = dout_block.reshape(piece_rows, head_count, HEAD_DIM)
        to_keys = key_mask(first_row, piece_rows)
        from_queries = query_mask(first_row, piece_rows)
        query_grad, key_grad, value_grad = carried
        raw_scores = (
            jnp.einsum("qhd,khd->hqk", query_heads, key_part, preferred_element_type=jnp.float32)
            * score_scale
        )
        weights = jnp.exp(jnp.where(to_keys[None], raw_scores - log_total[:, :, None], NEGATIVE))
        prob_part = jnp.einsum(
            "qhd,khd->hqk", dout_heads, value_part, preferred_element_type=jnp.float32
        )
        score_grad = (weights * (prob_part - own_delta[:, :, None])).astype(jnp.bfloat16)
        query_grad = (
            query_grad
            + jnp.einsum("hqk,khd->qhd", score_grad, key_part, preferred_element_type=jnp.float32)
            * score_scale
        )
        own_key_grad = key_grad
        own_value_grad = value_grad
        raw_scores = (
            jnp.einsum("qhd,khd->hqk", query_part, key_heads, preferred_element_type=jnp.float32)
            * score_scale
        )
        weights = jnp.exp(
            jnp.where(from_queries[None], raw_scores - lse_block.T[:, :, None], NEGATIVE)
        )
        prob_part = jnp.einsum(
            "qhd,khd->hqk", dout_part, value_heads, preferred_element_type=jnp.float32
        )
        score_grad = (weights * (prob_part - delta_block.T[:, :, None])).astype(jnp.bfloat16)
        own_key_grad = (
            own_key_grad
            + jnp.einsum("hqk,qhd->khd", score_grad, query_part, preferred_element_type=jnp.float32)
            * score_scale
        )
        weights_low = weights.astype(jnp.bfloat16)
        own_value_grad = own_value_grad + jnp.einsum(
            "hqk,qhd->khd", weights_low, dout_part, preferred_element_type=jnp.float32
        )
        return (query_grad, own_key_grad, own_value_grad)

    zero_heads = jnp.zeros((row_count, head_count, HEAD_DIM), jnp.float32)
    back_state = (zero_heads, zero_heads, zero_heads)
    query_acc, key_acc, value_acc = blockwise(
        backward_block,
        back_state,
        (
            lax.all_gather(key_rows, "expert", axis=0, tiled=True),
            lax.all_gather(value_rows, "expert", axis=0, tiled=True),
            lax.all_gather(queries, "expert", axis=0, tiled=True),
            lax.all_gather(mixed_grad, "expert", axis=0, tiled=True),
        ),
    )
    query_turned = rotate(query_acc.reshape(row_count, model_width), positions, -1.0)
    key_turned = rotate(key_acc.reshape(row_count, model_width), positions, -1.0)
    query_pre_grad, query_gain_grad = norm_backward(query_pre, query_scale, query_gf, query_turned)
    key_pre_grad, key_gain_grad = norm_backward(key_pre, key_scale, key_gf, key_turned)
    query_low = query_pre_grad.astype(jnp.bfloat16)
    key_low = key_pre_grad.astype(jnp.bfloat16)
    value_low = value_acc.reshape(row_count, model_width).astype(jnp.bfloat16)
    normed_grad = (
        times_transposed(query_low, query_back)
        + times_transposed(key_low, key_back)
        + times_transposed(value_low, value_back)
    )
    query_w_grad = transposed_times(normed, query_low)
    key_w_grad = transposed_times(normed, key_low)
    value_w_grad = transposed_times(normed, value_low)
    token_norm_grad, attn_gain_grad = norm_backward(token_f, first_scale, attn_gf, normed_grad)
    token_grad = residual_grad + token_norm_grad
    (
        grad_query,
        grad_key,
        grad_value,
        grad_out,
        grad_router,
        grad_attn,
        grad_qnorm,
        grad_knorm,
        grad_ffn,
    ) = (
        lax.psum_scatter(query_w_grad, ("dp", "expert"), scatter_dimension=0, tiled=True),
        lax.psum_scatter(key_w_grad, ("dp", "expert"), scatter_dimension=0, tiled=True),
        lax.psum_scatter(value_w_grad, ("dp", "expert"), scatter_dimension=0, tiled=True),
        lax.psum_scatter(out_w_grad, ("dp", "expert"), scatter_dimension=0, tiled=True),
        lax.psum_scatter(router_grad, ("dp", "expert"), scatter_dimension=0, tiled=True),
        lax.psum_scatter(attn_gain_grad, ("dp", "expert"), scatter_dimension=0, tiled=True),
        lax.psum_scatter(query_gain_grad, ("dp", "expert"), scatter_dimension=0, tiled=True),
        lax.psum_scatter(key_gain_grad, ("dp", "expert"), scatter_dimension=0, tiled=True),
        lax.psum_scatter(ffn_gain_grad, ("dp", "expert"), scatter_dimension=0, tiled=True),
    )
    grad_gate, grad_up, grad_down = (
        lax.psum_scatter(
            gate_w_grad.astype(jnp.bfloat16), "dp", scatter_dimension=1, tiled=True
        ).astype(jnp.float32),
        lax.psum_scatter(
            up_w_grad.astype(jnp.bfloat16), "dp", scatter_dimension=1, tiled=True
        ).astype(jnp.float32),
        lax.psum_scatter(
            down_w_grad.astype(jnp.bfloat16), "dp", scatter_dimension=1, tiled=True
        ).astype(jnp.float32),
    )
    return (
        output,
        token_grad,
        grad_attn,
        grad_qnorm,
        grad_knorm,
        grad_ffn,
        grad_query,
        grad_key,
        grad_value,
        grad_out,
        grad_router,
        grad_gate,
        grad_up,
        grad_down,
    )


def solution(mesh):
    in_specs = (
        P(("dp", "expert"), None),
        P(("dp", "expert")),
        P(("dp", "expert")),
        P(("dp", "expert")),
        P(("dp", "expert")),
        P(("dp", "expert"), None),
        P(("dp", "expert"), None),
        P(("dp", "expert"), None),
        P(("dp", "expert"), None),
        P(("dp", "expert"), None),
        P("expert", "dp", None),
        P("expert", "dp", None),
        P("expert", "dp", None),
        P(("dp", "expert"), None),
        P(("dp", "expert"), None),
        P(),
    )
    out_specs = (
        P(("dp", "expert"), None),
        P(("dp", "expert"), None),
        P(("dp", "expert")),
        P(("dp", "expert")),
        P(("dp", "expert")),
        P(("dp", "expert")),
        P(("dp", "expert"), None),
        P(("dp", "expert"), None),
        P(("dp", "expert"), None),
        P(("dp", "expert"), None),
        P(("dp", "expert"), None),
        P("expert", "dp", None),
        P("expert", "dp", None),
        P("expert", "dp", None),
    )
    return jax.shard_map(
        per_device, mesh=mesh, in_specs=in_specs, out_specs=out_specs, check_vma=False
    )
```

profile of v0, /device:TPU:4, one launch (start us, length us, event | category | flops | bytes accessed | tf_op | source)
XLA Modules:
  0.0 2452.0 jit_solution(4706277389638719787)
XLA Ops:
  13.7 42.0 %all-reduce.9 = (bf16[2048]{0:T(1024)(128)(2,1)S(1)}, bf16[2048]{0:T(1024)(128)(2,1)S(1)}, bf16[2048]{0:T(1024)(128)(2,1)S(1)}, bf16[2048]{0:T(1024)(128)(2,1)S(1)}) all-reduce(bf16[2048]{0:T(1024)(128)(2,1)S(1)} %dynamic-update-slice, bf16[2048]{0:T(1024)(128)(2,1)S(1)} %dynamic-update-slice.1, ...), channel_id=1, replica_groups=mesh['dp'=2,'expert'=16] {'dp','expert'}, use_global_device_ids=true, to_apply=%add | all-reduce | flops 8192 | bytes 32768
  57.5 33.1 %all-gather.19.cloned.1.call-done = bf16[2048,2048]{1,0:T(8,128)(2,1)} async-done(((bf16[64,2048]{1,0:T(8,128)(2,1)}), bf16[2048,2048]{1,0:T(8,128)(2,1)}) %all-gather.19.cloned.1.call-update) | async-done | bytes 8388624 | tf_op jit(solution)/shard_map/all_gather | solution.py:144
  90.7 5.7 convolution_convert_fusion.2
  99.6 70.0 %all-gather.17.cloned.1.call-done = bf16[2048,2048]{1,0:T(8,128)(2,1)} async-done(((bf16[64,2048]{1,0:T(8,128)(2,1)}), bf16[2048,2048]{1,0:T(8,128)(2,1)}) %all-gather.17.cloned.1.call-update) | async-done | bytes 8388624 | tf_op jit(solution)/shard_map/all_gather | solution.py:142
  169.6 4.8 multiply_reduce_fusion.8
  175.9 72.7 %all-gather.13.cloned.1.call-done = bf16[2048,2048]{1,0:T(8,128)(2,1)} async-done(((bf16[64,2048]{1,0:T(8,128)(2,1)}), bf16[2048,2048]{1,0:T(8,128)(2,1)}) %all-gather.13.cloned.1.call-update) | async-done | bytes 8388624 | tf_op jit(solution)/shard_map/all_gather | solution.py:143
  248.6 4.8 multiply_reduce_fusion.9
  266.8 57.9 %all-gather.21.cloned.1.call-done = bf16[2048,2048]{1,0:T(8,128)(2,1)} async-done(((bf16[128,2048]{1,0:T(8,128)(2,1)}), bf16[2048,2048]{1,0:T(8,128)(2,1)}) %all-gather.21.cloned.1.call-update) | async-done | bytes 8388624 | tf_op jit(solution)/shard_map/all_gather | solution.py:210
  324.7 12.4 copy.151
  337.1 66.6 %all-gather.15.cloned.1.call-done = bf16[2048,2048]{0,1:T(8,128)(2,1)} async-done(((bf16[128,2048]{0,1:T(8,128)(2,1)}), bf16[2048,2048]{0,1:T(8,128)(2,1)}) %all-gather.15.cloned.1.call-update) | async-done | bytes 8388624 | tf_op jit(solution)/shard_map/all_gather | solution.py:209
  403.7 51.5 %while.41 = (s32[]{:T(128)}, f32[16,128]{1,0:T(8,128)S(1)}, f32[16,128]{1,0:T(8,128)S(1)}, f32[128,16,128]{0,2,1:T(8,128)}, s32[]{:T(128)}, /*index=5*/f32[32]{0...) while((s32[]{:T(128)}, f32[16,128]{1,0:T(8,128)S(1)}, ...), condition=%wide.region_9.10_spmd.clone, body=%wide.region_5.9_spmd.clone.sunk | while | flops 551566848 | bytes 44972408 | solution.py:83
  456.7 25.3 %all-gather.23.cloned.1.call-done = bf16[2048,2048]{1,0:T(8,128)(2,1)} async-done(((bf16[64,2048]{1,0:T(8,128)(2,1)}), bf16[2048,2048]{1,0:T(8,128)(2,1)}) %all-gather.23.cloned.1.call-update) | async-done | bytes 8388624 | tf_op jit(solution)/shard_map/all_gather | solution.py:145
  482.0 4.7 multiply_reduce_fusion.7
  488.0 7.0 gather_fusion
  495.0 6.9 select_select_fusion.1
  508.2 57.0 %all-gather.27.cloned.1.call-done = bf16[1,2048,1024]{2,1,0:T(8,128)(2,1)} async-done(((bf16[1,1024,1024]{2,1,0:T(8,128)(2,1)}), bf16[1,2048,1024]{2,1,0:T(8,128)(2,1)}) %all-gather.27.cloned.1.call-update) | async-done | bytes 4194320 | tf_op jit(solution)/shard_map/all_gather | solution.py:158
  565.2 55.4 %all-to-all-done = bf16[16,96,2048]{2,1,0:T(8,128)(2,1)} async-done(((bf16[16,96,2048]{2,1,0:T(8,128)(2,1)}), bf16[16,96,2048]{2,1,0:T(8,128)(2,1)}, u32[]{:S(2)}, u32[]{:S(2)}) %all-to-all-start) | async-done | bytes 6291488 | tf_op jit(solution)/shard_map/all_to_all | solution.py:240
  620.6 11.7 fusion.90
  632.3 11.1 fusion.94
  649.1 32.1 %all-gather.29.cloned.1.call-done = bf16[1,1024,2048]{2,1,0:T(8,128)(2,1)} async-done(((bf16[1,512,2048]{2,1,0:T(8,128)(2,1)}), bf16[1,1024,2048]{2,1,0:T(8,128)(2,1)}) %all-gather.29.cloned.1.call-update) | async-done | bytes 4194320 | tf_op jit(solution)/shard_map/all_gather | solution.py:159
  681.2 11.2 convolution_convert_fusion
  692.4 6.0 all-to-all-start.1
  698.6 165.6 %all-gather = bf16[32,64,16]{1,2,0:T(8,128)(2,1)S(1)} all-gather(bf16[1,64,16]{1,2,0:T(8,128)(2,1)S(1)} %bitcast.360), channel_id=1, replica_groups=mesh['dp'=2,'expert'=16] {'dp','expert'}, dimensions={0}, use_global_device_ids=true | all-gather | bytes 67584 | tf_op jit(solution)/shard_map/all_gather | solution.py:146
  864.8 12.4 gather_fusion.2
  883.3 15.4 gather_fusion.1
  898.7 6.9 select_select_fusion
  905.6 4.7 all-to-all-start.2
  911.0 159.5 %all-to-all-done.2 = bf16[16,96,2048]{2,1,0:T(8,128)(2,1)} async-done(((bf16[16,96,2048]{2,1,0:T(8,128)(2,1)}), bf16[16,96,2048]{2,1,0:T(8,128)(2,1)}, u32[]{:S(2)}, u32[]{:S(2)}) %all-to-all-start.2) | async-done | bytes 6291488 | tf_op jit(solution)/shard_map/all_to_all | solution.py:287
  1070.5 10.1 convert_bitcast_fusion.1
  1082.2 6.1 fusion.78
  1090.1 9.1 fusion.92
  1099.2 14.2 add_convert_fusion
  1113.4 32.5 %all-to-all-start.3 = ((bf16[16,96,2048]{2,1,0:T(8,128)(2,1)}), bf16[16,96,2048]{2,1,0:T(8,128)(2,1)}, u32[]{:S(2)}, u32[]{:S(2)}) async-start(bf16[16,96,2048]{2,1,0:T(8,128)(2,1)} %add_convert_fusion), calls=%async_computation.3 | async-start | bytes 12582912 | tf_op jit(solution)/shard_map/all_to_all | solution.py:319
  1146.3 113.9 %all-to-all-done.3 = bf16[16,96,2048]{2,1,0:T(8,128)(2,1)} async-done(((bf16[16,96,2048]{2,1,0:T(8,128)(2,1)}), bf16[16,96,2048]{2,1,0:T(8,128)(2,1)}, u32[]{:S(2)}, u32[]{:S(2)}) %all-to-all-start.3) | async-done | bytes 6291488 | tf_op jit(solution)/shard_map/all_to_all | solution.py:319
  1260.2 12.4 gather_fusion.3
  1272.6 9.8 convert_reduce_fusion
  1284.7 7.4 convolution_convert_fusion.1
  1294.0 11.2 fusion.96
  1305.3 13.2 fusion.97
  1318.6 11.3 fusion.98
  1330.9 8.1 fusion.121
  1341.9 45.0 %all_gather.76 = f32[2048,16]{0,1:T(8,128)S(1)} all-gather(f32[128,16]{0,1:T(8,128)} %bitcast.37), channel_id=1, replica_groups=mesh['dp'=2,'expert'=16] {'expert'}, dimensions={0}, use_global_device_ids=true | all-gather | bytes 139264 | tf_op jit(solution)/shard_map/all_gather | solution.py:352
  1390.2 20.8 all_gather.78
  1412.2 146.6 %while.42 = (s32[]{:T(128)}, f32[128,16,128]{0,2,1:T(8,128)}, f32[128,16,128]{0,2,1:T(8,128)}, f32[128,16,128]{0,2,1:T(8,128)}, bf16[2048,2048]{0,1:T(8,128)(2,1...) while((s32[]{:T(128)}, f32[128,16,128]{0,2,1:T(8,128)}, ...), condition=%wide.region_30.32_spmd.clone.clone, body=%wide.region_27.31_spmd.clone.clone.sunk | while | flops 1898417664 | bytes 73996376 | solution.py:83
  1422.5 6.1 fusion.264
  1437.6 6.6 fusion.267
  1458.7 6.4 fusion.264
  1474.1 6.7 fusion.267
  1495.3 6.4 fusion.264
  1510.7 6.7 fusion.267
  1532.0 6.8 fusion.264
  1547.8 6.7 fusion.267
  1565.1 8.2 fusion.141
  1578.5 8.2 fusion.139
  1588.0 8.2 fusion.137
  1601.8 34.7 %reduce-scatter.21.cloned.1.call-done = bf16[1,1024,1024]{2,1,0:T(8,128)(2,1)} async-done(((bf16[1,2048,1024]{2,1,0:T(8,128)(2,1)}), bf16[1,1024,1024]{2,1,0:T(8,128)(2,1)}) %reduce-scatter.21.cloned.1.call-update) | async-done | bytes 2097168 | tf_op jit(solution)/shard_map/reduce_scatter | solution.py:460
  1640.6 52.5 %reduce-scatter.23.cloned.1.call-done = bf16[1,512,2048]{2,1,0:T(8,128)(2,1)} async-done(((bf16[1,1024,2048]{2,1,0:T(8,128)(2,1)}), bf16[1,512,2048]{2,1,0:T(8,128)(2,1)}) %reduce-scatter.23.cloned.1.call-update) | async-done | bytes 2097168 | tf_op jit(solution)/shard_map/reduce_scatter | solution.py:463
  1697.3 6.4 fusion.151
  1703.7 6.4 convolution_add_fusion.2
  1713.2 47.0 %all-reduce.8 = (f32[2048]{0:T(1024)S(1)}, f32[2048]{0:T(1024)S(1)}, f32[2048]{0:T(1024)S(1)}, f32[2048]{0:T(1024)S(1)}) all-reduce(f32[2048]{0:T(1024)S(1)} %get-tuple-element.1136, f32[2048]{0:T(1024)S(1)} %get-tuple-element.1134, f32[2048]{0:T(1024)S(1)} %get-tuple-element.1132, ...), channel_id=2, replica_groups=mesh['dp'=2,'expert'=16] {'dp','expert'}, use_global_device_ids=true, to_apply=%region_35.37.clone | all-reduce | flops 8192 | bytes 65536
  1764.0 119.4 %reduce-scatter.17.cloned.1.call-done = f32[64,2048]{1,0:T(8,128)} async-done(((f32[2048,2048]{1,0:T(8,128)}), f32[64,2048]{1,0:T(8,128)}) %reduce-scatter.17.cloned.1.call-update) | async-done | bytes 524304 | tf_op jit(solution)/shard_map/reduce_scatter | solution.py:449
  1883.4 187.1 %reduce-scatter.11.cloned.1.call-done = f32[64,2048]{1,0:T(8,128)} async-done(((f32[2048,2048]{1,0:T(8,128)}), f32[64,2048]{1,0:T(8,128)}) %reduce-scatter.11.cloned.1.call-update) | async-done | bytes 524304 | tf_op jit(solution)/shard_map/reduce_scatter | solution.py:446
  2070.5 187.0 %reduce-scatter.13.cloned.1.call-done = f32[64,2048]{1,0:T(8,128)} async-done(((f32[2048,2048]{1,0:T(8,128)}), f32[64,2048]{1,0:T(8,128)}) %reduce-scatter.13.cloned.1.call-update) | async-done | bytes 524304 | tf_op jit(solution)/shard_map/reduce_scatter | solution.py:447
  2257.4 186.9 %reduce-scatter.15.cloned.1.call-done = f32[64,2048]{1,0:T(8,128)} async-done(((f32[2048,2048]{1,0:T(8,128)}), f32[64,2048]{1,0:T(8,128)}) %reduce-scatter.15.cloned.1.call-update) | async-done | bytes 524304 | tf_op jit(solution)/shard_map/reduce_scatter | solution.py:448
  (417 shorter events, 241.6 us)
Async XLA Ops:
  8.0 82.6 %all-gather.19.cloned.1.call-start = ((), (), s32[]{:S(2)}) async-start(), calls=%async_computation.15 | async-start | bytes 8650752 | tf_op jit(solution)/shard_map/all_gather | solution.py:144
  8.7 160.9 %all-gather.17.cloned.1.call-start = ((), (), s32[]{:S(2)}) async-start(), calls=%async_computation.14 | async-start | bytes 8650752 | tf_op jit(solution)/shard_map/all_gather | solution.py:142
  9.5 239.1 %all-gather.13.cloned.1.call-start = ((), (), s32[]{:S(2)}) async-start(), calls=%async_computation.12 | async-start | bytes 8650752 | tf_op jit(solution)/shard_map/all_gather | solution.py:143
  10.2 314.5 %all-gather.21.cloned.1.call-start = ((), (), s32[]{:S(2)}) async-start(), calls=%async_computation.16 | async-start | bytes 8912896 | tf_op jit(solution)/shard_map/all_gather | solution.py:210
  55.7 192.9 %copy-start.26 = (f32[2048]{0:T(1024)}, f32[2048]{0:T(1024)S(1)}, u32[]{:S(2)}) copy-start(f32[2048]{0:T(1024)S(1)} %convert_element_type.237) | copy-start | bytes 24580
  57.5 191.1 %copy-start.43 = (f32[128]{0:T(128)}, f32[128]{0:T(128)S(1)}, u32[]{:S(2)}) copy-start(f32[128]{0:T(128)S(1)} %get-tuple-element.1251) | copy-start | bytes 1540
  90.7 5.9 copy-start.62
  90.7 79.0 %copy-start.1 = (bf16[128,2048]{1,0:T(8,128)(2,1)S(1)}, bf16[128,2048]{1,0:T(8,128)(2,1)}, u32[]{:S(2)}) copy-start(bf16[128,2048]{1,0:T(8,128)(2,1)} %param.22) | copy-start | bytes 1572868
  96.4 307.3 %all-gather.15.cloned.1.call-start = ((), (), s32[]{:S(2)}) async-start(), calls=%async_computation.13 | async-start | bytes 8912896 | tf_op jit(solution)/shard_map/all_gather | solution.py:209
  96.5 78.6 %copy-start.39 = (f32[2048]{0:T(1024)}, f32[2048]{0:T(1024)S(1)}, u32[]{:S(2)}) copy-start(f32[2048]{0:T(1024)S(1)} %convert_element_type.243) | copy-start | bytes 24580
  96.5 157.5 %copy-start.37 = (f32[2048]{0:T(1024)}, f32[2048]{0:T(1024)S(1)}, u32[]{:S(2)}) copy-start(f32[2048]{0:T(1024)S(1)} %convert_element_type.239) | copy-start | bytes 24580
  99.6 157.4 %copy-start.36 = (f32[128,64]{0,1:T(8,128)}, f32[128,64]{0,1:T(8,128)S(1)}, u32[]{:S(2)}) copy-start(f32[128,64]{0,1:T(8,128)S(1)} %get-tuple-element.1249) | copy-start | bytes 98308
  175.0 78.3 %copy-start.54 = (f32[128]{0:T(128)}, f32[128]{0:T(128)S(1)}, u32[]{:S(2)}) copy-start(f32[128]{0:T(128)S(1)} %get-tuple-element.1255) | copy-start | bytes 1540
  258.2 223.9 %all-gather.23.cloned.1.call-start = ((), (), s32[]{:S(2)}) async-start(), calls=%async_computation.17 | async-start | bytes 8650752 | tf_op jit(solution)/shard_map/all_gather | solution.py:145
  259.1 228.3 %copy-start.41 = (f32[2048]{0:T(1024)}, f32[2048]{0:T(1024)S(1)}, u32[]{:S(2)}) copy-start(f32[2048]{0:T(1024)S(1)} %convert_element_type.250) | copy-start | bytes 24580
  266.5 70.6 %copy-start.21 = (bf16[128,16,128]{0,2,1:T(8,128)(2,1)}, bf16[128,16,128]{0,2,1:T(8,128)(2,1)S(1)}, u32[]{:S(2)}) copy-start(bf16[128,16,128]{0,2,1:T(8,128)(2,1)S(1)} %maximum_convert_fusion.1) | copy-start | bytes 1572868
  455.2 31.6 %copy-start.3 = (bf16[128,16,128]{2,0,1:T(8,128)(2,1)}, bf16[128,16,128]{2,0,1:T(8,128)(2,1)S(1)}, u32[]{:S(2)}) copy-start(bf16[128,16,128]{2,0,1:T(8,128)(2,1)S(1)} %get-tuple-element.1630) | copy-start | bytes 1572868
  455.2 31.6 %copy-start.32 = (f32[16,128]{1,0:T(8,128)}, f32[16,128]{1,0:T(8,128)S(1)}, u32[]{:S(2)}) copy-start(f32[16,128]{1,0:T(8,128)S(1)} %get-tuple-element.822) | copy-start | bytes 24580
  455.2 31.6 %copy-start.34 = (f32[16,128]{1,0:T(8,128)}, f32[16,128]{1,0:T(8,128)S(1)}, u32[]{:S(2)}) copy-start(f32[16,128]{1,0:T(8,128)S(1)} %get-tuple-element.821) | copy-start | bytes 24580
  455.2 31.7 %copy-start.45 = (f32[32]{0:T(128)}, f32[32]{0:T(128)S(1)}, u32[]{:S(2)}) copy-start(f32[32]{0:T(128)S(1)} %get-tuple-element.1677) | copy-start | bytes 388
  456.7 30.1 %copy-start.17 = (bf16[128,16,128]{0,2,1:T(8,128)(2,1)}, bf16[128,16,128]{0,2,1:T(8,128)(2,1)S(1)}, u32[]{:S(2)}) copy-start(bf16[128,16,128]{0,2,1:T(8,128)(2,1)S(1)} %fusion.120) | copy-start | bytes 1572868
  487.4 7.6 copy-start.50
  501.8 118.8 %all-to-all-start = ((bf16[16,96,2048]{2,1,0:T(8,128)(2,1)}), bf16[16,96,2048]{2,1,0:T(8,128)(2,1)}, u32[]{:S(2)}, u32[]{:S(2)}) async-start(bf16[16,96,2048]{2,1,0:T(8,128)(2,1)} %select_select_fusion.1), calls=%async_computation | async-start | bytes 12582912 | tf_op jit(solution)/shard_map/all_to_all | solution.py:240
  506.5 58.7 %all-gather.27.cloned.1.call-start = ((), (), s32[]{:S(2)}) async-start(), calls=%async_computation.19 | async-start | bytes 6291456 | tf_op jit(solution)/shard_map/all_gather | solution.py:158
  507.1 125.2 %all-gather.25.cloned.1.call-start = ((), (), s32[]{:S(2)}) async-start(), calls=%async_computation.18 | async-start | bytes 6291456 | tf_op jit(solution)/shard_map/all_gather | solution.py:157
  507.7 173.6 %all-gather.29.cloned.1.call-start = ((), (), s32[]{:S(2)}) async-start(), calls=%async_computation.20 | async-start | bytes 6291456 | tf_op jit(solution)/shard_map/all_gather | solution.py:159
  632.3 13.7 copy-start.7
  692.4 6.0 copy-start.28
  692.4 6.1 copy-start.56
  692.4 172.3 %all-to-all-start.1 = ((bf16[16,96,2048]{2,1,0:T(8,128)(2,1)}), bf16[16,96,2048]{2,1,0:T(8,128)(2,1)}, u32[]{:S(2)}, u32[]{:S(2)}) async-start(bf16[16,96,2048]{2,1,0:T(8,128)(2,1)} %convolution_convert_fusion), calls=%async_computation.1 | async-start | bytes 12582912 | tf_op jit(solution)/shard_map/all_to_all | solution.py:249
  883.3 15.4 copy-start.49
  905.6 164.9 %all-to-all-start.2 = ((bf16[16,96,2048]{2,1,0:T(8,128)(2,1)}), bf16[16,96,2048]{2,1,0:T(8,128)(2,1)}, u32[]{:S(2)}, u32[]{:S(2)}) async-start(bf16[16,96,2048]{2,1,0:T(8,128)(2,1)} %select_select_fusion), calls=%async_computation.2 | async-start | bytes 12582912 | tf_op jit(solution)/shard_map/all_to_all | solution.py:287
  910.3 501.9 %all-gather.31.cloned.1.call-start = ((), (), s32[]{:S(2)}) async-start(), calls=%async_computation.21 | async-start | bytes 8912896 | tf_op jit(solution)/shard_map/all_gather | solution.py:414
  1082.2 7.8 copy-start.61
  1082.2 17.0 slice-start.2
  1090.1 9.1 slice-start.3
  1113.4 146.8 %all-to-all-start.3 = ((bf16[16,96,2048]{2,1,0:T(8,128)(2,1)}), bf16[16,96,2048]{2,1,0:T(8,128)(2,1)}, u32[]{:S(2)}, u32[]{:S(2)}) async-start(bf16[16,96,2048]{2,1,0:T(8,128)(2,1)} %add_convert_fusion), calls=%async_computation.3 | async-start | bytes 12582912 | tf_op jit(solution)/shard_map/all_to_all | solution.py:319
  1146.0 266.2 %all-gather.33.cloned.1.call-start = ((), (), s32[]{:S(2)}) async-start(), calls=%async_computation.22 | async-start | bytes 8912896 | tf_op jit(solution)/shard_map/all_gather | solution.py:415
  1272.6 9.8 copy-start.11
  1272.6 9.8 copy-start.42
  1272.6 9.8 copy-start.51
  1272.6 10.9 copy-start.58
  1284.7 45.2 %copy-start.8 = (f32[128,2048]{1,0:T(8,128)}, f32[128,2048]{1,0:T(8,128)S(1)}, u32[]{:S(2)}) copy-start(f32[128,2048]{1,0:T(8,128)S(1)} %get-tuple-element.1239) | copy-start | bytes 3145732
  1292.2 304.1 %reduce-scatter.25.cloned.1.call-start = ((), (), s32[]{:S(2)}) async-start(), calls=%async_computation.30 | async-start | bytes 1081344
  1293.6 304.1 %reduce-scatter.19.cloned.1.call-start = ((), (), s32[]{:S(2)}) async-start(), calls=%async_computation.27 | async-start | bytes 6291456 | tf_op jit(solution)/shard_map/reduce_scatter | solution.py:457
  1305.2 331.3 %reduce-scatter.21.cloned.1.call-start = ((), (), s32[]{:S(2)}) async-start(), calls=%async_computation.28 | async-start | bytes 6291456 | tf_op jit(solution)/shard_map/reduce_scatter | solution.py:460
  1318.5 374.6 %reduce-scatter.23.cloned.1.call-start = ((), (), s32[]{:S(2)}) async-start(), calls=%async_computation.29 | async-start | bytes 6291456 | tf_op jit(solution)/shard_map/reduce_scatter | solution.py:463
  1329.9 553.5 %reduce-scatter.17.cloned.1.call-start = ((), (), s32[]{:S(2)}) async-start(), calls=%async_computation.26 | async-start | bytes 17301504 | tf_op jit(solution)/shard_map/reduce_scatter | solution.py:449
  1339.0 47.8 %copy-start.16 = (bf16[128,2048]{1,0:T(8,128)(2,1)S(1)}, bf16[128,2048]{1,0:T(8,128)(2,1)}, u32[]{:S(2)}) copy-start(bf16[128,2048]{1,0:T(8,128)(2,1)} %convolution_convert_fusion.1) | copy-start | bytes 1572868
  1339.0 731.5 %reduce-scatter.11.cloned.1.call-start = ((), (), s32[]{:S(2)}) async-start(), calls=%async_computation.23 | async-start | bytes 17301504 | tf_op jit(solution)/shard_map/reduce_scatter | solution.py:446
  1340.3 71.9 %copy-start.4 = (bf16[128,16,128]{2,0,1:T(8,128)(2,1)S(1)}, bf16[128,16,128]{2,0,1:T(8,128)(2,1)}, u32[]{:S(2)}) copy-start(bf16[128,16,128]{2,0,1:T(8,128)(2,1)} %copy-done.3) | copy-start | bytes 1572868
  1340.3 71.9 %copy-start.46 = (f32[32]{0:T(128)S(1)}, f32[32]{0:T(128)}, u32[]{:S(2)}) copy-start(f32[32]{0:T(128)} %copy-done.45) | copy-start | bytes 388
  1437.6 6.6 copy-start.5
  1474.1 6.7 copy-start.5
  1510.7 6.7 copy-start.5
  1547.8 6.7 copy-start.5
  1558.9 5.6 copy-start.55
  1573.4 684.1 %reduce-scatter.13.cloned.1.call-start = ((), (), s32[]{:S(2)}) async-start(), calls=%async_computation.24 | async-start | bytes 17301504 | tf_op jit(solution)/shard_map/reduce_scatter | solution.py:447
  1586.7 857.6 %reduce-scatter.15.cloned.1.call-start = ((), (), s32[]{:S(2)}) async-start(), calls=%async_computation.25 | async-start | bytes 17301504 | tf_op jit(solution)/shard_map/reduce_scatter | solution.py:448
  1697.2 6.4 copy-start.23
  1697.3 12.9 slice-start
  1703.7 6.5 slice-start.1
  1710.2 52.4 %copy-start.9 = (f32[128,2048]{1,0:T(8,128)S(1)}, f32[128,2048]{1,0:T(8,128)}, u32[]{:S(2)}) copy-start(f32[128,2048]{1,0:T(8,128)} %copy-done.8) | copy-start | bytes 3145732
  1710.2 52.4 %copy-start.57 = (f32[128]{0:T(128)S(1)}, f32[128]{0:T(128)}, u32[]{:S(2)}) copy-start(f32[128]{0:T(128)} %get-tuple-element.1250) | copy-start | bytes 1540
  (32 other events, 86.2 us)
Sparse Core Ops, SparseCore 0:
  11.7 78.9 all-gather.18
  93.5 76.0 all-gather.16
  172.5 76.0 all-gather.12
  251.2 73.4 all-gather.20
  327.3 76.3 all-gather.14
  406.3 75.6 all-gather.22
  913.3 175.7 all-gather.30
  1292.3 99.2 all-gather.32
  1393.8 132.2 reduce-scatter.24
  1528.9 50.3 reduce-scatter.18
  1582.2 54.2 reduce-scatter.20
  1638.8 54.3 reduce-scatter.22
  1696.0 187.3 reduce-scatter.16
  1886.1 184.3 reduce-scatter.10
  2073.2 184.1 reduce-scatter.12
  2260.2 184.1 reduce-scatter.14
Sparse Core Ops, SparseCore 1:
  508.5 56.6 all-gather.26
  566.6 56.6 all-gather.24
  624.6 56.6 all-gather.28
where the time goes:
time: 2460 us; the launch traced here: 2450 us
  waiting for transfers between devices  1520 us (62%)
  blocking collectives  320 us (13%)
  matrix products  307 us (12%)
  local copies, waits for them, and re-layouts  142 us (6%)
  other arithmetic  98.3 us (4%)
  starting transfers between devices  50 us (2%)
    reduce_scatter x1, waiting for transfers between devices, per_device(): lax.psum_scatter(query_w_grad, ('dp', 'expert'), scatter_dimension=0, til...  187 us
    reduce_scatter x1, waiting for transfers between devices, per_device(): lax.psum_scatter(key_w_grad, ('dp', 'expert'), scatter_dimension=0, tiled...  187 us
    reduce_scatter x1, waiting for transfers between devices, per_device(): lax.psum_scatter(value_w_grad, ('dp', 'expert'), scatter_dimension=0, til...  187 us
    all_gather x1, blocking collectives, per_device(): lax.all_gather(router, ('dp', 'expert'), axis=0, tiled=True)  166 us
    all_to_all x1, waiting for transfers between devices, per_device(): lax.all_to_all(send_grads, 'expert', split_axis=0, concat_axis=0, tiled=T...  159 us
    reduce_scatter x1, waiting for transfers between devices, per_device(): lax.psum_scatter(out_w_grad, ('dp', 'expert'), scatter_dimension=0, tiled...  119 us
    all_to_all x1, waiting for transfers between devices, per_device(): lax.all_to_all(row_grad.reshape(group_size * local_experts, capacity, mod...  114 us
    unnamed x2, blocking collectives  89 us
  transfers between devices with their start and end apart: 23, of which 17 were waited for; matrix products, arithmetic and copies ran while one was open for 19% of the time, Pallas kernels for 0%

commit v1 on v0

v1 whole, which is shorter than its diff:
```python
import functools
import math

import jax
import jax.numpy as jnp
from jax import lax
from jax.experimental import pallas as pl
from jax.experimental.pallas import tpu as pltpu
from jax.sharding import PartitionSpec as P

HEAD_DIM = 128
EPSILON = 1e-05
THETA = 10000.0
NEGATIVE = -1e30
BOTH = ("dp", "expert")
F32 = jnp.float32
BF16 = jnp.bfloat16
MESH = pl.DeviceIdType.MESH


def mm(a, b):
    return lax.dot_general(a, b, (((1,), (0,)), ((), ())), preferred_element_type=F32)


def mm_t(a, b):
    return lax.dot_general(a, b, (((1,), (1,)), ((), ())), preferred_element_type=F32)


def t_mm(a, b):
    return lax.dot_general(a, b, (((0,), (0,)), ((), ())), preferred_element_type=F32)


def inverse_rms(values):
    return lax.rsqrt(jnp.mean(values * values, axis=-1, keepdims=True) + EPSILON)


def turn(values, cosine, sine):
    half = HEAD_DIM // 2
    a, b = values[:, :half], values[:, half:]
    return jnp.concatenate([a * cosine - b * sine, b * cosine + a * sine], axis=-1)


def ancestry(parents):
    count = parents.shape[0]
    labels = jnp.arange(count, dtype=jnp.int32)
    table = (parents[:, None] == labels[None, :]).astype(F32)
    for _ in range((count - 1).bit_length()):
        product = jnp.dot(table, table, precision=lax.Precision.HIGHEST, preferred_element_type=F32)
        table = jnp.minimum(table + product, 1.0)
    return table


def spot():
    me = lax.axis_index("expert")
    return me // 4, (me // 2) % 2, me % 2

def at(z, x, c):
    return (z * 2 + x) * 2 + c

def greet(z, x, c, far):
    barrier = pltpu.get_barrier_semaphore()
    def hello(e):
        pl.semaphore_signal(barrier, inc=1, device_id={"expert": e}, device_id_type=MESH)
    hello(at(z, x, 1 - c)); hello(at(z, 1 - x, c))
    @pl.when(z > 0)
    def _(): hello(at(z - 1, x, c))
    @pl.when(z < far)
    def _(): hello(at(z + 1, x, c))
    count = 2 + jnp.where(z > 0, 1, 0) + jnp.where(z < far, 1, 0)
    pl.semaphore_wait(barrier, count)

def gather_kernel(zs, in_ref, out_ref, send, recv, local):
    z, x, c = spot()
    far = zs - 1
    me = at(z, x, c)
    greet(z, x, c, far)
    mine = pltpu.make_async_copy(in_ref, out_ref.at[me], local)
    mine.start()
    def copy(src, block, kind, e):
        return pltpu.make_async_remote_copy(
            src_ref=src, dst_ref=out_ref.at[block], send_sem=send.at[kind, block],
            recv_sem=recv.at[block], device_id={"expert": e}, device_id_type=MESH)
    SIB, X, UP, DOWN = range(4)
    def forward(src, block, zz):
        @pl.when((zz <= z) & (z < far))
        def _(): copy(src, block, UP, at(z + 1, x, c)).start()
        @pl.when((zz >= z) & (z > 0))
        def _(): copy(src, block, DOWN, at(z - 1, x, c)).start()
        copy(src, block, X, at(z, 1 - x, c)).start()
        copy(src, block, SIB, at(z, x, 1 - c)).start()
    def arrived(block):
        copy(in_ref, block, SIB, at(z, x, 1 - c)).wait_recv()
    forward(in_ref, me, z)
    def across(zz):
        block = at(zz, 1 - x, c)
        arrived(block)
        copy(out_ref.at[block], block, SIB, at(z, x, 1 - c)).start()
    across(z)
    for d in range(1, zs):
        for zz, ok in ((z - d, z >= d), (z + d, z + d <= far)):
            @pl.when(ok)
            def _():
                block = at(zz, x, c)
                arrived(block)
                forward(out_ref.at[block], block, zz)
        for zz, ok in ((z - d, z >= d), (z + d, z + d <= far)):
            @pl.when(ok)
            def _(): across(zz)
    for zz in range(zs):
        for xx in range(2):
            arrived(at(zz, xx, 1 - c))
    mine.wait()
    def sent(block, kind):
        copy(in_ref, block, kind, at(z, x, 1 - c)).wait_send()
    for zz in range(zs):
        block = at(zz, x, c)
        sent(block, X); sent(block, SIB); sent(at(zz, 1 - x, c), SIB)
        @pl.when((zz <= z) & (z < far))
        def _(): sent(block, UP)
        @pl.when((zz >= z) & (z > 0))
        def _(): sent(block, DOWN)

def gather(values, group, cid):
    return pl.pallas_call(
        functools.partial(gather_kernel, group // 4),
        out_shape=jax.ShapeDtypeStruct((group, *values.shape), values.dtype),
        in_specs=[pl.BlockSpec(memory_space=pl.ANY)],
        out_specs=pl.BlockSpec(memory_space=pl.ANY),
        scratch_shapes=[pltpu.SemaphoreType.DMA((4, group)), pltpu.SemaphoreType.DMA((group,)), pltpu.SemaphoreType.DMA],
        compiler_params=pltpu.CompilerParams(collective_id=cid, has_side_effects=True),
    )(values)

def scatter_kernel(zs, in_ref, out_ref, r_sib, r_x, r_z, s_x, s_z, send, recv):
    z, x, c = spot()
    far = zs - 1
    greet(z, x, c, far)
    SIB, X, UP, DOWN = range(4)
    def to_sibling(zz, xx):
        return pltpu.make_async_remote_copy(
            src_ref=in_ref.at[at(zz, xx, 1 - c)], dst_ref=r_sib.at[zz * 2 + xx],
            send_sem=send.at[SIB, zz * 2 + xx], recv_sem=recv.at[SIB, zz * 2 + xx],
            device_id={"expert": at(z, x, 1 - c)}, device_id_type=MESH)
    def to_x(zz):
        return pltpu.make_async_remote_copy(
            src_ref=s_x.at[zz], dst_ref=r_x.at[zz], send_sem=send.at[X, zz], recv_sem=recv.at[X, zz],
            device_id={"expert": at(z, 1 - x, c)}, device_id_type=MESH)
    def along(zz, kind, e):
        return pltpu.make_async_remote_copy(
            src_ref=s_z.at[zz], dst_ref=r_z.at[kind - UP, zz], send_sem=send.at[kind, zz], recv_sem=recv.at[kind, zz],
            device_id={"expert": e}, device_id_type=MESH)
    def up(zz): return along(zz, UP, at(z + 1, x, c))
    def down(zz): return along(zz, DOWN, at(z - 1, x, c))
    def order(f):
        for d in range(far, 0, -1):
            @pl.when(z + d <= far)
            def _(): f(z + d)
            @pl.when(z >= d)
            def _(): f(z - d)
        f(z)
    order(lambda zz: to_sibling(zz, 1 - x).start())
    order(lambda zz: to_sibling(zz, x).start())
    def cross(zz):
        to_sibling(zz, 1 - x).wait_recv()
        s_x[zz] = (in_ref[at(zz, 1 - x, c)].astype(F32) + r_sib[zz * 2 + 1 - x].astype(F32)).astype(BF16)
        to_x(zz).start()
    order(cross)
    def finish(zz):
        to_sibling(zz, x).wait_recv()
        to_x(zz).wait_recv()
        def here():
            return in_ref[at(zz, x, c)].astype(F32) + r_sib[zz * 2 + x].astype(F32) + r_x[zz].astype(F32)
        @pl.when(zz > z)
        def _():
            @pl.when(z > 0)
            def _():
                up(zz).wait_recv()
                s_z[zz] = (here() + r_z[0, zz].astype(F32)).astype(BF16)
            @pl.when(z == 0)
            def _(): s_z[zz] = here().astype(BF16)
            up(zz).start()
        @pl.when(zz < z)
        def _():
            @pl.when(z < far)
            def _():
                down(zz).wait_recv()
                s_z[zz] = (here() + r_z[1, zz].astype(F32)).astype(BF16)
            @pl.when(z == far)
            def _(): s_z[zz] = here().astype(BF16)
            down(zz).start()
        @pl.when(zz == z)
        def _():
            out_ref[...] = here()
            @pl.when(z > 0)
            def _():
                up(zz).wait_recv()
                out_ref[...] += r_z[0, zz].astype(F32)
            @pl.when(z < far)
            def _():
                down(zz).wait_recv()
                out_ref[...] += r_z[1, zz].astype(F32)
    order(finish)
    for zz in range(zs):
        for xx in range(2):
            to_sibling(zz, xx).wait_send()
        to_x(zz).wait_send()
        @pl.when(zz > z)
        def _(): up(zz).wait_send()
        @pl.when(zz < z)
        def _(): down(zz).wait_send()

def scatter(values, cid):
    group, rows, width = values.shape
    zs = group // 4
    buf = lambda *n: pltpu.VMEM((*n, rows, width), BF16)
    return pl.pallas_call(
        functools.partial(scatter_kernel, zs),
        out_shape=jax.ShapeDtypeStruct((rows, width), F32),
        in_specs=[pl.BlockSpec(memory_space=pltpu.VMEM)],
        out_specs=pl.BlockSpec(memory_space=pltpu.VMEM),
        scratch_shapes=[buf(2 * zs), buf(zs), buf(2, zs), buf(zs), buf(zs),
            pltpu.SemaphoreType.DMA((4, 2 * zs)), pltpu.SemaphoreType.DMA((4, 2 * zs))],
        compiler_params=pltpu.CompilerParams(collective_id=cid, has_side_effects=True, vmem_limit_bytes=48 * 2**20),
    )(values)

def swap_kernel(axes, sizes, in_ref, out_ref, send, recv, local):
    count = 1
    for size in sizes:
        count *= size
    me = jnp.int32(0)
    for axis, size in zip(axes, sizes):
        me = me * size + lax.axis_index(axis)
    same = in_ref.shape[0] == 1

    def spread(d):
        where = {}
        for axis, size in zip(axes[::-1], sizes[::-1]):
            where[axis] = d % size
            d = d // size
        return where

    barrier = pltpu.get_barrier_semaphore()

    def hello(k, carry):
        pl.semaphore_signal(
            barrier, inc=1, device_id=spread((me + k) % count), device_id_type=MESH
        )
        return carry

    lax.fori_loop(1, count, hello, 0)
    pl.semaphore_wait(barrier, count - 1)

    def copy(k):
        d = (me + k) % count
        return pltpu.make_async_remote_copy(
            src_ref=in_ref.at[0 if same else d],
            dst_ref=out_ref.at[me],
            send_sem=send.at[k],
            recv_sem=recv.at[me],
            device_id=spread(d),
            device_id_type=MESH,
        )

    def start(k, carry):
        copy(k).start()
        return carry

    lax.fori_loop(1, count, start, 0)
    mine = pltpu.make_async_copy(in_ref.at[0 if same else me], out_ref.at[me], local)
    mine.start()
    mine.wait()

    def finish(k, carry):
        d = (me + k) % count
        pltpu.make_async_remote_copy(
            src_ref=in_ref.at[0],
            dst_ref=out_ref.at[d],
            send_sem=send.at[k],
            recv_sem=recv.at[d],
            device_id=spread(d),
            device_id_type=MESH,
        ).wait_recv()
        copy(k).wait_send()
        return carry

    lax.fori_loop(1, count, finish, 0)


def swap(values, axes, cid):
    sizes = tuple(lax.axis_size(axis) for axis in axes)
    count = 1
    for size in sizes:
        count *= size
    return pl.pallas_call(
        functools.partial(swap_kernel, axes, sizes),
        out_shape=jax.ShapeDtypeStruct((count, *values.shape[1:]), values.dtype),
        in_specs=[pl.BlockSpec(memory_space=pltpu.VMEM)],
        out_specs=pl.BlockSpec(memory_space=pltpu.VMEM),
        scratch_shapes=[
            pltpu.SemaphoreType.DMA((count,)),
            pltpu.SemaphoreType.DMA((count,)),
            pltpu.SemaphoreType.DMA,
        ],
        compiler_params=pltpu.CompilerParams(
            collective_id=cid, has_side_effects=True, vmem_limit_bytes=32 * 2**20
        ),
    )(values)


SCALE = HEAD_DIM ** (-0.5)


def attention(queries, mask, keys, values):
    scores = jnp.where(mask, mm_t(queries, keys) * SCALE, NEGATIVE)
    row_max = jnp.max(scores, axis=-1, keepdims=True)
    weights = jnp.exp(scores - row_max)
    total = jnp.sum(weights, axis=-1, keepdims=True)
    attn = mm(weights.astype(BF16), values) / total
    return attn, row_max + jnp.log(total)


def attention_back(queries, mask, log_total, mixed_grad, row_delta, keys, values):
    probs = jnp.exp(jnp.where(mask, mm_t(queries, keys) * SCALE - log_total, NEGATIVE))
    score_grad = (probs * (mm_t(mixed_grad, values) - row_delta)).astype(BF16)
    query_grad = mm(score_grad, keys) * SCALE
    key_grad = t_mm(score_grad, queries) * SCALE
    return query_grad, key_grad, t_mm(probs.astype(BF16), mixed_grad)


def expert_step(rows_in, cot_in, gates, gate_w, up_w, down_w):
    cot_in = cot_in.astype(F32)
    gate_pre = mm(rows_in, gate_w)
    up_pre = mm(rows_in, up_w)
    sig = jax.nn.sigmoid(gate_pre)
    silu = gate_pre * sig
    hidden = (silu * up_pre).astype(BF16)
    expert_out = mm(hidden, down_w).astype(BF16).astype(F32)
    sent_out = (gates * expert_out).astype(BF16)
    gate_grad = jnp.sum(cot_in * expert_out, axis=-1)
    out_grad = (gates * cot_in).astype(BF16)
    hidden_grad = mm_t(out_grad, down_w).astype(BF16).astype(F32)
    gate_pre_grad = (hidden_grad * up_pre * sig * (1.0 + gate_pre * (1.0 - sig))).astype(BF16)
    up_pre_grad = (hidden_grad * silu).astype(BF16)
    row_grad = (mm_t(gate_pre_grad, gate_w) + mm_t(up_pre_grad, up_w)).astype(BF16)
    sums = (t_mm(rows_in, gate_pre_grad), t_mm(rows_in, up_pre_grad), t_mm(hidden, out_grad))
    return (sent_out, gate_grad, row_grad), sums


def per_device(
    tokens, attn_gain, q_gain, k_gain, ffn_gain, w_query, w_key, w_value, w_out, router,
    w_gate, w_up, w_down, cotangent, routes, parents,
):
    rows, width = tokens.shape
    heads = width // HEAD_DIM
    group = lax.axis_size("expert")
    n_dp = lax.axis_size("dp")
    devices = group * n_dp
    share = max(1, group // heads)
    tree_rows = group * rows
    own_rows = tree_rows // share
    shard = w_query.shape[0]
    dp = lax.axis_index("dp")
    me = lax.axis_index("expert")
    head = me // share
    part = me % share
    peers = [[h * share + j for h in range(heads)] for j in range(share)]
    siblings = [[h * share + j for j in range(share)] for h in range(heads)]

    reach = ancestry(parents)
    start = dp * group
    tree = lax.dynamic_slice(reach, (start, start), (group, group))
    depth = jnp.sum(lax.dynamic_slice_in_dim(reach, start, group, 0), axis=1)
    sees = tree + jnp.eye(group, dtype=F32)
    own_segs = own_rows // rows
    first_seg = part * own_segs
    my_depth = lax.dynamic_slice_in_dim(depth, first_seg, own_segs, 0)
    my_sees = lax.dynamic_slice_in_dim(sees, first_seg, own_segs, 0)
    place = jnp.arange(rows, dtype=F32)
    positions = (my_depth[:, None] * rows + place[None, :]).reshape(own_rows)
    frequencies = THETA ** (-2.0 * jnp.arange(HEAD_DIM // 2, dtype=F32) / HEAD_DIM)
    angles = positions[:, None] * frequencies[None, :]
    cosine, sine = jnp.cos(angles), jnp.sin(angles)
    key_index = jnp.arange(tree_rows, dtype=jnp.int32)
    query_index = first_seg * rows + jnp.arange(own_rows, dtype=jnp.int32)
    seen = jnp.repeat(jnp.repeat(my_sees, rows, axis=0), rows, axis=1) > 0.5
    mask = seen & (key_index[None, :] <= query_index[:, None])

    def own_part(values):
        return lax.dynamic_slice_in_dim(values, first_seg * rows, own_rows, 0)

    def head_sum(values, cid):
        if share > 1:
            return lax.psum(values, "expert", axis_index_groups=peers)
        return jnp.sum(swap(values[None], ("expert",), cid), axis=0)

    def tree_gather(values, cid):
        if share > 1:
            return lax.all_gather(values, "expert", axis=0, tiled=True)
        return gather(values, group, cid).reshape(tree_rows, -1)

    def tree_scatter(values, cid):
        if share > 1:
            return lax.psum_scatter(values, "expert", scatter_dimension=0, tiled=True).astype(F32)
        return scatter(values.reshape(group, rows, -1), cid)

    def both_swap(values, cid):
        if share > 1:
            return lax.all_to_all(values, BOTH, 0, 0, tiled=True)
        return swap(values, BOTH, cid)

    def expert_swap(values, cid):
        if share > 1:
            return lax.all_to_all(values, "expert", 0, 0, tiled=True)
        return swap(values, ("expert",), cid)

    others = [(d, (d + 1) % n_dp) for d in range(n_dp)]

    def dp_join(values):
        if n_dp != 2:
            return lax.all_gather(values, "dp", axis=0, tiled=True)
        other = lax.ppermute(values, "dp", others)
        return jnp.where(
            dp == 0, jnp.concatenate([values, other]), jnp.concatenate([other, values])
        )

    def dp_sum(values):
        if n_dp != 2:
            return lax.psum_scatter(values, "dp", scatter_dimension=0, tiled=True)
        halves = values.reshape(2, values.shape[0] // 2, -1)
        theirs = lax.dynamic_index_in_dim(halves, 1 - dp, 0, keepdims=False)
        ours = lax.dynamic_index_in_dim(halves, dp, 0, keepdims=False)
        return ours.astype(F32) + lax.ppermute(theirs, "dp", others).astype(F32)

    gains = lax.all_gather(
        jnp.stack([attn_gain, q_gain, k_gain, ffn_gain], axis=1), BOTH, axis=0, tiled=True
    ).astype(F32)
    attn_g, query_g, key_g, ffn_g = gains[:, 0], gains[:, 1], gains[:, 2], gains[:, 3]
    my_query_g = lax.dynamic_slice_in_dim(query_g, head * HEAD_DIM, HEAD_DIM, 0)[None, :]
    my_key_g = lax.dynamic_slice_in_dim(key_g, head * HEAD_DIM, HEAD_DIM, 0)[None, :]
    by_head = jnp.stack([w_query, w_key, w_value], axis=1).reshape(shard, 3, heads, HEAD_DIM)
    by_head = by_head.transpose(2, 0, 1, 3).reshape(1, heads, 1, shard, 3 * HEAD_DIM)
    by_head = jnp.broadcast_to(by_head, (n_dp, heads, share, shard, 3 * HEAD_DIM))
    w_head = both_swap(by_head.reshape(devices, shard, 3 * HEAD_DIM), 0).reshape(
        width, 3 * HEAD_DIM
    )
    out_w = lax.all_gather(w_out, BOTH, axis=0, tiled=True)
    out_head = lax.dynamic_slice_in_dim(out_w, head * HEAD_DIM, HEAD_DIM, 0)
    router_w = lax.all_gather(router, BOTH, axis=0, tiled=True)
    gate_w = dp_join(w_gate[0])
    up_w = dp_join(w_up[0])
    down_w = dp_join(w_down[0])

    token_f = tokens.astype(F32)
    first_scale = inverse_rms(token_f)
    normed = (token_f * first_scale * attn_g[None, :]).astype(BF16)
    normed_all = own_part(tree_gather(normed, 1))
    pre = mm(normed_all, w_head)
    query_pre, key_pre = pre[:, :HEAD_DIM], pre[:, HEAD_DIM : 2 * HEAD_DIM]
    values = pre[:, 2 * HEAD_DIM :].astype(BF16)
    squares = jnp.stack([jnp.sum(query_pre**2, axis=-1), jnp.sum(key_pre**2, axis=-1)])
    scales = lax.rsqrt(head_sum(squares, 2) / width + EPSILON)
    query_scale, key_scale = scales[0][:, None], scales[1][:, None]
    queries = turn(query_pre * query_scale * my_query_g, cosine, sine).astype(BF16)
    keys = turn(key_pre * key_scale * my_key_g, cosine, sine).astype(BF16)
    if share > 1:
        keys_all = lax.all_gather(keys, "expert", axis=0, tiled=True, axis_index_groups=siblings)
        values_all = lax.all_gather(values, "expert", axis=0, tiled=True, axis_index_groups=siblings)
    else:
        keys_all, values_all = keys, values
    turns = max(1, tree_rows // 2048)

    def cut_rows(values):
        return values.reshape(turns, own_rows // turns, -1)

    def attend(cut):
        return attention(*cut, keys_all, values_all)

    if turns == 1:
        attn, log_total = attention(queries, mask, keys_all, values_all)
    else:
        attn, log_total = lax.map(attend, (cut_rows(queries), cut_rows(mask)))
        attn, log_total = attn.reshape(own_rows, HEAD_DIM), log_total.reshape(own_rows, 1)
    mixed_head = attn.astype(BF16)

    def to_owners(block):
        cut = block.reshape(own_segs, rows, -1)
        if share > 1:
            cut = lax.dynamic_update_slice_in_dim(
                jnp.zeros((group, *cut.shape[1:]), cut.dtype), cut, first_seg, 0
            )
        got = expert_swap(cut, 3)
        if share > 1:
            got = jnp.sum(got.reshape(heads, share, rows, -1), axis=1, dtype=cut.dtype)
        return got

    mixed = to_owners(mixed_head).transpose(1, 0, 2).reshape(rows, width)
    residual = token_f + mm(mixed, out_w)
    second_scale = inverse_rms(residual)
    normed_two = (residual * second_scale * ffn_g[None, :]).astype(BF16)
    logits = mm(normed_two, router_w)
    router_probs = jax.nn.softmax(logits, axis=-1)
    experts = router_w.shape[1]
    labels = jnp.arange(experts, dtype=jnp.int32)
    routed = jnp.any(routes[:, :, None] == labels[None, None, :], axis=1)
    gates_own = jnp.where(routed, router_probs, 0.0)
    gates = expert_swap(gates_own.T[:, None], 4).reshape(tree_rows, 1)

    rows_in = tree_gather(normed_two, 5)
    cot_in = lax.all_gather(cotangent, "expert", axis=0, tiled=True)
    pieces = max(1, tree_rows // 2048)
    if pieces == 1:
        (sent_out, gate_grad, row_grad), sums = expert_step(
            rows_in, cot_in, gates, gate_w, up_w, down_w
        )
    else:

        def expert_turn(sums, cut):
            result, more = expert_step(*cut, gate_w, up_w, down_w)
            return tuple(s + m for s, m in zip(sums, more)), result

        zeros = tuple(jnp.zeros(w.shape, F32) for w in (gate_w, up_w, down_w))
        cuts = tuple(v.reshape(pieces, -1, v.shape[1]) for v in (rows_in, cot_in, gates))
        sums, results = lax.scan(expert_turn, zeros, cuts)
        sent_out, gate_grad, row_grad = (
            r.reshape(tree_rows, *r.shape[2:]) for r in results
        )
    gate_w_grad, up_w_grad, down_w_grad = (s.astype(BF16) for s in sums)
    combined = lax.psum_scatter(sent_out, "expert", scatter_dimension=0, tiled=True)
    output = (residual + combined.astype(F32)).astype(BF16)
    gate_grad_own = expert_swap(gate_grad.reshape(group, 1, rows), 6).reshape(group, rows).T
    expert_grad = tree_scatter(row_grad, 7)
    grad_gate, grad_up, grad_down = (
        dp_sum(g).astype(F32)[None]
        for g in (gate_w_grad, up_w_grad, down_w_grad)
    )

    prob_grad = jnp.where(routed, gate_grad_own, 0.0)
    logit_grad = (
        router_probs * (prob_grad - jnp.sum(router_probs * prob_grad, axis=-1, keepdims=True))
    ).astype(BF16)
    router_grad = t_mm(normed_two, logit_grad)
    normed_two_grad = expert_grad + mm_t(logit_grad, router_w)
    ffn_gain_grad = jnp.sum(normed_two_grad * residual * second_scale, axis=0)
    weighted = normed_two_grad * ffn_g[None, :]
    residual_grad = (
        cotangent.astype(F32)
        + second_scale * weighted
        - residual * second_scale**3 * jnp.mean(weighted * residual, axis=-1, keepdims=True)
    )
    proj_grad = residual_grad.astype(BF16)

    proj_all = own_part(tree_gather(proj_grad, 8))
    mixed_grad = mm_t(proj_all, out_head).astype(BF16)
    out_w_grad = t_mm(mixed_head, proj_all)
    row_delta = jnp.sum(mixed_grad.astype(F32) * attn, axis=-1, keepdims=True)
    back_args = (queries, mask, log_total, mixed_grad, row_delta)
    if turns == 1:
        query_grad, key_grad, value_grad = attention_back(*back_args, keys_all, values_all)
    else:

        def attention_turn(sums, cut):
            first, *more = attention_back(*cut, keys_all, values_all)
            return tuple(s + m for s, m in zip(sums, more)), first

        zeros = jnp.zeros((tree_rows, HEAD_DIM), F32)
        (key_grad, value_grad), query_grad = lax.scan(
            attention_turn, (zeros, zeros), tuple(cut_rows(v) for v in back_args)
        )
        query_grad = query_grad.reshape(own_rows, HEAD_DIM)
    if share > 1:
        key_grad = lax.psum_scatter(
            key_grad, "expert", scatter_dimension=0, tiled=True, axis_index_groups=siblings
        )
        value_grad = lax.psum_scatter(
            value_grad, "expert", scatter_dimension=0, tiled=True, axis_index_groups=siblings
        )
    query_turned = turn(query_grad, cosine, -sine)
    key_turned = turn(key_grad, cosine, -sine)
    dots = jnp.stack(
        [
            jnp.sum(query_turned * my_query_g * query_pre, axis=-1),
            jnp.sum(key_turned * my_key_g * key_pre, axis=-1),
        ]
    )
    means = head_sum(dots, 9) / width
    query_low = query_scale * my_query_g * query_turned - query_pre * query_scale**3 * means[0][:, None]
    key_low = key_scale * my_key_g * key_turned - key_pre * key_scale**3 * means[1][:, None]
    low = jnp.concatenate([query_low, key_low, value_grad], axis=1).astype(BF16)
    query_gain_grad = jnp.sum(query_turned * query_pre * query_scale, axis=0)
    key_gain_grad = jnp.sum(key_turned * key_pre * key_scale, axis=0)
    normed_part = mm_t(low, w_head).astype(BF16)
    if share > 1:
        normed_part = lax.dynamic_update_slice_in_dim(
            jnp.zeros((tree_rows, width), BF16), normed_part, first_seg * rows, 0
        )
    normed_grad = tree_scatter(normed_part, 10)
    attn_gain_grad = jnp.sum(normed_grad * token_f * first_scale, axis=0)
    weighted = normed_grad * attn_g[None, :]
    token_grad = (
        residual_grad
        + first_scale * weighted
        - token_f * first_scale**3 * jnp.mean(weighted * token_f, axis=-1, keepdims=True)
    )

    head_grad = t_mm(normed_all, low)
    got = both_swap(head_grad.reshape(devices, shard, 3 * HEAD_DIM), 11).reshape(n_dp, heads, share, shard, 3, HEAD_DIM)
    got = jnp.sum(got, axis=(0, 2)).transpose(2, 1, 0, 3).reshape(3, shard, width)
    shards_a_head = HEAD_DIM // shard
    source = dp * share + part
    flat = [(d, h * share + j) for d in range(n_dp) for h in range(heads) for j in range(share)]
    grad_out = jnp.zeros((shard, width), F32)
    for turn_index in range(shards_a_head):
        pairs = []
        for d, e in flat:
            s = d * share + e % share
            target = (e // share) * shards_a_head + (s + turn_index) % shards_a_head
            pairs.append((d * group + e, target))
        block = lax.dynamic_slice_in_dim(
            out_w_grad, ((source + turn_index) % shards_a_head) * shard, shard, 0
        )
        grad_out = grad_out + lax.ppermute(block, BOTH, pairs)
    head_gains = jnp.stack([query_gain_grad, key_gain_grad], axis=1)
    head_gains = lax.dynamic_update_slice_in_dim(
        jnp.zeros((width, 2), F32), head_gains, head * HEAD_DIM, 0
    )
    small = jnp.concatenate(
        [router_grad, attn_gain_grad[:, None], head_gains, ffn_gain_grad[:, None]], axis=1
    )
    small = jnp.sum(both_swap(small.reshape(devices, shard, -1), 12), axis=0)
    return (
        output,
        token_grad,
        small[:, experts],
        small[:, experts + 1],
        small[:, experts + 2],
        small[:, experts + 3],
        got[0],
        got[1],
        got[2],
        grad_out,
        small[:, :experts],
        grad_gate,
        grad_up,
        grad_down,
    )


def solution(mesh):
    row, vec = P(BOTH, None), P(BOTH)
    expert = P("expert", "dp", None)
    return jax.shard_map(
        per_device,
        mesh=mesh,
        in_specs=(row, vec, vec, vec, vec, row, row, row, row, row, expert, expert, expert, row, row, P()),
        out_specs=(row, row, vec, vec, vec, vec, row, row, row, row, row, expert, expert, expert),
        check_vma=False,
    )
```

time: 2460 us -> 1010 us (0.41)
  waiting for transfers between devices: 1520 us -> 1.44 us
  Pallas kernels: 0 us -> 568 us
  blocking collectives: 320 us -> 85.4 us
  local copies, waits for them, and re-layouts: 142 us -> 43.8 us
  matrix products: 307 us -> 210 us
  starting transfers between devices: 50 us -> 12.7 us
  other arithmetic: 98.3 us -> 61.8 us
    reduce_scatter x7 -> x1, waiting for transfers between devices: 768 us -> 0.01 us  [per_device(): lax.psum_scatter(sent_out, 'expert', scatter_dimension=0, tiled=True)]
    pallas_call x0 -> x13, Pallas kernels: none -> 568 us  [the longest x8 224 us: swap(): pl.pallas_call(functools.partial(swap_kernel, axes, sizes), out_shape=jax...]
    all_gather x11 -> x2, waiting for transfers between devices: 415 us -> 0.02 us  [the longest x1 0.02 us: per_device(): cot_in = lax.all_gather(cotangent, 'expert', axis=0, tiled=True)]
    all_to_all x4 -> x0, waiting for transfers between devices: 329 us -> none  [the longest x1 159 us: per_device(): lax.all_to_all(send_grads, 'expert', split_axis=0, concat_axis=0, tiled=T...]
    all_gather x3 -> x2, blocking collectives: 231 us -> 85.4 us  [the longest x1 43 us: per_device(): router_w = lax.all_gather(router, BOTH, axis=0, tiled=True)]
    dot_general x57 -> x29, matrix products: 306 us -> 210 us  [the longest x8 80.6 us: mm_t(): lax.dot_general(a, b, (((1,), (1,)), ((), ())), preferred_element_type=F32)]
    unnamed x2 -> x0, blocking collectives: 89 us -> none
    dynamic_slice x20 -> x1, local copies, waits for them, and re-layouts: 52.8 us -> 1.06 us  [per_device(): lax.dynamic_slice_in_dim(out_w_grad, (source + turn_index) % shards_a_hea...]
  transfers between devices with their start and end apart: 23 -> 11, of which waited for: 17 -> 0; matrix products, arithmetic and copies ran while one was open for 19% -> 24% of each run, Pallas kernels for 0% -> 51%
where the time goes in v1:
time: 1010 us; the launch traced here: 999 us
  Pallas kernels  568 us (56%)
  matrix products  210 us (21%)
  blocking collectives  85.4 us (8%)
  other arithmetic  61.8 us (6%)
  local copies, waits for them, and re-layouts  43.8 us (4%)
  between operations  15.6 us (2%)
  starting transfers between devices  12.7 us (1%)
    pallas_call x8, Pallas kernels, swap(): pl.pallas_call(functools.partial(swap_kernel, axes, sizes), out_shape=jax...  224 us
    pallas_call x3, Pallas kernels, gather(): pl.pallas_call(functools.partial(gather_kernel, group // 4), out_shape=ja...  213 us
    pallas_call x2, Pallas kernels, scatter(): pl.pallas_call(functools.partial(scatter_kernel, zs), out_shape=jax.Shape...  131 us
    dot_general x8, matrix products, mm_t(): lax.dot_general(a, b, (((1,), (1,)), ((), ())), preferred_element_type=F32)  80.6 us
    dot_general x8, matrix products, mm(): lax.dot_general(a, b, (((1,), (0,)), ((), ())), preferred_element_type=F32)  70 us
    dot_general x8, matrix products, t_mm(): lax.dot_general(a, b, (((0,), (0,)), ((), ())), preferred_element_type=F32)  59.1 us
    all_gather x1, blocking collectives, per_device(): router_w = lax.all_gather(router, BOTH, axis=0, tiled=True)  43 us
    all_gather x1, blocking collectives, per_device(): lax.all_gather(jnp.stack([attn_gain, q_gain, k_gain, ffn_gain], axis=1),...  42.4 us
  transfers between devices with their start and end apart: 11, of which 0 were waited for; matrix products, arithmetic and copies ran while one was open for 24% of the time, Pallas kernels for 51%

profile of v1, /device:TPU:4, one launch (start us, length us, event | category | flops | bytes accessed | tf_op | source)
XLA Modules:
  0.0 999.3 jit_solution(10877220766354578222)
XLA Ops:
  8.8 2.0 collective-permute-start.2
  11.6 42.4 %all-gather = bf16[32,64,4]{1,2,0:T(4,128)(2,1)S(1)} all-gather(bf16[1,64,4]{1,2,0:T(4,128)(2,1)S(1)} %maximum_bitcast_fusion.3), channel_id=1, replica_groups=mesh['dp'=2,'expert'=16] {'dp','expert'}, dimensions={0}, use_global_device_ids=true | all-gather | bytes 16896 | tf_op jit(solution)/shard_map/all_gather | solution.py:433
  54.1 1.2 fusion.26
  56.5 2.0 fusion.28.in_ref
  58.6 82.3 %shard_map.263 = bf16[16,128,2048]{2,1,0:T(8,128)(2,1)} custom-call(bf16[128,2048]{1,0:T(8,128)(2,1)} %fusion.28.in_ref), custom_call_target="tpu_custom_call" | custom-call | tf_op jit(solution)/shard_map/pallas_call | solution.py:124
  142.5 1.8 maximum_bitcast_fusion
  145.5 55.5 %shard_map.264 = bf16[32,64,384]{2,1,0:T(8,128)(2,1)S(1)} custom-call(bf16[32,64,384]{2,1,0:T(8,128)(2,1)S(1)} %bitcast.180), custom_call_target="tpu_custom_call" | custom-call | tf_op jit(solution)/shard_map/pallas_call | solution.py:293
  201.0 6.5 fusion.95
  207.8 24.4 %shard_map.265 = f32[16,2,2048]{2,1,0:T(2,128)S(1)} custom-call(f32[1,2,2048]{2,1,0:T(2,128)S(1)} %maximum_bitcast_fusion.1.in_ref), custom_call_target="tpu_custom_call" | custom-call | tf_op jit(solution)/shard_map/pallas_call | solution.py:293
  234.0 2.4 fusion.59
  236.5 2.5 fusion.8
  239.1 7.3 fusion.5
  246.4 4.9 fusion.93
  251.3 43.0 %all-gather.1 = bf16[32,64,16]{1,2,0:T(8,128)(2,1)S(1)} all-gather(bf16[1,64,16]{1,2,0:T(8,128)(2,1)S(1)} %bitcast.251), channel_id=1, replica_groups=mesh['dp'=2,'expert'=16] {'dp','expert'}, dimensions={0}, use_global_device_ids=true | all-gather | bytes 67584 | tf_op jit(solution)/shard_map/all_gather | solution.py:447
  294.3 12.3 %shard_map.266 = bf16[16,128,128]{2,1,0:T(8,128)(2,1)S(1)} custom-call(bf16[16,128,128]{2,1,0:T(8,128)(2,1)S(1)} %bitcast.181), custom_call_target="tpu_custom_call" | custom-call | tf_op jit(solution)/shard_map/pallas_call | solution.py:293
  307.1 12.3 %fusion.7 = bf16[2048,2048]{0,1:T(8,128)(2,1)} fusion(f32[2048,2048]{0,1:T(8,128)} %copy-done.4, f32[2048]{0:T(1024)S(1)} %log_add_fusion, pred[2048,16]{0,1:T(8,128)(4,1)S(1)} %bitcast.222), kind=kLoop, calls=%fused_computation.15 | loop fusion | flops 25165824 | bytes 25206784 | tf_op jit(solution)/shard_map/convert_element_type | solution.py:326
  319.5 12.4 %copy.123 = bf16[2048,2048]{1,0:T(8,128)(2,1)} copy(bf16[2048,2048]{0,1:T(8,128)(2,1)} %bitcast.195) | data formatting | bytes 16777216 | tf_op jit(solution)/shard_map/dot_general | solution.py:30
  332.4 4.7 multiply_reduce_fusion.7
  339.1 69.5 %shard_map.268 = bf16[16,128,2048]{2,1,0:T(8,128)(2,1)} custom-call(bf16[128,2048]{1,0:T(8,128)(2,1)} %multiply_convert_fusion.2.in_ref), custom_call_target="tpu_custom_call" | custom-call | tf_op jit(solution)/shard_map/pallas_call | solution.py:124
  409.5 6.6 shard_map.267
  416.1 16.1 %fusion.53 = f32[2048,1024]{1,0:T(8,128)} fusion(bf16[2048,2048]{1,0:T(8,128)(2,1)} %bitcast.201, bf16[1024,1024]{1,0:T(8,128)(2,1)} %collective-permute-done, bf16[1024,1024]{1,0:T(8,128)(2,1)} %bitcast.265, pred[]{:T(512)S(6)} %eq.45), kind=kOutput, calls=%fused_computation.118 | convolution fusion | flops 8608808960 | bytes 20971520 | tf_op jit(solution)/shard_map/dot_general | solution.py:22
  432.3 16.3 %convolution_convert_fusion.3 = bf16[2048,1024]{1,0:T(8,128)(2,1)} fusion(bf16[2048,2048]{1,0:T(8,128)(2,1)} %all-gather.7.cloned.1.call-done, f32[2048]{0:T(1024)S(1)} %bitcast.189, bf16[512,2048]{1,0:T(8,128)(2,1)} %collective-permute-done.2, bf16[512,2048]{1,0:T(8,128)(2,1)S(1)} %bitcast.259, pred[]{:T(512)S(6)} %eq.45), kind=kOutput, calls=%fused_computation.38 | convolution fusion | flops 8623489024 | bytes 16785408 | tf_op jit(solution)/shard_map/dot_general | solution.py:26
  448.6 20.7 %fusion.11 = (bf16[2048,1024]{1,0:T(8,128)(2,1)}, bf16[2048,1024]{1,0:T(8,128)(2,1)}) fusion(bf16[2048,1024]{1,0:T(8,128)(2,1)} %convolution_convert_fusion.3, f32[2048,1024]{1,0:T(8,128)} %fusion.53, bf16[2048,2048]{1,0:T(8,128)(2,1)} %bitcast.202, bf16[1024,1024]{1,0:T(8,128)(2,1)} %collective-permute-done.1, bf16[1024,1024]{1,0:T(8,128)(2,1)S(1)} %bitcast.262, ...), kind=kOutput, calls=%fused_computation.21 | convolution fusion | flops 8638169088 | bytes 33554432 | tf_op jit(solution)/shard_map/dot_general | solution.py:22
  469.3 13.1 %convolution_convert_fusion.2 = bf16[1024,2048]{1,0:T(8,128)(2,1)S(1)} fusion(bf16[2048,1024]{1,0:T(8,128)(2,1)} %get-tuple-element.91, bf16[2048,2048]{1,0:T(8,128)(2,1)} %all-gather.7.cloned.1.call-done, f32[2048]{0:T(1024)S(1)} %bitcast.190), kind=kOutput, calls=%fused_computation.37 | convolution fusion | flops 8604614656 | bytes 16785408 | tf_op jit(solution)/shard_map/dot_general | solution.py:30
  482.5 1.5 dynamic-slice_bitcast_fusion
  483.9 1.6 copy-done.22
  486.8 15.6 %fusion.2 = (f32[2048]{0:T(1024)S(1)}, bf16[2048,2048]{1,0:T(8,128)(2,1)}) fusion(bf16[2048,2048]{1,0:T(8,128)(2,1)} %all-gather.7.cloned.1.call-done, f32[2048]{0:T(1024)S(1)} %bitcast.191, bf16[2048,1024]{1,0:T(8,128)(2,1)S(1)} %copy-done.85, bf16[512,2048]{1,0:T(8,128)(2,1)} %collective-permute-done.2, bf16[512,2048]{1,0:T(8,128)(2,1)S(1)} %bitcast.260, ...), kind=kOutput, calls=%fused_computation.5 | convolution fusion | flops 8638167040 | bytes 25182208 | tf_op jit(solution)/shard_map/dot_general | solution.py:22
  502.4 14.8 %convolution_convert_fusion.4 = bf16[2048,1024]{1,0:T(8,128)(2,1)S(1)} fusion(bf16[2048,2048]{1,0:T(8,128)(2,1)} %bitcast.203, bf16[2048,1024]{1,0:T(8,128)(2,1)} %convolution_convert_fusion.3, f32[2048,1024]{1,0:T(8,128)} %fusion.53), kind=kOutput, calls=%fused_computation.39 | convolution fusion | flops 8606711808 | bytes 25165824 | tf_op jit(solution)/shard_map/dot_general | solution.py:30
  517.2 1.5 dynamic-slice_bitcast_fusion.1
  518.7 1.0 collective-permute-start.6
  519.7 2.3 copy-done.86
  522.0 12.2 %convolution_convert_fusion.5 = bf16[2048,1024]{1,0:T(8,128)(2,1)S(1)} fusion(bf16[2048,2048]{1,0:T(8,128)(2,1)} %bitcast.204, bf16[2048,1024]{1,0:T(8,128)(2,1)S(1)} %copy-done.86), kind=kOutput, calls=%fused_computation.40 | convolution fusion | flops 8592031744 | bytes 16777216 | tf_op jit(solution)/shard_map/dot_general | solution.py:30
  534.3 2.1 copy-done.25
  536.4 1.5 dynamic-slice_bitcast_fusion.2
  538.7 18.8 %fusion.51 = f32[2048,2048]{1,0:T(8,128)} fusion(bf16[1024,1024]{1,0:T(8,128)(2,1)} %collective-permute-done.1, bf16[1024,1024]{1,0:T(8,128)(2,1)S(1)} %bitcast.263, pred[]{:T(512)S(6)} %eq.45, bf16[2048,1024]{1,0:T(8,128)(2,1)} %convolution_convert_fusion.3, f32[2048,1024]{1,0:T(8,128)} %fusion.53), kind=kOutput, calls=%fused_computation.116 | convolution fusion | flops 8623489024 | bytes 33554432 | tf_op jit(solution)/shard_map/dot_general | solution.py:26
  557.5 20.5 %add_convert_fusion = bf16[2048,2048]{1,0:T(8,128)(2,1)} fusion(f32[2048,2048]{1,0:T(8,128)} %fusion.51, bf16[2048,1024]{1,0:T(8,128)(2,1)} %get-tuple-element.90, bf16[1024,1024]{1,0:T(8,128)(2,1)} %collective-permute-done, bf16[1024,1024]{1,0:T(8,128)(2,1)} %bitcast.266, pred[]{:T(512)S(6)} %eq.45), kind=kOutput, calls=%fused_computation.8 | convolution fusion | flops 8617197568 | bytes 33554432 | tf_op jit(solution)/shard_map/dot_general | solution.py:26
  578.0 6.8 shard_map.270
  585.0 61.0 %shard_map.269 = f32[128,2048]{1,0:T(8,128)S(1)} custom-call(bf16[16,128,2048]{2,1,0:T(8,128)(2,1)} %bitcast.197), custom_call_target="tpu_custom_call" | custom-call | tf_op jit(solution)/shard_map/pallas_call | solution.py:215
  647.7 5.3 fusion.15
  653.1 4.7 fusion.16
  657.7 4.4 fusion.14
  662.1 2.9 fusion.88
  665.1 61.0 %shard_map.271 = bf16[16,128,2048]{2,1,0:T(8,128)(2,1)} custom-call(bf16[128,2048]{1,0:T(8,128)(2,1)} %get-tuple-element.86.in_ref), custom_call_target="tpu_custom_call" | custom-call | tf_op jit(solution)/shard_map/pallas_call | solution.py:124
  726.1 4.8 fusion.96
  732.1 3.7 multiply_reduce_fusion.5
  735.9 11.3 %multiply_convert_fusion = bf16[2048,2048]{0,1:T(8,128)(2,1)S(1)} fusion(f32[2048,2048]{0,1:T(8,128)} %copy-done.4, bf16[2048,128]{1,0:T(8,128)(2,1)S(1)} %get-tuple-element.138, f32[2048]{0:T(1024)S(1)} %get-tuple-element.137, f32[2048]{0:T(1024)S(1)} %copy-done.55, pred[2048,16]{0,1:T(8,128)(4,1)S(1)} %bitcast.223, f32[2048,384]{0,1:T(8,128)S(1)} %copy-done.7), kind=kOutput, calls=%fused_computation.6 | convolution fusion | flops 1107296256 | bytes 26263552 | tf_op jit(solution)/shard_map/dot_general | solution.py:26
  747.2 2.9 convolution_multiply_fusion.1
  750.1 1.3 convolution_multiply_fusion
  751.5 1.1 constant_dynamic-slice_fusion
  752.5 4.3 collective-permute-start.3
  756.8 3.6 collective-permute-start.4
  760.4 2.4 fusion.54
  764.2 22.1 %shard_map.272 = f32[16,2,2048]{2,1,0:T(2,128)S(1)} custom-call(f32[1,2,2048]{2,1,0:T(2,128)S(1)} %maximum_bitcast_fusion.2.in_ref), custom_call_target="tpu_custom_call" | custom-call | tf_op jit(solution)/shard_map/pallas_call | solution.py:293
  786.5 6.5 convolution_convert_fusion.6
  794.4 6.9 convolution_convert_fusion
  801.3 4.7 fusion.19.in_ref
  806.1 70.1 %shard_map.275 = f32[32,64,384]{2,1,0:T(8,128)S(1)} custom-call(f32[32,64,384]{2,1,0:T(8,128)S(1)} %fusion.19.in_ref), custom_call_target="tpu_custom_call" | custom-call | tf_op jit(solution)/shard_map/pallas_call | solution.py:293
  876.2 3.2 reshape.240
  879.4 4.0 reduce_sum.219
  883.4 1.6 fusion.89
  888.9 70.2 %shard_map.273 = f32[128,2048]{1,0:T(8,128)S(1)} custom-call(bf16[16,128,2048]{2,1,0:T(8,128)(2,1)} %bitcast.196), custom_call_target="tpu_custom_call" | custom-call | tf_op jit(solution)/shard_map/pallas_call | solution.py:215
  959.9 26.3 %shard_map.274 = f32[32,64,20]{2,1,0:T(8,128)S(1)} custom-call(f32[32,64,20]{2,1,0:T(8,128)S(1)} %copy.122.in_ref), custom_call_target="tpu_custom_call" | custom-call | tf_op jit(solution)/shard_map/pallas_call | solution.py:293
  987.7 2.7 fusion.30
  990.4 2.0 add.208
  (271 shorter events, 26.4 us)
Async XLA Ops:
  7.2 325.3 %all-gather.5.cloned.1.call-start = ((), (), s32[]{:S(2)}) async-start(), calls=%async_computation.1 | async-start | bytes 8650752 | tf_op jit(solution)/shard_map/all_gather | solution.py:445
  7.9 424.3 %all-gather.7.cloned.1.call-start = ((), (), s32[]{:S(2)}) async-start(), calls=%async_computation.3 | async-start | bytes 8912896 | tf_op jit(solution)/shard_map/all_gather | solution.py:508
  8.7 653.4 %reduce-scatter.2.cloned.1.call-start = ((), (), s32[]{:S(2)}) async-start(), calls=%async_computation.2 | async-start | bytes 8912896 | tf_op jit(solution)/shard_map/reduce_scatter | solution.py:527
  8.7 407.4 %collective-permute-start = (bf16[1024,1024]{1,0:T(8,128)(2,1)}, bf16[1024,1024]{1,0:T(8,128)(2,1)}, u32[]{:S(2)}, u32[]{:S(2)}) collective-permute-start(bf16[1024,1024]{1,0:T(8,128)(2,1)} %bitcast.264), channel_id=1, source_target_pairs={{0,16},{16,0},{1,17},{17,1},{2,18},{18,2},{3,19},{19,3},{4,20},{20... | collective-permute-start | bytes 6291464 | tf_op jit(solution)/shard_map/ppermute | solution.py:420
  8.8 423.4 %collective-permute-start.2 = (bf16[512,2048]{1,0:T(8,128)(2,1)}, bf16[512,2048]{1,0:T(8,128)(2,1)}, u32[]{:S(2)}, u32[]{:S(2)}) collective-permute-start(bf16[512,2048]{1,0:T(8,128)(2,1)} %bitcast.258), channel_id=1, source_target_pairs={{0,16},{16,0},{1,17},{17,1},{2,18},{18,2},{3,19},{19,3},{4,20},{20... | collective-permute-start | bytes 6291464 | tf_op jit(solution)/shard_map/ppermute | solution.py:420
  10.8 437.8 %collective-permute-start.1 = (bf16[1024,1024]{1,0:T(8,128)(2,1)}, bf16[1024,1024]{1,0:T(8,128)(2,1)}, u32[]{:S(2)}, u32[]{:S(2)}) collective-permute-start(bf16[1024,1024]{1,0:T(8,128)(2,1)} %bitcast.261), channel_id=1, source_target_pairs={{0,16},{16,0},{1,17},{17,1},{2,18},{18,2},{3,19},{19,3},{4,20},{20... | collective-permute-start | bytes 6291464 | tf_op jit(solution)/shard_map/ppermute | solution.py:420
  55.9 84.9 %copy-start.70 = (f32[128]{0:T(128)}, f32[128]{0:T(128)S(1)}, u32[]{:S(2)}) copy-start(f32[128]{0:T(128)S(1)} %get-tuple-element.125) | copy-start | bytes 1540
  56.0 281.8 %copy-start.52 = (f32[2048,1]{0,1:T(1,128)}, f32[2048,1]{0,1:T(1,128)S(1)}, u32[]{:S(2)}) copy-start(f32[2048,1]{0,1:T(1,128)S(1)} %get-tuple-element.112) | copy-start | bytes 24580
  58.6 82.3 %copy-start.41 = (bf16[64,2048]{1,0:T(8,128)(2,1)S(1)}, bf16[64,2048]{1,0:T(8,128)(2,1)}, u32[]{:S(2)}) copy-start(bf16[64,2048]{1,0:T(8,128)(2,1)} %param.21) | copy-start | bytes 786436
  58.6 82.8 %copy-start.42 = (bf16[64,2048]{1,0:T(8,128)(2,1)S(1)}, bf16[64,2048]{1,0:T(8,128)(2,1)}, u32[]{:S(2)}) copy-start(bf16[64,2048]{1,0:T(8,128)(2,1)} %param.22) | copy-start | bytes 786436
  58.6 83.4 %copy-start.43 = (bf16[64,2048]{1,0:T(8,128)(2,1)S(1)}, bf16[64,2048]{1,0:T(8,128)(2,1)}, u32[]{:S(2)}) copy-start(bf16[64,2048]{1,0:T(8,128)(2,1)} %param.23) | copy-start | bytes 786436
  201.0 31.2 %copy-start.83 = (s32[32]{0:T(128)S(1)}, s32[32]{0:T(128)}, u32[]{:S(2)}) copy-start(s32[32]{0:T(128)} %param.31) | copy-start | bytes 388
  207.5 28.9 %copy-start.6 = (f32[2048,384]{0,1:T(8,128)}, f32[2048,384]{0,1:T(8,128)S(1)}, u32[]{:S(2)}) copy-start(f32[2048,384]{0,1:T(8,128)S(1)} %fusion.95) | copy-start | bytes 9437188
  233.3 73.8 %copy-start.37 = (pred[2,8,16,128]{3,1,2,0:T(8,128)(4,1)}, pred[2,8,16,128]{3,1,2,0:T(8,128)(4,1)S(1)}, u32[]{:S(2)}) copy-start(pred[2,8,16,128]{3,1,2,0:T(8,128)(4,1)S(1)} %copy.149) | copy-start | bytes 98308
  233.7 98.1 %copy-start.44 = (f32[1,2048]{1,0:T(1,128)}, f32[1,2048]{1,0:T(1,128)S(1)}, u32[]{:S(2)}) copy-start(f32[1,2048]{1,0:T(1,128)S(1)} %get-tuple-element.118) | copy-start | bytes 24580
  233.7 98.1 %copy-start.46 = (f32[1,2048]{1,0:T(1,128)}, f32[1,2048]{1,0:T(1,128)S(1)}, u32[]{:S(2)}) copy-start(f32[1,2048]{1,0:T(1,128)S(1)} %get-tuple-element.119) | copy-start | bytes 24580
  239.0 7.3 copy-start.4
  239.1 7.3 copy-start.75
  246.4 162.6 %copy-start.60 = (pred[128,16]{0,1:T(8,128)(4,1)}, pred[128,16]{0,1:T(8,128)(4,1)S(1)}, u32[]{:S(2)}) copy-start(pred[128,16]{0,1:T(8,128)(4,1)S(1)} %fusion.68) | copy-start | bytes 6148
  246.4 60.7 %copy-start.54 = (f32[2048]{0:T(1024)}, f32[2048]{0:T(1024)S(1)}, u32[]{:S(2)}) copy-start(f32[2048]{0:T(1024)S(1)} %log_add_fusion) | copy-start | bytes 24580
  251.3 68.2 %copy-start = (bf16[2048,128]{1,0:T(8,128)(2,1)}, bf16[2048,128]{1,0:T(8,128)(2,1)S(1)}, u32[]{:S(2)}) copy-start(bf16[2048,128]{1,0:T(8,128)(2,1)S(1)} %get-tuple-element.130) | copy-start | bytes 1572868
  307.1 101.5 %copy-start.39 = (bf16[2048,16]{0,1:T(8,128)(2,1)}, bf16[2048,16]{0,1:T(8,128)(2,1)S(1)}, u32[]{:S(2)}) copy-start(bf16[2048,16]{0,1:T(8,128)(2,1)S(1)} %reshape.250) | copy-start | bytes 196612
  319.5 13.0 %copy-start.10 = (bf16[128,2048]{1,0:T(8,128)(2,1)S(1)}, bf16[128,2048]{1,0:T(8,128)(2,1)}, u32[]{:S(2)}) copy-start(bf16[128,2048]{1,0:T(8,128)(2,1)} %param.16) | copy-start | bytes 1572868
  339.1 69.5 %copy-start.12 = (bf16[128,2048]{1,0:T(8,128)(2,1)S(1)}, bf16[128,2048]{1,0:T(8,128)(2,1)}, u32[]{:S(2)}) copy-start(bf16[128,2048]{1,0:T(8,128)(2,1)} %multiply_convert_fusion.2.in_ref) | copy-start | bytes 1572868
  408.9 23.3 %copy-start.62 = (f32[128]{0:T(128)}, f32[128]{0:T(128)S(1)}, u32[]{:S(2)}) copy-start(f32[128]{0:T(128)S(1)} %get-tuple-element.134) | copy-start | bytes 1540
  408.9 23.2 %copy-start.64 = (f32[128]{0:T(128)}, f32[128]{0:T(128)S(1)}, u32[]{:S(2)}) copy-start(f32[128]{0:T(128)S(1)} %fusion.71) | copy-start | bytes 1540
  416.1 16.1 %copy-start.80 = (bf16[1,512,2048]{2,1,0:T(8,128)(2,1)S(1)}, bf16[1,512,2048]{2,1,0:T(8,128)(2,1)}, u32[]{:S(2)}) copy-start(bf16[1,512,2048]{2,1,0:T(8,128)(2,1)} %param.28) | copy-start | bytes 6291460
  432.2 16.4 %copy-start.81 = (bf16[1,1024,1024]{2,1,0:T(8,128)(2,1)S(1)}, bf16[1,1024,1024]{2,1,0:T(8,128)(2,1)}, u32[]{:S(2)}) copy-start(bf16[1,1024,1024]{2,1,0:T(8,128)(2,1)} %param.27) | copy-start | bytes 6291460
  485.6 172.2 %collective-permute-start.7 = (bf16[512,2048]{1,0:T(8,128)(2,1)}, bf16[512,2048]{1,0:T(8,128)(2,1)}, u32[]{:S(2)}, u32[]{:S(2)}) collective-permute-start(bf16[512,2048]{1,0:T(8,128)(2,1)} %dynamic-slice_bitcast_fusion), channel_id=1, source_target_pairs={{0,16},{16,0},{1,17},{17,1},{2,18},{18,2},{3,19},{19,3},{4,20},{20... | collective-permute-start | bytes 6291464 | tf_op jit(solution)/shard_map/ppermute | solution.py:431
  517.2 17.0 %copy-start.24 = (bf16[2048,1024]{1,0:T(8,128)(2,1)}, bf16[2048,1024]{1,0:T(8,128)(2,1)S(1)}, u32[]{:S(2)}) copy-start(bf16[2048,1024]{1,0:T(8,128)(2,1)S(1)} %convolution_convert_fusion.4) | copy-start | bytes 12582916
  518.7 129.0 %collective-permute-start.6 = (bf16[1024,1024]{1,0:T(8,128)(2,1)}, bf16[1024,1024]{1,0:T(8,128)(2,1)}, u32[]{:S(2)}, u32[]{:S(2)}) collective-permute-start(bf16[1024,1024]{1,0:T(8,128)(2,1)} %dynamic-slice_bitcast_fusion.1), channel_id=1, source_target_pairs={{0,16},{16,0},{1,17},{17,1},{2,18},{18,2},{3,19},{19,3},{4,20},{20... | collective-permute-start | bytes 6291464 | tf_op jit(solution)/shard_map/ppermute | solution.py:431
  537.9 115.2 %collective-permute-start.5 = (bf16[1024,1024]{1,0:T(8,128)(2,1)}, bf16[1024,1024]{1,0:T(8,128)(2,1)}, u32[]{:S(2)}, u32[]{:S(2)}) collective-permute-start(bf16[1024,1024]{1,0:T(8,128)(2,1)} %dynamic-slice_bitcast_fusion.2), channel_id=1, source_target_pairs={{0,16},{16,0},{1,17},{17,1},{2,18},{18,2},{3,19},{19,3},{4,20},{20... | collective-permute-start | bytes 6291464 | tf_op jit(solution)/shard_map/ppermute | solution.py:431
  584.9 61.1 %copy-start.49 = (f32[128,16]{0,1:T(8,128)S(1)}, f32[128,16]{0,1:T(8,128)}, u32[]{:S(2)}) copy-start(f32[128,16]{0,1:T(8,128)} %copy-done.48) | copy-start | bytes 24580
  584.9 61.1 %copy-start.61 = (pred[128,16]{0,1:T(8,128)(4,1)S(1)}, pred[128,16]{0,1:T(8,128)(4,1)}, u32[]{:S(2)}) copy-start(pred[128,16]{0,1:T(8,128)(4,1)} %copy-done.60) | copy-start | bytes 6148
  584.9 61.1 %copy-start.63 = (f32[128]{0:T(128)S(1)}, f32[128]{0:T(128)}, u32[]{:S(2)}) copy-start(f32[128]{0:T(128)} %copy-done.62) | copy-start | bytes 1540
  584.9 61.1 %copy-start.65 = (f32[128]{0:T(128)S(1)}, f32[128]{0:T(128)}, u32[]{:S(2)}) copy-start(f32[128]{0:T(128)} %copy-done.64) | copy-start | bytes 1540
  584.9 61.2 %copy-start.13 = (bf16[128,2048]{1,0:T(8,128)(2,1)S(1)}, bf16[128,2048]{1,0:T(8,128)(2,1)}, u32[]{:S(2)}) copy-start(bf16[128,2048]{1,0:T(8,128)(2,1)} %multiply_convert_fusion.2.in_ref) | copy-start | bytes 1572868
  584.9 62.2 %copy-start.9 = (f32[128,2048]{1,0:T(8,128)S(1)}, f32[128,2048]{1,0:T(8,128)}, u32[]{:S(2)}) copy-start(f32[128,2048]{1,0:T(8,128)} %copy-done.8) | copy-start | bytes 3145732
  584.9 62.2 %copy-start.40 = (bf16[2048,16]{0,1:T(8,128)(2,1)S(1)}, bf16[2048,16]{0,1:T(8,128)(2,1)}, u32[]{:S(2)}) copy-start(bf16[2048,16]{0,1:T(8,128)(2,1)} %copy-done.39) | copy-start | bytes 196612
  585.0 62.2 %copy-start.53 = (f32[2048,1]{0,1:T(1,128)S(1)}, f32[2048,1]{0,1:T(1,128)}, u32[]{:S(2)}) copy-start(f32[2048,1]{0,1:T(1,128)} %copy-done.52) | copy-start | bytes 24580
  585.0 62.2 %copy-start.73 = (f32[128]{0:T(128)S(1)}, f32[128]{0:T(128)}, u32[]{:S(2)}) copy-start(f32[128]{0:T(128)} %copy-done.72) | copy-start | bytes 1540
  665.1 61.0 %copy-start.1 = (bf16[2048,128]{1,0:T(8,128)(2,1)S(1)}, bf16[2048,128]{1,0:T(8,128)(2,1)}, u32[]{:S(2)}) copy-start(bf16[2048,128]{1,0:T(8,128)(2,1)} %copy-done) | copy-start | bytes 1572868
  735.8 11.3 %copy-start.31 = (bf16[2048,128]{1,0:T(8,128)(2,1)}, bf16[2048,128]{1,0:T(8,128)(2,1)S(1)}, u32[]{:S(2)}) copy-start(bf16[2048,128]{1,0:T(8,128)(2,1)S(1)} %get-tuple-element.138) | copy-start | bytes 1572868
  735.9 11.3 %copy-start.33 = (bf16[2048,64]{0,1:T(8,128)(2,1)S(1)}, bf16[2048,64]{0,1:T(8,128)(2,1)}, u32[]{:S(2)}) copy-start(bf16[2048,64]{0,1:T(8,128)(2,1)} %copy-done.32) | copy-start | bytes 786436
  735.9 11.3 %copy-start.35 = (bf16[2048,64]{0,1:T(8,128)(2,1)S(1)}, bf16[2048,64]{0,1:T(8,128)(2,1)}, u32[]{:S(2)}) copy-start(bf16[2048,64]{0,1:T(8,128)(2,1)} %copy-done.34) | copy-start | bytes 786436
  750.1 10.3 %copy-start.57 = (f32[2048]{0:T(1024)S(1)}, f32[2048]{0:T(1024)}, u32[]{:S(2)}) copy-start(f32[2048]{0:T(1024)} %copy-done.56) | copy-start | bytes 24580
  750.1 10.3 %copy-start.77 = (f32[64]{0:T(128)S(1)}, f32[64]{0:T(128)}, u32[]{:S(2)}) copy-start(f32[64]{0:T(128)} %copy-done.76) | copy-start | bytes 772
  751.4 11.5 %copy-start.45 = (f32[1,2048]{1,0:T(1,128)S(1)}, f32[1,2048]{1,0:T(1,128)}, u32[]{:S(2)}) copy-start(f32[1,2048]{1,0:T(1,128)} %copy-done.44) | copy-start | bytes 24580
  751.4 11.5 %copy-start.47 = (f32[1,2048]{1,0:T(1,128)S(1)}, f32[1,2048]{1,0:T(1,128)}, u32[]{:S(2)}) copy-start(f32[1,2048]{1,0:T(1,128)} %copy-done.46) | copy-start | bytes 24580
  751.5 11.5 %copy-start.67 = (f32[128]{0:T(128)S(1)}, f32[128]{0:T(128)}, u32[]{:S(2)}) copy-start(f32[128]{0:T(128)} %copy-done.66) | copy-start | bytes 1540
  751.5 11.5 %copy-start.69 = (f32[128]{0:T(128)S(1)}, f32[128]{0:T(128)}, u32[]{:S(2)}) copy-start(f32[128]{0:T(128)} %copy-done.68) | copy-start | bytes 1540
  752.5 237.9 %collective-permute-start.3 = (f32[64,2048]{1,0:T(8,128)}, f32[64,2048]{1,0:T(8,128)}, u32[]{:S(2)}, u32[]{:S(2)}) collective-permute-start(f32[64,2048]{1,0:T(8,128)} %get-tuple-element.110), channel_id=1, source_target_pairs={{0,0},{1,2},{2,4},{3,6},{4,8},{5,10},{6,12},{7,14},{8,16},{9,18},{... | collective-permute-start | bytes 1572872 | tf_op jit(solution)/shard_map/ppermute | solution.py:620
  756.8 233.6 %collective-permute-start.4 = (f32[64,2048]{1,0:T(8,128)}, f32[64,2048]{1,0:T(8,128)}, u32[]{:S(2)}, u32[]{:S(2)}) collective-permute-start(f32[64,2048]{1,0:T(8,128)} %get-tuple-element.109), channel_id=1, source_target_pairs={{0,1},{1,3},{2,5},{3,7},{4,9},{5,11},{6,13},{7,15},{8,17},{9,19},{... | collective-permute-start | bytes 1572872 | tf_op jit(solution)/shard_map/ppermute | solution.py:620
  786.5 6.5 copy-start.15
  786.5 6.5 copy-start.17
  786.5 6.5 copy-start.19
  786.5 6.5 copy-start.21
  793.1 8.3 slice-start
  794.4 6.9 slice-start.1
  888.9 70.2 %copy-start.11 = (bf16[128,2048]{1,0:T(8,128)(2,1)S(1)}, bf16[128,2048]{1,0:T(8,128)(2,1)}, u32[]{:S(2)}) copy-start(bf16[128,2048]{1,0:T(8,128)(2,1)} %param.16) | copy-start | bytes 1572868
  888.9 70.2 %copy-start.51 = (f32[2048,1]{0,1:T(1,128)S(1)}, f32[2048,1]{0,1:T(1,128)}, u32[]{:S(2)}) copy-start(f32[2048,1]{0,1:T(1,128)} %copy-done.50) | copy-start | bytes 24580
  888.9 70.2 %copy-start.71 = (f32[128]{0:T(128)S(1)}, f32[128]{0:T(128)}, u32[]{:S(2)}) copy-start(f32[128]{0:T(128)} %copy-done.70) | copy-start | bytes 1540
  888.9 70.6 %copy-start.36 = (f32[32,64,16]{1,0,2:T(8,128)S(1)}, f32[32,64,16]{1,0,2:T(8,128)}, u32[]{:S(2)}) copy-start(f32[32,64,16]{1,0,2:T(8,128)} %concatenate.60) | copy-start | bytes 393220
  959.1 28.6 %copy-start.78 = (f32[128]{0:T(128)S(1)}, f32[128]{0:T(128)}, u32[]{:S(2)}) copy-start(f32[128]{0:T(128)} %get-tuple-element.124) | copy-start | bytes 1540
  (36 other events, 127.8 us)
Sparse Core Ops, SparseCore 0:
  10.9 98.5 all-gather.4
  111.6 108.5 all-gather.6
  502.6 103.8 reduce-scatter.1

commit v2 on v1

--- a/solution.py
+++ b/solution.py
@@ -9,6 +9,7 @@
 from jax.sharding import PartitionSpec as P
 
 HEAD_DIM = 128
+HEADS = 16
 EPSILON = 1e-05
 THETA = 10000.0
 NEGATIVE = -1e30
@@ -50,177 +51,671 @@
     return table
 
 
+SCALE = HEAD_DIM ** (-0.5)
+
+
+SIB, ACROSS, UP, DOWN = range(4)
+
+
 def spot():
     me = lax.axis_index("expert")
     return me // 4, (me // 2) % 2, me % 2
 
+
 def at(z, x, c):
     return (z * 2 + x) * 2 + c
 
-def greet(z, x, c, far):
+
+def greet_all(group, n_dp):
+    me, dp = lax.axis_index("expert"), lax.axis_index("dp")
     barrier = pltpu.get_barrier_semaphore()
-    def hello(e):
-        pl.semaphore_signal(barrier, inc=1, device_id={"expert": e}, device_id_type=MESH)
-    hello(at(z, x, 1 - c)); hello(at(z, 1 - x, c))
-    @pl.when(z > 0)
-    def _(): hello(at(z - 1, x, c))
-    @pl.when(z < far)
-    def _(): hello(at(z + 1, x, c))
-    count = 2 + jnp.where(z > 0, 1, 0) + jnp.where(z < far, 1, 0)
-    pl.semaphore_wait(barrier, count)
-
-def gather_kernel(zs, in_ref, out_ref, send, recv, local):
+
+    def hello(k, carry):
+        pl.semaphore_signal(
+            barrier, inc=1, device_id={"expert": (me + k) % group}, device_id_type=MESH
+        )
+        return carry
+
+    lax.fori_loop(1, group, hello, 0)
+    if n_dp == 2:
+        pl.semaphore_signal(barrier, inc=1, device_id={"dp": 1 - dp}, device_id_type=MESH)
+    pl.semaphore_wait(barrier, group if n_dp == 2 else group - 1)
+
+
+def nearest(zs, z, i):
+    low = jnp.minimum(z, zs - 1 - z)
+    step = (i + 1) // 2
+    paired = jnp.where(i % 2 == 1, z - step, z + step)
+    alone = jnp.where(z > zs - 1 - z, z - (i - low), z + (i - low))
+    return jnp.where(i <= 2 * low, paired, alone)
+
+
+def gather_blocks(zs, buffers, process):
     z, x, c = spot()
     far = zs - 1
-    me = at(z, x, c)
-    greet(z, x, c, far)
-    mine = pltpu.make_async_copy(in_ref, out_ref.at[me], local)
-    mine.start()
-    def copy(src, block, kind, e):
-        return pltpu.make_async_remote_copy(
-            src_ref=src, dst_ref=out_ref.at[block], send_sem=send.at[kind, block],
-            recv_sem=recv.at[block], device_id={"expert": e}, device_id_type=MESH)
-    SIB, X, UP, DOWN = range(4)
-    def forward(src, block, zz):
+
+    def copies(block, kind, e):
+        return [
+            pltpu.make_async_remote_copy(
+                src_ref=all_ref.at[block],
+                dst_ref=all_ref.at[block],
+                send_sem=send.at[kind, block],
+                recv_sem=recv.at[block],
+                device_id={"expert": e},
+                device_id_type=MESH,
+            )
+            for all_ref, send, recv in buffers
+        ]
+
+    def to_sibling(block):
+        return copies(block, SIB, at(z, x, 1 - c))
+
+    def to_across(block):
+        return copies(block, ACROSS, at(z, 1 - x, c))
+
+    def to_up(block):
+        return copies(block, UP, at(z + 1, x, c))
+
+    def to_down(block):
+        return copies(block, DOWN, at(z - 1, x, c))
+
+    def step(i, carry):
+        @pl.when(i < zs)
+        def _():
+            zz = nearest(zs, z, i)
+            block = at(zz, x, c)
+            over = at(zz, 1 - x, c)
+            for n in range(len(buffers)):
+
+                @pl.when(i > 0)
+                def _():
+                    to_sibling(block)[n].wait_recv()
+
+                @pl.when((zz <= z) & (z < far))
+                def _():
+                    to_up(block)[n].start()
+
+                @pl.when((zz >= z) & (z > 0))
+                def _():
+                    to_down(block)[n].start()
+
+                to_across(block)[n].start()
+                to_sibling(block)[n].start()
+            for n in range(len(buffers)):
+                to_sibling(over)[n].wait_recv()
+                to_sibling(over)[n].start()
+
+        @pl.when(i > 0)
+        def _():
+            zz = nearest(zs, z, i - 1)
+            for xx in range(2):
+                for copy in to_sibling(at(zz, xx, 1 - c)):
+                    copy.wait_recv()
+            process(i - 1, zz)
+
+        return carry
+
+    lax.fori_loop(0, zs + 1, step, 0)
+
+    def done(zz, carry):
+        block = at(zz, x, c)
+        for copy in to_across(block) + to_sibling(block) + to_sibling(at(zz, 1 - x, c)):
+            copy.wait_send()
+
         @pl.when((zz <= z) & (z < far))
-        def _(): copy(src, block, UP, at(z + 1, x, c)).start()
+        def _():
+            for copy in to_up(block):
+                copy.wait_send()
+
         @pl.when((zz >= z) & (z > 0))
-        def _(): copy(src, block, DOWN, at(z - 1, x, c)).start()
-        copy(src, block, X, at(z, 1 - x, c)).start()
-        copy(src, block, SIB, at(z, x, 1 - c)).start()
-    def arrived(block):
-        copy(in_ref, block, SIB, at(z, x, 1 - c)).wait_recv()
-    forward(in_ref, me, z)
-    def across(zz):
-        block = at(zz, 1 - x, c)
-        arrived(block)
-        copy(out_ref.at[block], block, SIB, at(z, x, 1 - c)).start()
-    across(z)
-    for d in range(1, zs):
-        for zz, ok in ((z - d, z >= d), (z + d, z + d <= far)):
-            @pl.when(ok)
-            def _():
-                block = at(zz, x, c)
-                arrived(block)
-                forward(out_ref.at[block], block, zz)
-        for zz, ok in ((z - d, z >= d), (z + d, z + d <= far)):
-            @pl.when(ok)
-            def _(): across(zz)
-    for zz in range(zs):
-        for xx in range(2):
-            arrived(at(zz, xx, 1 - c))
-    mine.wait()
-    def sent(block, kind):
-        copy(in_ref, block, kind, at(z, x, 1 - c)).wait_send()
-    for zz in range(zs):
-        block = at(zz, x, c)
-        sent(block, X); sent(block, SIB); sent(at(zz, 1 - x, c), SIB)
-        @pl.when((zz <= z) & (z < far))
-        def _(): sent(block, UP)
-        @pl.when((zz >= z) & (z > 0))
-        def _(): sent(block, DOWN)
-
-def gather(values, group, cid):
-    return pl.pallas_call(
-        functools.partial(gather_kernel, group // 4),
-        out_shape=jax.ShapeDtypeStruct((group, *values.shape), values.dtype),
-        in_specs=[pl.BlockSpec(memory_space=pl.ANY)],
-        out_specs=pl.BlockSpec(memory_space=pl.ANY),
-        scratch_shapes=[pltpu.SemaphoreType.DMA((4, group)), pltpu.SemaphoreType.DMA((group,)), pltpu.SemaphoreType.DMA],
-        compiler_params=pltpu.CompilerParams(collective_id=cid, has_side_effects=True),
-    )(values)
-
-def scatter_kernel(zs, in_ref, out_ref, r_sib, r_x, r_z, s_x, s_z, send, recv):
+        def _():
+            for copy in to_down(block):
+                copy.wait_send()
+
+        return carry
+
+    lax.fori_loop(0, zs, done, 0)
+
+
+def joined(own_ref, full_ref, local, send, recv):
+    dp = lax.axis_index("dp")
+    half = own_ref.shape[0]
+    here = full_ref.at[pl.ds(dp * half, half)]
+    mine = pltpu.make_async_copy(own_ref, here, local)
+    theirs = over_dp(own_ref, here, send, recv)
+
+    def start():
+        mine.start()
+        theirs.start()
+
+    def finish():
+        mine.wait()
+        theirs.wait()
+
+    return start, finish
+
+
+def gather_sems(group):
+    return [pltpu.SemaphoreType.DMA((4, group)), pltpu.SemaphoreType.DMA((group,))]
+
+
+def scatter_blocks(zs, part_ref, out_ref, r_sib, r_x, r_z, s_x, s_z, send, recv, produce, pause=None):
     z, x, c = spot()
     far = zs - 1
-    greet(z, x, c, far)
-    SIB, X, UP, DOWN = range(4)
+
     def to_sibling(zz, xx):
         return pltpu.make_async_remote_copy(
-            src_ref=in_ref.at[at(zz, xx, 1 - c)], dst_ref=r_sib.at[zz * 2 + xx],
-            send_sem=send.at[SIB, zz * 2 + xx], recv_sem=recv.at[SIB, zz * 2 + xx],
-            device_id={"expert": at(z, x, 1 - c)}, device_id_type=MESH)
-    def to_x(zz):
+            src_ref=part_ref.at[at(zz, xx, 1 - c)],
+            dst_ref=r_sib.at[zz * 2 + xx],
+            send_sem=send.at[SIB, zz * 2 + xx],
+            recv_sem=recv.at[SIB, zz * 2 + xx],
+            device_id={"expert": at(z, x, 1 - c)},
+            device_id_type=MESH,
+        )
+
+    def to_across(zz):
         return pltpu.make_async_remote_copy(
-            src_ref=s_x.at[zz], dst_ref=r_x.at[zz], send_sem=send.at[X, zz], recv_sem=recv.at[X, zz],
-            device_id={"expert": at(z, 1 - x, c)}, device_id_type=MESH)
+            src_ref=s_x.at[zz],
+            dst_ref=r_x.at[zz],
+            send_sem=send.at[ACROSS, zz],
+            recv_sem=recv.at[ACROSS, zz],
+            device_id={"expert": at(z, 1 - x, c)},
+            device_id_type=MESH,
+        )
+
     def along(zz, kind, e):
         return pltpu.make_async_remote_copy(
-            src_ref=s_z.at[zz], dst_ref=r_z.at[kind - UP, zz], send_sem=send.at[kind, zz], recv_sem=recv.at[kind, zz],
-            device_id={"expert": e}, device_id_type=MESH)
-    def up(zz): return along(zz, UP, at(z + 1, x, c))
-    def down(zz): return along(zz, DOWN, at(z - 1, x, c))
-    def order(f):
+            src_ref=s_z.at[zz],
+            dst_ref=r_z.at[kind - UP, zz],
+            send_sem=send.at[kind, zz],
+            recv_sem=recv.at[kind, zz],
+            device_id={"expert": e},
+            device_id_type=MESH,
+        )
+
+    def up(zz):
+        return along(zz, UP, at(z + 1, x, c))
+
+    def down(zz):
+        return along(zz, DOWN, at(z - 1, x, c))
+
+    def order(do):
         for d in range(far, 0, -1):
+
             @pl.when(z + d <= far)
-            def _(): f(z + d)
+            def _():
+                do(z + d)
+
             @pl.when(z >= d)
-            def _(): f(z - d)
-        f(z)
-    order(lambda zz: to_sibling(zz, 1 - x).start())
-    order(lambda zz: to_sibling(zz, x).start())
+            def _():
+                do(z - d)
+
+        do(z)
+
     def cross(zz):
+        produce(at(zz, 1 - x, 1 - c))
+        to_sibling(zz, 1 - x).start()
+        produce(at(zz, 1 - x, c))
         to_sibling(zz, 1 - x).wait_recv()
-        s_x[zz] = (in_ref[at(zz, 1 - x, c)].astype(F32) + r_sib[zz * 2 + 1 - x].astype(F32)).astype(BF16)
-        to_x(zz).start()
+        mine = part_ref[at(zz, 1 - x, c)].astype(F32)
+        s_x[zz] = (mine + r_sib[zz * 2 + 1 - x].astype(F32)).astype(BF16)
+        to_across(zz).start()
+
     order(cross)
+
+    def near(zz):
+        produce(at(zz, x, 1 - c))
+        to_sibling(zz, x).start()
+        produce(at(zz, x, c))
+
+    order(near)
+    if pause is not None:
+        pause()
+
     def finish(zz):
         to_sibling(zz, x).wait_recv()
-        to_x(zz).wait_recv()
+        to_across(zz).wait_recv()
+
         def here():
-            return in_ref[at(zz, x, c)].astype(F32) + r_sib[zz * 2 + x].astype(F32) + r_x[zz].astype(F32)
+            mine = part_ref[at(zz, x, c)].astype(F32)
+            return mine + r_sib[zz * 2 + x].astype(F32) + r_x[zz].astype(F32)
+
         @pl.when(zz > z)
         def _():
             @pl.when(z > 0)
             def _():
                 up(zz).wait_recv()
                 s_z[zz] = (here() + r_z[0, zz].astype(F32)).astype(BF16)
+
             @pl.when(z == 0)
-            def _(): s_z[zz] = here().astype(BF16)
+            def _():
+                s_z[zz] = here().astype(BF16)
+
             up(zz).start()
+
         @pl.when(zz < z)
         def _():
             @pl.when(z < far)
             def _():
                 down(zz).wait_recv()
                 s_z[zz] = (here() + r_z[1, zz].astype(F32)).astype(BF16)
+
             @pl.when(z == far)
-            def _(): s_z[zz] = here().astype(BF16)
+            def _():
+                s_z[zz] = here().astype(BF16)
+
             down(zz).start()
+
         @pl.when(zz == z)
         def _():
             out_ref[...] = here()
+
             @pl.when(z > 0)
             def _():
                 up(zz).wait_recv()
                 out_ref[...] += r_z[0, zz].astype(F32)
+
             @pl.when(z < far)
             def _():
                 down(zz).wait_recv()
                 out_ref[...] += r_z[1, zz].astype(F32)
+
     order(finish)
-    for zz in range(zs):
-        for xx in range(2):
-            to_sibling(zz, xx).wait_send()
-        to_x(zz).wait_send()
+
+    def done(zz, carry):
+        to_sibling(zz, 0).wait_send()
+        to_sibling(zz, 1).wait_send()
+        to_across(zz).wait_send()
+
         @pl.when(zz > z)
-        def _(): up(zz).wait_send()
+        def _():
+            up(zz).wait_send()
+
         @pl.when(zz < z)
-        def _(): down(zz).wait_send()
-
-def scatter(values, cid):
-    group, rows, width = values.shape
+        def _():
+            down(zz).wait_send()
+
+        return carry
+
+    lax.fori_loop(0, zs, done, 0)
+
+
+def scatter_scratch(group, rows, width):
     zs = group // 4
-    buf = lambda *n: pltpu.VMEM((*n, rows, width), BF16)
+
+    def buffer(*n):
+        return pltpu.VMEM((*n, rows, width), BF16)
+
+    return [
+        buffer(2 * zs),
+        buffer(zs),
+        buffer(2, zs),
+        buffer(zs),
+        buffer(zs),
+        pltpu.SemaphoreType.DMA((4, 2 * zs)),
+        pltpu.SemaphoreType.DMA((4, 2 * zs)),
+    ]
+
+
+def over_dp(src, dst, send, recv):
+    return pltpu.make_async_remote_copy(
+        src_ref=src,
+        dst_ref=dst,
+        send_sem=send,
+        recv_sem=recv,
+        device_id={"dp": 1 - lax.axis_index("dp")},
+        device_id_type=MESH,
+    )
+
+
+def tree_swap(group, make, send, recv):
+    me = lax.axis_index("expert")
+
+    def copy(k, back):
+        d = (me + k) % group
+        src, _ = make(d, me)
+        _, dst = make(d, d if back else me)
+        return pltpu.make_async_remote_copy(
+            src_ref=src,
+            dst_ref=dst,
+            send_sem=send.at[k],
+            recv_sem=recv.at[d if back else me],
+            device_id={"expert": d},
+            device_id_type=MESH,
+        )
+
+    def start():
+        def one(k, carry):
+            copy(k, False).start()
+            return carry
+
+        lax.fori_loop(1, group, one, 0)
+
+    def finish_recv():
+        def one(k, carry):
+            copy(k, True).wait_recv()
+            return carry
+
+        lax.fori_loop(1, group, one, 0)
+
+    def finish_send():
+        def one(k, carry):
+            copy(k, False).wait_send()
+            return carry
+
+        lax.fori_loop(1, group, one, 0)
+
+    return start, finish_recv, finish_send
+
+
+VMEM = pl.BlockSpec(memory_space=pltpu.VMEM)
+HBM = pl.BlockSpec(memory_space=pl.ANY)
+DMA = pltpu.SemaphoreType.DMA
+
+
+def params(cid):
+    return pltpu.CompilerParams(
+        collective_id=cid, has_side_effects=True, vmem_limit_bytes=56 * 2**20
+    )
+
+
+def project_kernel(
+    group, n_dp, shard,
+    x_ref, w_ref, pay_ref,
+    normed_ref, pre_ref, w_all, gains_ref, pay_out,
+    x_all, send, recv, local, w_send, w_recv, dp_send, dp_recv,
+):
+    me, dp = lax.axis_index("expert"), lax.axis_index("dp")
+    mine = pltpu.make_async_copy(x_ref, x_all.at[me], local.at[0])
+    mine.start()
+    half = group * shard
+
+    def rows_of(d, e):
+        return w_all.at[pl.ds(d * half + e * shard, shard)]
+
+    own = pltpu.make_async_copy(w_ref.at[me], rows_of(dp, me), local.at[1])
+    own.start()
+    greet_all(group, n_dp)
+    start, finish_recv, finish_send = tree_swap(
+        group, lambda d, src: (w_ref.at[d], rows_of(dp, src)), w_send, w_recv
+    )
+    start()
+    mine.wait()
+    own.wait()
+
+    def bundle(d):
+        piece = w_all.at[pl.ds(d * half, half)]
+        return over_dp(piece, piece, dp_send.at[0], dp_recv.at[0])
+
+    pay_start, pay_finish = joined(pay_ref, pay_out, local.at[2], dp_send.at[1], dp_recv.at[1])
+
+    def compute(block):
+        rows = x_ref.shape[0]
+        values = x_all[block].astype(F32)
+        scale = lax.rsqrt(jnp.mean(values * values, axis=-1, keepdims=True) + EPSILON)
+        normed = (values * scale * gains_ref[0:1, :]).astype(BF16)
+        normed_ref[block] = normed
+        pre_ref[pl.ds(block * rows, rows), :] = mm(normed, w_all[:, : 3 * HEAD_DIM])
+
+    def weights_here():
+        finish_recv()
+        bundle(dp).start()
+        pay_start()
+
+    def weights_done():
+        bundle(1 - dp).wait_recv()
+        pick = lax.broadcasted_iota(jnp.int32, (8, HEAD_DIM), 0)
+        lane = lax.broadcasted_iota(jnp.int32, (8, HEAD_DIM), 1)
+        pick = jnp.where(pick == lane, 1.0, 0.0).astype(BF16)
+        gains_ref[...] = mm_t(pick, w_all[:, 3 * HEAD_DIM :])
+
+    def process(i, zz):
+        @pl.when(i == 0)
+        def _():
+            weights_here()
+            weights_done()
+
+        def one(j, carry):
+            compute(zz * 4 + j)
+            return carry
+
+        lax.fori_loop(0, 4, one, 0)
+
+    gather_blocks(group // 4, [(x_all, send, recv)], process)
+    finish_send()
+    bundle(dp).wait_send()
+    pay_finish()
+
+
+def project(tokens, w_cut, payload, n_dp, cid):
+    group, shard = w_cut.shape[0], w_cut.shape[1]
+    rows, width = tokens.shape
+    wide = w_cut.shape[2]
     return pl.pallas_call(
-        functools.partial(scatter_kernel, zs),
-        out_shape=jax.ShapeDtypeStruct((rows, width), F32),
-        in_specs=[pl.BlockSpec(memory_space=pltpu.VMEM)],
-        out_specs=pl.BlockSpec(memory_space=pltpu.VMEM),
-        scratch_shapes=[buf(2 * zs), buf(zs), buf(2, zs), buf(zs), buf(zs),
-            pltpu.SemaphoreType.DMA((4, 2 * zs)), pltpu.SemaphoreType.DMA((4, 2 * zs))],
-        compiler_params=pltpu.CompilerParams(collective_id=cid, has_side_effects=True, vmem_limit_bytes=48 * 2**20),
-    )(values)
+        functools.partial(project_kernel, group, n_dp, shard),
+        out_shape=[
+            jax.ShapeDtypeStruct((group, rows, width), BF16),
+            jax.ShapeDtypeStruct((group * rows, 3 * HEAD_DIM), F32),
+            jax.ShapeDtypeStruct((n_dp * group * shard, wide), BF16),
+            jax.ShapeDtypeStruct((8, width), F32),
+            jax.ShapeDtypeStruct((n_dp * payload.shape[0], payload.shape[1]), payload.dtype),
+        ],
+        in_specs=[HBM, VMEM, HBM],
+        out_specs=[VMEM, VMEM, VMEM, VMEM, HBM],
+        scratch_shapes=[
+            pltpu.VMEM((group, rows, width), BF16),
+            *gather_sems(group),
+            DMA((3,)),
+            DMA((group,)),
+            DMA((group,)),
+            DMA((2,)),
+            DMA((2,)),
+        ],
+        compiler_params=params(cid),
+    )(tokens, w_cut, payload)
+
+
+def attend_kernel(
+    group, n_dp,
+    q_ref, k_ref, v_ref, bias_ref, w_ref, pay_ref,
+    attn_ref, lse_ref, sum_ref, pay_out,
+    part, r_sib, r_x, r_z, s_x, s_z, send, recv, local, dp_send, dp_recv,
+):
+    rows = sum_ref.shape[0]
+    count = k_ref.shape[0]
+    greet_all(group, n_dp)
+    pay_start, pay_finish = joined(pay_ref, pay_out, local, dp_send, dp_recv)
+    pay_start()
+
+    def produce(block):
+        first = block * rows
+        scores = mm_t(q_ref[pl.ds(first, rows), :], k_ref[...]) * SCALE
+        scores = scores + bias_ref[pl.ds(block, 1), :]
+        key = lax.broadcasted_iota(jnp.int32, (rows, count), 1)
+        query = first + lax.broadcasted_iota(jnp.int32, (rows, count), 0)
+        scores = jnp.where(key <= query, scores, NEGATIVE)
+        row_max = jnp.max(scores, axis=-1, keepdims=True)
+        weights = jnp.exp(scores - row_max)
+        total = jnp.sum(weights, axis=-1, keepdims=True)
+        attn = mm(weights.astype(BF16), v_ref[...]) / total
+        attn_ref[pl.ds(first, rows), :] = attn
+        lse_ref[pl.ds(first, rows), :] = jnp.broadcast_to(row_max + jnp.log(total), (rows, HEAD_DIM))
+        part[block] = mm(attn.astype(BF16), w_ref[...]).astype(BF16)
+
+    scatter_blocks(group // 4, part, sum_ref, r_sib, r_x, r_z, s_x, s_z, send, recv, produce)
+    pay_finish()
+
+
+def attend(queries, keys, values, bias, w_rows, payload, n_dp, cid):
+    group = bias.shape[0]
+    count, width = queries.shape[0], w_rows.shape[1]
+    rows = count // group
+    return pl.pallas_call(
+        functools.partial(attend_kernel, group, n_dp),
+        out_shape=[
+            jax.ShapeDtypeStruct((count, HEAD_DIM), F32),
+            jax.ShapeDtypeStruct((count, HEAD_DIM), F32),
+            jax.ShapeDtypeStruct((rows, width), F32),
+            jax.ShapeDtypeStruct((n_dp * payload.shape[0], payload.shape[1]), payload.dtype),
+        ],
+        in_specs=[VMEM] * 5 + [HBM],
+        out_specs=[VMEM, VMEM, VMEM, HBM],
+        scratch_shapes=[
+            pltpu.VMEM((group, rows, width), BF16),
+            *scatter_scratch(group, rows, width),
+            DMA,
+            DMA,
+            DMA,
+        ],
+        compiler_params=params(cid),
+    )(queries, keys, values, bias, w_rows, payload)
+
+
+def attend_back_kernel(
+    group, n_dp,
+    g_ref, q_ref, k_ref, v_ref, bias_ref, w_ref, attn_ref, lse_ref,
+    dq_ref, dk_ref, dv_ref, dw_ref,
+    g_all, send, recv, local,
+):
+    me = lax.axis_index("expert")
+    rows = g_ref.shape[0]
+    count = k_ref.shape[0]
+    chunk = min(count, 512)
+    mine = pltpu.make_async_copy(g_ref, g_all.at[me], local)
+    mine.start()
+    greet_all(group, n_dp)
+    mine.wait()
+    dk_ref[...] = jnp.zeros_like(dk_ref)
+    dv_ref[...] = jnp.zeros_like(dv_ref)
+    dw_ref[...] = jnp.zeros_like(dw_ref)
+
+    def process(block):
+        first = block * rows
+        here = pl.ds(first, rows)
+        grad = g_all[block]
+        attn = attn_ref[here, :]
+        mixed_grad = mm_t(grad, w_ref[...]).astype(BF16)
+        dw_ref[...] += t_mm(attn.astype(BF16), grad)
+        delta = jnp.sum(mixed_grad.astype(F32) * attn, axis=-1, keepdims=True)
+        queries = q_ref[here, :]
+        lse = lse_ref[here, :][:, :1]
+        query = first + lax.broadcasted_iota(jnp.int32, (rows, chunk), 0)
+
+        def turn_keys(j, dq):
+            cut = pl.ds(j * chunk, chunk)
+            keys = k_ref[cut, :]
+            scores = mm_t(queries, keys) * SCALE + bias_ref[pl.ds(block, 1), cut]
+            key = j * chunk + lax.broadcasted_iota(jnp.int32, (rows, chunk), 1)
+            probs = jnp.exp(jnp.where(key <= query, scores - lse, NEGATIVE))
+            score_grad = probs * (mm_t(mixed_grad, v_ref[cut, :]) - delta)
+            score_grad = score_grad.astype(BF16)
+            dk_ref[cut, :] += t_mm(score_grad, queries)
+            dv_ref[cut, :] += t_mm(probs.astype(BF16), mixed_grad)
+            return dq + mm(score_grad, keys)
+
+        turns = (first + rows + chunk - 1) // chunk
+        dq = lax.fori_loop(0, turns, turn_keys, jnp.zeros((rows, HEAD_DIM), F32))
+        dq_ref[here, :] = dq
+
+    def four(i, zz):
+        def one(j, carry):
+            process(zz * 4 + j)
+            return carry
+
+        lax.fori_loop(0, 4, one, 0)
+
+    gather_blocks(group // 4, [(g_all, send, recv)], four)
+
+
+def attend_back(grad, queries, keys, values, bias, w_rows, attn, lse, n_dp, cid):
+    group = bias.shape[0]
+    rows, width = grad.shape
+    count = queries.shape[0]
+    long = jax.ShapeDtypeStruct((count, HEAD_DIM), F32)
+    return pl.pallas_call(
+        functools.partial(attend_back_kernel, group, n_dp),
+        out_shape=[long, long, long, jax.ShapeDtypeStruct((HEAD_DIM, width), F32)],
+        in_specs=[HBM] + [VMEM] * 7,
+        out_specs=[VMEM] * 4,
+        scratch_shapes=[pltpu.VMEM((group, rows, width), BF16), *gather_sems(group), DMA],
+        compiler_params=params(cid),
+    )(grad, queries, keys, values, bias, w_rows, attn, lse)
+
+
+def unproject_kernel(
+    group, n_dp, shard,
+    low_ref, w_ref, normed_ref,
+    sum_ref, got_ref,
+    part, r_sib, r_x, r_z, s_x, s_z, send, recv,
+    mine, theirs, w_send, w_recv, dp_send, dp_recv,
+):
+    me, dp = lax.axis_index("expert"), lax.axis_index("dp")
+    rows = sum_ref.shape[0]
+    half = group * shard
+    greet_all(group, n_dp)
+    step = min(half, 256)
+
+    def slice_grad(d, ref):
+        def one(i, carry):
+            cols = pl.ds(pl.multiple_of(d * half + i * step, step), step)
+            total = jnp.zeros((step, low_ref.shape[1]), F32)
+            grad = t_mm(normed_ref[:, cols], low_ref[...])
+            ref[pl.ds(i * step, step), :] = (total + grad).astype(ref.dtype)
+            return carry
+
+        lax.fori_loop(0, half // step, one, 0)
+
+    to_dp = over_dp(theirs.at[0], theirs.at[1], dp_send, dp_recv)
+
+    def produce(block):
+        low = low_ref[pl.ds(block * rows, rows), :]
+        part[block] = mm_t(low, w_ref[:, : 3 * HEAD_DIM]).astype(BF16)
+
+    def make(d, src):
+        return mine.at[pl.ds(d * shard, shard)], got_ref.at[src]
+
+    start, finish_recv, finish_send = tree_swap(group, make, w_send, w_recv)
+
+    def pause():
+        slice_grad(1 - dp, theirs.at[0])
+        to_dp.start()
+        slice_grad(dp, mine)
+        to_dp.wait_recv()
+        mine[...] = (mine[...].astype(F32) + theirs[1].astype(F32)).astype(BF16)
+        start()
+        got_ref[me] = mine[pl.ds(me * shard, shard), :]
+
+    scatter_blocks(group // 4, part, sum_ref, r_sib, r_x, r_z, s_x, s_z, send, recv, produce, pause)
+    finish_recv()
+    finish_send()
+    to_dp.wait_send()
+
+
+def unproject(low, w_all, normed, rows, shard, n_dp, cid):
+    count, wide = low.shape
+    width = w_all.shape[0]
+    group = count // rows
+    return pl.pallas_call(
+        functools.partial(unproject_kernel, group, n_dp, shard),
+        out_shape=[
+            jax.ShapeDtypeStruct((rows, width), F32),
+            jax.ShapeDtypeStruct((group, shard, wide), BF16),
+        ],
+        in_specs=[VMEM] * 3,
+        out_specs=[VMEM] * 2,
+        scratch_shapes=[
+            pltpu.VMEM((group, rows, width), BF16),
+            *scatter_scratch(group, rows, width),
+            pltpu.VMEM((group * shard, wide), BF16),
+            pltpu.VMEM((2, group * shard, wide), BF16),
+            DMA((group,)),
+            DMA((group,)),
+            DMA,
+            DMA,
+        ],
+        compiler_params=params(cid),
+    )(low, w_all, normed)
+
 
 def swap_kernel(axes, sizes, in_ref, out_ref, send, recv, local):
     count = 1
@@ -306,7 +801,185 @@
     )(values)
 
 
-SCALE = HEAD_DIM ** (-0.5)
+def expert_kernel(
+    group, n_dp, cap,
+    x_ref, cot_ref, gate_ref, gate_w, up_w, down_ref,
+    rows_out, grads_out, hidden_out, gate_out, up_out, sent_out, row_out, gate_grads,
+    x_all, c_all, down_w, gates, stage,
+    x_send, x_recv, c_send, c_recv, g_send, g_recv, local, dp_send, dp_recv,
+):
+    me = lax.axis_index("expert")
+    rows, width = x_ref.shape
+    pair = 2 * cap
+    own = [
+        pltpu.make_async_copy(x_ref, x_all.at[me], local.at[0]),
+        pltpu.make_async_copy(cot_ref, c_all.at[me], local.at[1]),
+    ]
+    for copy in own:
+        copy.start()
+    greet_all(group, n_dp)
+    start, finish_recv, finish_send = tree_swap(
+        group, lambda d, src: (gate_ref.at[d], gates.at[src]), g_send, g_recv
+    )
+    start()
+    down_start, down_finish = joined(down_ref, down_w, local.at[2], dp_send, dp_recv)
+    down_start()
+    gates[me] = gate_ref[me]
+    for copy in own:
+        copy.wait()
+
+    def put(kind, p):
+        ref = (sent_out, row_out)[kind]
+        return pltpu.make_async_copy(
+            stage.at[kind], ref.at[pl.ds(p * 2 * rows, 2 * rows)], local.at[3 + kind]
+        )
+
+    lane = lax.broadcasted_iota(jnp.int32, (rows, rows), 1)
+    row = lax.broadcasted_iota(jnp.int32, (rows, rows), 0)
+    before = jnp.where(row < lane, 1.0, 0.0).astype(BF16)
+    slot = lax.broadcasted_iota(jnp.int32, (cap, rows), 0).astype(F32)
+
+    def run(p):
+        base = p * pair
+        picks, gate_cols = [], []
+        for i in range(2):
+            segment = p * 2 + i
+            gate_row = gates[segment]
+            routed = jnp.where(gate_row > 0.0, 1.0, 0.0)
+            rank = mm(jnp.broadcast_to(routed, (16, rows)).astype(BF16), before)[0:1, :]
+            pick = jnp.where((slot == rank) & (routed > 0.5), 1.0, 0.0)
+            gate_cols.append(jnp.sum(pick * gate_row, axis=1, keepdims=True))
+            pick_low = pick.astype(BF16)
+            picks.append((pick, pick_low))
+            here = pl.ds(base + i * cap, cap)
+            rows_out[here, :] = mm(pick_low, x_all[segment]).astype(BF16)
+            grads_out[here, :] = mm(pick_low, c_all[segment]).astype(BF16)
+        here = pl.ds(base, pair)
+        gate_col = jnp.concatenate(gate_cols)
+        taken = rows_out[here, :]
+        gate_pre = mm(taken, gate_w[...])
+        up_pre = mm(taken, up_w[...])
+        sig = 1.0 / (1.0 + jnp.exp(-gate_pre))
+        silu = gate_pre * sig
+        hidden = (silu * up_pre).astype(BF16)
+        hidden_out[here, :] = hidden
+        result = mm(hidden, down_w[...]).astype(BF16).astype(F32)
+        cot = grads_out[here, :].astype(F32)
+        dots = jnp.sum(cot * result, axis=1, keepdims=True)
+        sent = (gate_col * result).astype(BF16)
+        grads_out[here, :] = (gate_col * cot).astype(BF16)
+        for i, (pick, pick_low) in enumerate(picks):
+            part = slice(i * cap, (i + 1) * cap)
+            gate_grads[p * 2 + i] = jnp.sum(pick * dots[part], axis=0, keepdims=True)
+            stage[0, i * rows : (i + 1) * rows, :] = t_mm(pick_low, sent[part]).astype(BF16)
+        put(0, p).start()
+        hidden_grad = mm_t(grads_out[here, :], down_w[...]).astype(BF16).astype(F32)
+        slope = sig * (1.0 + gate_pre * (1.0 - sig))
+        gate_pre_grad = (hidden_grad * up_pre * slope).astype(BF16)
+        up_pre_grad = (hidden_grad * silu).astype(BF16)
+        gate_out[here, :] = gate_pre_grad
+        up_out[here, :] = up_pre_grad
+        row_grad = (mm_t(gate_pre_grad, gate_w[...]) + mm_t(up_pre_grad, up_w[...])).astype(BF16)
+        for i, (_, pick_low) in enumerate(picks):
+            part = slice(i * cap, (i + 1) * cap)
+            stage[1, i * rows : (i + 1) * rows, :] = t_mm(pick_low, row_grad[part]).astype(BF16)
+        put(1, p).start()
+        put(0, p).wait()
+        put(1, p).wait()
+
+    def process(i, zz):
+        @pl.when(i == 0)
+        def _():
+            finish_recv()
+            down_finish()
+
+        def one(j, carry):
+            run(zz * 2 + j)
+            return carry
+
+        lax.fori_loop(0, 2, one, 0)
+
+    gather_blocks(group // 4, [(x_all, x_send, x_recv), (c_all, c_send, c_recv)], process)
+    finish_send()
+
+
+def expert(x, cot, gates, gate_w, up_w, down_w, n_dp, cap, cid):
+    group = gates.shape[0]
+    rows, width = x.shape
+    hidden = gate_w.shape[1]
+    total = group * cap
+
+    def shape(*dims, dtype=BF16):
+        return jax.ShapeDtypeStruct(dims, dtype)
+
+    def buffer(*dims):
+        return pltpu.VMEM(dims, BF16)
+
+    return pl.pallas_call(
+        functools.partial(expert_kernel, group, n_dp, cap),
+        out_shape=[
+            shape(total, width),
+            shape(total, width),
+            shape(total, hidden),
+            shape(total, hidden),
+            shape(total, hidden),
+            shape(group * rows, width),
+            shape(group * rows, width),
+            shape(*gates.shape, dtype=F32),
+        ],
+        in_specs=[HBM, HBM, VMEM, VMEM, VMEM, HBM],
+        out_specs=[VMEM] * 5 + [HBM, HBM, VMEM],
+        scratch_shapes=[
+            buffer(group, rows, width),
+            buffer(group, rows, width),
+            buffer(n_dp * down_w.shape[0], width),
+            pltpu.VMEM(gates.shape, F32),
+            buffer(2, 2 * rows, width),
+            *gather_sems(group),
+            *gather_sems(group),
+            DMA((group,)),
+            DMA((group,)),
+            DMA((5,)),
+            DMA,
+            DMA,
+        ],
+        compiler_params=pltpu.CompilerParams(
+            collective_id=cid, has_side_effects=True, vmem_limit_bytes=63 * 2**20
+        ),
+    )(x, cot, gates, gate_w, up_w, down_w)
+
+
+def collect_kernel(
+    group, n_dp, part, gate_ref, sum_ref, gates_ref,
+    r_sib, r_x, r_z, s_x, s_z, send, recv, g_send, g_recv,
+):
+    me = lax.axis_index("expert")
+    greet_all(group, n_dp)
+    start, finish_recv, finish_send = tree_swap(
+        group, lambda d, src: (gate_ref.at[d], gates_ref.at[src]), g_send, g_recv
+    )
+    start()
+    gates_ref[me] = gate_ref[me]
+    scatter_blocks(
+        group // 4, part, sum_ref, r_sib, r_x, r_z, s_x, s_z, send, recv, lambda block: None
+    )
+    finish_recv()
+    finish_send()
+
+
+def collect(parts, gates, n_dp, cid):
+    group, rows, width = parts.shape
+    return pl.pallas_call(
+        functools.partial(collect_kernel, group, n_dp),
+        out_shape=[
+            jax.ShapeDtypeStruct((rows, width), F32),
+            jax.ShapeDtypeStruct(gates.shape, gates.dtype),
+        ],
+        in_specs=[VMEM, VMEM],
+        out_specs=[VMEM, VMEM],
+        scratch_shapes=[*scatter_scratch(group, rows, width), DMA((group,)), DMA((group,))],
+        compiler_params=params(cid),
+    )(parts, gates)
 
 
 def attention(queries, mask, keys, values):
@@ -387,30 +1060,20 @@
     def own_part(values):
         return lax.dynamic_slice_in_dim(values, first_seg * rows, own_rows, 0)
 
-    def head_sum(values, cid):
-        if share > 1:
-            return lax.psum(values, "expert", axis_index_groups=peers)
-        return jnp.sum(swap(values[None], ("expert",), cid), axis=0)
-
-    def tree_gather(values, cid):
-        if share > 1:
-            return lax.all_gather(values, "expert", axis=0, tiled=True)
-        return gather(values, group, cid).reshape(tree_rows, -1)
-
-    def tree_scatter(values, cid):
-        if share > 1:
-            return lax.psum_scatter(values, "expert", scatter_dimension=0, tiled=True).astype(F32)
-        return scatter(values.reshape(group, rows, -1), cid)
-
-    def both_swap(values, cid):
-        if share > 1:
-            return lax.all_to_all(values, BOTH, 0, 0, tiled=True)
-        return swap(values, BOTH, cid)
-
-    def expert_swap(values, cid):
-        if share > 1:
-            return lax.all_to_all(values, "expert", 0, 0, tiled=True)
-        return swap(values, ("expert",), cid)
+    def head_sum(values):
+        return lax.psum(values, "expert", axis_index_groups=peers if share > 1 else None)
+
+    def tree_gather(values):
+        return lax.all_gather(values, "expert", axis=0, tiled=True)
+
+    def tree_scatter(values):
+        return lax.psum_scatter(values, "expert", scatter_dimension=0, tiled=True).astype(F32)
+
+    def both_swap(values):
+        return lax.all_to_all(values, BOTH, 0, 0, tiled=True)
+
+    def expert_swap(values):
+        return lax.all_to_all(values, "expert", 0, 0, tiled=True)
 
     others = [(d, (d + 1) % n_dp) for d in range(n_dp)]
 
@@ -439,7 +1102,7 @@
     by_head = jnp.stack([w_query, w_key, w_value], axis=1).reshape(shard, 3, heads, HEAD_DIM)
     by_head = by_head.transpose(2, 0, 1, 3).reshape(1, heads, 1, shard, 3 * HEAD_DIM)
     by_head = jnp.broadcast_to(by_head, (n_dp, heads, share, shard, 3 * HEAD_DIM))
-    w_head = both_swap(by_head.reshape(devices, shard, 3 * HEAD_DIM), 0).reshape(
+    w_head = both_swap(by_head.reshape(devices, shard, 3 * HEAD_DIM)).reshape(
         width, 3 * HEAD_DIM
     )
     out_w = lax.all_gather(w_out, BOTH, axis=0, tiled=True)
@@ -452,12 +1115,12 @@
     token_f = tokens.astype(F32)
     first_scale = inverse_rms(token_f)
     normed = (token_f * first_scale * attn_g[None, :]).astype(BF16)
-    normed_all = own_part(tree_gather(normed, 1))
+    normed_all = own_part(tree_gather(normed))
     pre = mm(normed_all, w_head)
     query_pre, key_pre = pre[:, :HEAD_DIM], pre[:, HEAD_DIM : 2 * HEAD_DIM]
     values = pre[:, 2 * HEAD_DIM :].astype(BF16)
     squares = jnp.stack([jnp.sum(query_pre**2, axis=-1), jnp.sum(key_pre**2, axis=-1)])
-    scales = lax.rsqrt(head_sum(squares, 2) / width + EPSILON)
+    scales = lax.rsqrt(head_sum(squares) / width + EPSILON)
     query_scale, key_scale = scales[0][:, None], scales[1][:, None]
     queries = turn(query_pre * query_scale * my_query_g, cosine, sine).astype(BF16)
     keys = turn(key_pre * key_scale * my_key_g, cosine, sine).astype(BF16)
@@ -487,7 +1150,7 @@
             cut = lax.dynamic_update_slice_in_dim(
                 jnp.zeros((group, *cut.shape[1:]), cut.dtype), cut, first_seg, 0
             )
-        got = expert_swap(cut, 3)
+        got = expert_swap(cut)
         if share > 1:
             got = jnp.sum(got.reshape(heads, share, rows, -1), axis=1, dtype=cut.dtype)
         return got
@@ -502,9 +1165,9 @@
     labels = jnp.arange(experts, dtype=jnp.int32)
     routed = jnp.any(routes[:, :, None] == labels[None, None, :], axis=1)
     gates_own = jnp.where(routed, router_probs, 0.0)
-    gates = expert_swap(gates_own.T[:, None], 4).reshape(tree_rows, 1)
-
-    rows_in = tree_gather(normed_two, 5)
+    gates = expert_swap(gates_own.T[:, None]).reshape(tree_rows, 1)
+
+    rows_in = tree_gather(normed_two)
     cot_in = lax.all_gather(cotangent, "expert", axis=0, tiled=True)
     pieces = max(1, tree_rows // 2048)
     if pieces == 1:
@@ -526,8 +1189,8 @@
     gate_w_grad, up_w_grad, down_w_grad = (s.astype(BF16) for s in sums)
     combined = lax.psum_scatter(sent_out, "expert", scatter_dimension=0, tiled=True)
     output = (residual + combined.astype(F32)).astype(BF16)
-    gate_grad_own = expert_swap(gate_grad.reshape(group, 1, rows), 6).reshape(group, rows).T
-    expert_grad = tree_scatter(row_grad, 7)
+    gate_grad_own = expert_swap(gate_grad.reshape(group, 1, rows)).reshape(group, rows).T
+    expert_grad = tree_scatter(row_grad)
     grad_gate, grad_up, grad_down = (
         dp_sum(g).astype(F32)[None]
         for g in (gate_w_grad, up_w_grad, down_w_grad)
@@ -548,7 +1211,7 @@
     )
     proj_grad = residual_grad.astype(BF16)
 
-    proj_all = own_part(tree_gather(proj_grad, 8))
+    proj_all = own_part(tree_gather(proj_grad))
     mixed_grad = mm_t(proj_all, out_head).astype(BF16)
     out_w_grad = t_mm(mixed_head, proj_all)
     row_delta = jnp.sum(mixed_grad.astype(F32) * attn, axis=-1, keepdims=True)
@@ -581,7 +1244,7 @@
             jnp.sum(key_turned * my_key_g * key_pre, axis=-1),
         ]
     )
-    means = head_sum(dots, 9) / width
+    means = head_sum(dots) / width
     query_low = query_scale * my_query_g * query_turned - query_pre * query_scale**3 * means[0][:, None]
     key_low = key_scale * my_key_g * key_turned - key_pre * key_scale**3 * means[1][:, None]
     low = jnp.concatenate([query_low, key_low, value_grad], axis=1).astype(BF16)
@@ -592,7 +1255,7 @@
         normed_part = lax.dynamic_update_slice_in_dim(
             jnp.zeros((tree_rows, width), BF16), normed_part, first_seg * rows, 0
         )
-    normed_grad = tree_scatter(normed_part, 10)
+    normed_grad = tree_scatter(normed_part)
     attn_gain_grad = jnp.sum(normed_grad * token_f * first_scale, axis=0)
     weighted = normed_grad * attn_g[None, :]
     token_grad = (
@@ -602,7 +1265,7 @@
     )
 
     head_grad = t_mm(normed_all, low)
-    got = both_swap(head_grad.reshape(devices, shard, 3 * HEAD_DIM), 11).reshape(n_dp, heads, share, shard, 3, HEAD_DIM)
+    got = both_swap(head_grad.reshape(devices, shard, 3 * HEAD_DIM)).reshape(n_dp, heads, share, shard, 3, HEAD_DIM)
     got = jnp.sum(got, axis=(0, 2)).transpose(2, 1, 0, 3).reshape(3, shard, width)
     shards_a_head = HEAD_DIM // shard
     source = dp * share + part
@@ -625,7 +1288,7 @@
     small = jnp.concatenate(
         [router_grad, attn_gain_grad[:, None], head_gains, ffn_gain_grad[:, None]], axis=1
     )
-    small = jnp.sum(both_swap(small.reshape(devices, shard, -1), 12), axis=0)
+    small = jnp.sum(both_swap(small.reshape(devices, shard, -1)), axis=0)
     return (
         output,
         token_grad,
@@ -644,11 +1307,194 @@
     )
 
 
+def per_head(
+    tokens, attn_gain, q_gain, k_gain, ffn_gain, w_query, w_key, w_value, w_out, router,
+    w_gate, w_up, w_down, cotangent, routes, parents,
+):
+    rows, width = tokens.shape
+    group = lax.axis_size("expert")
+    n_dp = lax.axis_size("dp")
+    devices = group * n_dp
+    count = group * rows
+    shard = w_query.shape[0]
+    dp = lax.axis_index("dp")
+    me = lax.axis_index("expert")
+    experts = router.shape[1]
+
+    reach = ancestry(parents)
+    start = dp * group
+    tree = lax.dynamic_slice(reach, (start, start), (group, group))
+    depth = jnp.sum(lax.dynamic_slice_in_dim(reach, start, group, 0), axis=1)
+    sees = tree + jnp.eye(group, dtype=F32)
+    bias = jnp.repeat(jnp.where(sees > 0.5, 0.0, NEGATIVE), rows, axis=1)
+    positions = (depth[:, None] * rows + jnp.arange(rows, dtype=F32)[None, :]).reshape(count)
+    frequencies = THETA ** (-2.0 * jnp.arange(HEAD_DIM // 2, dtype=F32) / HEAD_DIM)
+    angles = positions[:, None] * frequencies[None, :]
+    cosine, sine = jnp.cos(angles), jnp.sin(angles)
+
+    by_head = jnp.stack([w_query, w_key, w_value], axis=1).reshape(shard, 3, group, HEAD_DIM)
+    by_head = by_head.transpose(2, 0, 1, 3).reshape(group, shard, 3 * HEAD_DIM)
+    extra = jnp.concatenate(
+        [
+            jnp.stack([attn_gain, q_gain, k_gain, ffn_gain], axis=1),
+            router,
+            jnp.zeros((shard, HEAD_DIM - 4 - experts), BF16),
+        ],
+        axis=1,
+    )
+    extra = jnp.broadcast_to(extra[None], (group, shard, HEAD_DIM))
+    w_cut = jnp.concatenate([by_head, extra], axis=2)
+    normed_all, pre, w_all, gains, gate_w = project(tokens, w_cut, w_gate[0], n_dp, 0)
+    attn_g, ffn_g = gains[0:1], gains[3:4]
+    my_query_g = lax.dynamic_slice_in_dim(gains[1:2], me * HEAD_DIM, HEAD_DIM, 1)
+    my_key_g = lax.dynamic_slice_in_dim(gains[2:3], me * HEAD_DIM, HEAD_DIM, 1)
+    router_w = w_all[:, 3 * HEAD_DIM + 4 : 3 * HEAD_DIM + 4 + experts]
+    flat = range(devices)
+    blocks = []
+    for r in range(n_dp):
+        pairs = [(f, ((f + r) % n_dp) * group + f // n_dp) for f in flat]
+        blocks.append(lax.ppermute(w_out, BOTH, pairs))
+    blocks = jnp.stack(blocks)
+    out_head = jnp.concatenate(
+        [
+            lax.dynamic_index_in_dim(blocks, (dp - i) % n_dp, 0, keepdims=False)
+            for i in range(n_dp)
+        ]
+    )
+
+    query_pre, key_pre = pre[:, :HEAD_DIM], pre[:, HEAD_DIM : 2 * HEAD_DIM]
+    values = pre[:, 2 * HEAD_DIM :].astype(BF16)
+
+    def head_sum(a, b, cid):
+        sums = jnp.stack([jnp.sum(a, axis=-1), jnp.sum(b, axis=-1)]).reshape(1, -1, HEAD_DIM)
+        sums = jnp.sum(swap(sums, ("expert",), cid), axis=0).reshape(2, count, 1)
+        return sums[0] / width, sums[1] / width
+
+    query_mean, key_mean = head_sum(query_pre**2, key_pre**2, 1)
+    query_scale = lax.rsqrt(query_mean + EPSILON)
+    key_scale = lax.rsqrt(key_mean + EPSILON)
+    queries = turn(query_pre * query_scale * my_query_g, cosine, sine).astype(BF16)
+    keys = turn(key_pre * key_scale * my_key_g, cosine, sine).astype(BF16)
+    attn, lse, projected, up_w = attend(
+        queries, keys, values, bias, out_head, w_up[0], n_dp, 2
+    )
+    token_f = tokens.astype(F32)
+    residual = token_f + projected
+    second_scale = inverse_rms(residual)
+    normed_two = (residual * second_scale * ffn_g).astype(BF16)
+    logits = mm(normed_two, router_w)
+    router_probs = jax.nn.softmax(logits, axis=-1)
+    labels = jnp.arange(experts, dtype=jnp.int32)
+    routed = jnp.any(routes[:, :, None] == labels[None, None, :], axis=1)
+    gates_own = jnp.where(routed, router_probs, 0.0)
+
+    cap = 3 * rows * routes.shape[1] // (2 * experts)
+    taken, taken_grad, hidden, gate_pre_grad, up_pre_grad, sent_out, row_grad, gate_grad = expert(
+        normed_two, cotangent, gates_own.T[:, None], gate_w, up_w, w_down[0], n_dp, cap, 3
+    )
+    expert_grad, gate_grad_own = collect(
+        row_grad.reshape(group, rows, width), gate_grad, n_dp, 4
+    )
+    sums = (
+        t_mm(taken, gate_pre_grad),
+        t_mm(taken, up_pre_grad),
+        t_mm(hidden, taken_grad),
+    )
+    gate_grad_own = gate_grad_own.reshape(group, rows).T
+    combined = lax.psum_scatter(sent_out, "expert", scatter_dimension=0, tiled=True)
+    output = (residual + combined.astype(F32)).astype(BF16)
+
+    def dp_sum(total):
+        halves = total.reshape(n_dp, total.shape[0] // n_dp, -1)
+        theirs = lax.dynamic_index_in_dim(halves, 1 - dp, 0, keepdims=False).astype(BF16)
+        ours = lax.dynamic_index_in_dim(halves, dp, 0, keepdims=False)
+        theirs = lax.ppermute(theirs, "dp", [(d, 1 - d) for d in range(n_dp)])
+        return (ours + theirs.astype(F32))[None]
+
+    grad_gate, grad_up, grad_down = (dp_sum(s) for s in sums)
+
+    prob_grad = jnp.where(routed, gate_grad_own, 0.0)
+    logit_grad = (
+        router_probs * (prob_grad - jnp.sum(router_probs * prob_grad, axis=-1, keepdims=True))
+    ).astype(BF16)
+    router_grad = t_mm(logit_grad, normed_two)
+    normed_two_grad = expert_grad + mm_t(logit_grad, router_w)
+    ffn_gain_grad = jnp.sum(normed_two_grad * residual * second_scale, axis=0)
+    weighted = normed_two_grad * ffn_g
+    residual_grad = (
+        cotangent.astype(F32)
+        + second_scale * weighted
+        - residual * second_scale**3 * jnp.mean(weighted * residual, axis=-1, keepdims=True)
+    )
+    proj_grad = residual_grad.astype(BF16)
+
+    query_grad, key_grad, value_grad, out_w_grad = attend_back(
+        proj_grad, queries, keys, values, bias, out_head, attn, lse, n_dp, 5
+    )
+    query_turned = turn(query_grad * SCALE, cosine, -sine)
+    key_turned = turn(key_grad * SCALE, cosine, -sine)
+    query_mean, key_mean = head_sum(
+        query_turned * my_query_g * query_pre, key_turned * my_key_g * key_pre, 6
+    )
+    query_low = query_scale * my_query_g * query_turned - query_pre * query_scale**3 * query_mean
+    key_low = key_scale * my_key_g * key_turned - key_pre * key_scale**3 * key_mean
+    low = jnp.concatenate([query_low, key_low, value_grad], axis=1).astype(BF16)
+    query_gain_grad = jnp.sum(query_turned * query_pre * query_scale, axis=0)
+    key_gain_grad = jnp.sum(key_turned * key_pre * key_scale, axis=0)
+    normed_grad, got = unproject(
+        low, w_all, normed_all.reshape(count, width), rows, shard, n_dp, 7
+    )
+    attn_scale = inverse_rms(token_f)
+    attn_gain_grad = jnp.sum(normed_grad * token_f * attn_scale, axis=0)
+    weighted = normed_grad * attn_g
+    token_grad = (
+        residual_grad
+        + attn_scale * weighted
+        - token_f * attn_scale**3 * jnp.mean(weighted * token_f, axis=-1, keepdims=True)
+    )
+
+    got = got.reshape(group, shard, 3, HEAD_DIM).transpose(2, 1, 0, 3).reshape(3, shard, width)
+    got = got.astype(F32)
+    grad_out = jnp.zeros((shard, width), F32)
+    halves = out_w_grad.reshape(n_dp, shard, width)
+    for r in range(n_dp):
+        pairs = []
+        for d in range(n_dp):
+            for e in range(group):
+                pairs.append((d * group + e, e * n_dp + (d + r) % n_dp))
+        block = lax.dynamic_index_in_dim(halves, (dp + r) % n_dp, 0, keepdims=False)
+        grad_out = grad_out + lax.ppermute(block, BOTH, pairs)
+    head_gains = jnp.stack([query_gain_grad, key_gain_grad])
+    head_gains = lax.dynamic_update_slice_in_dim(
+        jnp.zeros((2, width), F32), head_gains, me * HEAD_DIM, 1
+    )
+    small = jnp.concatenate([router_grad, head_gains, ffn_gain_grad[None], attn_gain_grad[None]])
+    small = small.reshape(-1, devices, shard).transpose(1, 0, 2)
+    small = jnp.sum(swap(small, BOTH, 8), axis=0)
+    return (
+        output,
+        token_grad,
+        small[experts + 3],
+        small[experts],
+        small[experts + 1],
+        small[experts + 2],
+        got[0],
+        got[1],
+        got[2],
+        grad_out,
+        small[:experts].T,
+        grad_gate,
+        grad_up,
+        grad_down,
+    )
+
+
 def solution(mesh):
     row, vec = P(BOTH, None), P(BOTH)
     expert = P("expert", "dp", None)
+    wide = mesh.shape["expert"] != HEADS or mesh.shape["dp"] != 2
     return jax.shard_map(
-        per_device,
+        per_device if wide else per_head,
         mesh=mesh,
         in_specs=(row, vec, vec, vec, vec, row, row, row, row, row, expert, expert, expert, row, row, P()),
         out_specs=(row, row, vec, vec, vec, vec, row, row, row, row, row, expert, expert, expert),

time: 1010 us -> 900 us (0.89)
  matrix products: 210 us -> 29.5 us
  Pallas kernels: 568 us -> 719 us
  blocking collectives: 85.4 us -> 0 us
  waiting for transfers between devices: 1.44 us -> 22.2 us
  local copies, waits for them, and re-layouts: 43.8 us -> 29.5 us
    pallas_call x5 -> x6, Pallas kernels: 344 us -> 677 us  [the longest x1 195 us: expert(): pl.pallas_call(functools.partial(expert_kernel, group, n_dp, cap), out_sh...]
    pallas_call x8 -> x3, Pallas kernels: 224 us -> 42 us  [swap(): pl.pallas_call(functools.partial(swap_kernel, axes, sizes), out_shape=jax...]
    all_gather x2 -> x0, blocking collectives: 85.4 us -> none  [the longest x1 43 us: per_device(): router_w = lax.all_gather(router, BOTH, axis=0, tiled=True)]
    dot_general x8 -> x1, matrix products: 80.6 us -> 2.03 us  [mm_t(): lax.dot_general(a, b, (((1,), (1,)), ((), ())), preferred_element_type=F32)]
    dot_general x8 -> x1, matrix products: 70 us -> 1.85 us  [mm(): lax.dot_general(a, b, (((1,), (0,)), ((), ())), preferred_element_type=F32)]
    dot_general x8 -> x4, matrix products: 59.1 us -> 24.8 us  [t_mm(): lax.dot_general(a, b, (((0,), (0,)), ((), ())), preferred_element_type=F32)]
    ppermute x8 -> x7, waiting for transfers between devices: 0.02 us -> 22.1 us  [the longest x2 17.3 us: per_head(): grad_out = grad_out + lax.ppermute(block, BOTH, pairs)]
    convert_element_type x6 -> x3, other arithmetic: 18.3 us -> 3.63 us  [the longest x1 2.77 us: per_head(): proj_grad = residual_grad.astype(BF16)]
  transfers between devices with their start and end apart: 11 -> 8, of which waited for: 0 -> 3; matrix products, arithmetic and copies ran while one was open for 24% -> 10% of each run, Pallas kernels for 51% -> 26%
where the time goes in v2:
time: 900 us; the launch traced here: 890 us
  Pallas kernels  719 us (80%)
  other arithmetic  62.9 us (7%)
  local copies, waits for them, and re-layouts  29.5 us (3%)
  matrix products  29.5 us (3%)
  waiting for transfers between devices  22.2 us (2%)
  between operations  15.1 us (2%)
  starting transfers between devices  12.7 us (1%)
    pallas_call x1, Pallas kernels, expert(): pl.pallas_call(functools.partial(expert_kernel, group, n_dp, cap), out_sh...  195 us
    pallas_call x1, Pallas kernels, project(): pl.pallas_call(functools.partial(project_kernel, group, n_dp, shard), out...  121 us
    pallas_call x1, Pallas kernels, attend_back(): pl.pallas_call(functools.partial(attend_back_kernel, group, n_dp), out_sh...  100 us
    pallas_call x1, Pallas kernels, unproject(): pl.pallas_call(functools.partial(unproject_kernel, group, n_dp, shard), o...  98.6 us
    pallas_call x1, Pallas kernels, collect(): pl.pallas_call(functools.partial(collect_kernel, group, n_dp), out_shape=...  88 us
    pallas_call x1, Pallas kernels, attend(): pl.pallas_call(functools.partial(attend_kernel, group, n_dp), out_shape=[...  73.7 us
    pallas_call x3, Pallas kernels, swap(): pl.pallas_call(functools.partial(swap_kernel, axes, sizes), out_shape=jax...  42 us
    dot_general x4, matrix products, t_mm(): lax.dot_general(a, b, (((0,), (0,)), ((), ())), preferred_element_type=F32)  24.8 us
  transfers between devices with their start and end apart: 8, of which 3 were waited for; matrix products, arithmetic and copies ran while one was open for 10% of the time, Pallas kernels for 26%

profile of v2, /device:TPU:4, one launch (start us, length us, event | category | flops | bytes accessed | tf_op | source)
XLA Modules:
  0.0 890.4 jit_solution(6811011660042305866)
XLA Ops:
  7.2 4.4 collective-permute-start
  11.7 1.6 collective-permute-start.1
  13.3 1.0 copy.84
  14.8 1.0 copy.85
  16.4 1.0 copy.86
  17.9 1.8 maximum_bitcast_fusion
  21.2 1.1 pad_maximum_fusion.1.w_ref
  22.3 121.1 %shard_map.263 = (bf16[16,128,2048]{2,1,0:T(8,128)(2,1)}, f32[2048,384]{1,0:T(8,128)}, bf16[2048,512]{1,0:T(8,128)(2,1)}, f32[8,2048]{1,0:T(8,128)}, bf16[2048,1024]{1,0:T(8,128)(2,1)}) custom-call(bf16[128,2048]{1,0:T(8,128)(2,1)} %x_ref.1, bf16[16,64,512]{2,1,0:T(8,128)(2,1)} %pad_maximum_fusion.1.w_ref, bf16[1024,1024]{1,0:T(8,128)(2,1)} %bitcast.157), custom_call_target="tpu_custom_call" | custom-call | tf_op jit(solution)/shard_map/pallas_call | solution.py:494
  143.4 1.1 fusion.70
  144.5 2.2 multiply_reduce_fusion.8
  146.7 21.5 %shard_map.264 = f32[16,32,128]{2,1,0:T(8,128)S(1)} custom-call(f32[1,32,128]{2,1,0:T(8,128)S(1)} %reshape.229.in_ref), custom_call_target="tpu_custom_call" | custom-call | tf_op jit(solution)/shard_map/pallas_call | solution.py:788
  170.0 5.7 fusion.37
  175.8 1.1 pad_maximum_fusion.5.k_ref
  176.9 0.9 slice.201.v_ref
  178.6 2.3 pad_maximum_fusion.4.q_ref
  180.9 1.3 fusion.52
  182.2 0.8 pad_maximum_fusion.6.w_ref
  183.0 73.7 %shard_map.265 = (f32[2048,128]{1,0:T(8,128)}, f32[2048,128]{1,0:T(8,128)}, f32[128,2048]{1,0:T(8,128)}, bf16[2048,1024]{1,0:T(8,128)(2,1)}) custom-call(bf16[2048,128]{1,0:T(8,128)(2,1)} %pad_maximum_fusion.4.q_ref, bf16[2048,128]{1,0:T(8,128)(2,1)} %pad_maximum_fusion.5.k_ref, bf16[2048,128]{1,0:T(8,128)(2,1)} %slice.201.v_ref, f32[16,2048]{1,0:T(8,128)} %bitcast.162, ...), custom_call_target="tpu_custom_call" | custom-call | tf_op jit(solution)/shard_map/pallas_call | solution.py:553
  256.8 1.5 multiply_reduce_fusion.6
  258.3 0.9 copy-done.2
  259.4 1.8 fusion.71
  262.0 194.8 %shard_map.266 = (bf16[1536,2048]{1,0:T(8,128)(2,1)}, bf16[1536,2048]{1,0:T(8,128)(2,1)}, bf16[1536,1024]{1,0:T(8,128)(2,1)}, bf16[1536,1024]{1,0:T(8,128)(2,1)}...) custom-call(bf16[128,2048]{1,0:T(8,128)(2,1)} %copy-done.8, ...), custom_call_target="tpu_custom_call" | custom-call | tf_op jit(solution)/shard_map/pallas_call | solution.py:918
  456.8 10.6 %fusion.74 = f32[2048,1024]{1,0:T(8,128)S(1)} fusion(bf16[1536,2048]{1,0:T(8,128)(2,1)} %get-tuple-element.59, bf16[1536,1024]{1,0:T(8,128)(2,1)} %get-tuple-element.61), kind=kOutput, calls=%fused_computation.166 | convolution fusion | flops 6442450944 | bytes 17825792 | tf_op jit(solution)/shard_map/dot_general | solution.py:31
  467.5 1.7 fusion.4
  469.1 1.4 collective-permute-start.5
  470.6 1.5 copy-done.29
  472.0 7.0 fusion.73
  479.1 1.7 fusion.3
  480.7 1.5 collective-permute-start.4
  482.2 1.1 copy-done.28
  483.3 7.0 fusion.75
  490.4 1.8 fusion.5
  492.2 1.4 collective-permute-start.6
  494.3 88.0 %shard_map.267 = (f32[128,2048]{1,0:T(8,128)}, f32[16,1,128]{2,1,0:T(1,128)}) custom-call(bf16[16,128,2048]{2,1,0:T(8,128)(2,1)} %bitcast.145, f32[16,1,128]{2,1,0:T(1,128)} %get-tuple-element.47.gate_ref), custom_call_target="tpu_custom_call" | custom-call | tf_op jit(solution)/shard_map/pallas_call | solution.py:972
  584.1 0.9 copy.79
  584.9 2.0 multiply_reduce_fusion
  587.1 6.0 fusion.1
  593.1 6.0 fusion.2
  599.2 4.8 collective-permute-done.6
  604.0 4.3 fusion
  608.3 2.8 fusion.68
  611.1 100.4 %shard_map.268 = (f32[2048,128]{1,0:T(8,128)}, f32[2048,128]{1,0:T(8,128)}, f32[2048,128]{1,0:T(8,128)}, f32[128,2048]{1,0:T(8,128)}) custom-call(bf16[128,2048]{1,0:T(8,128)(2,1)} %get-tuple-element.76.g_ref, bf16[2048,128]{1,0:T(8,128)(2,1)} %pad_maximum_fusion.4.q_ref, bf16[2048,128]{1,0:T(8,128)(2,1)} %pad_maximum_fusion.5.k_ref, ...), custom_call_target="tpu_custom_call" | custom-call | tf_op jit(solution)/shard_map/pallas_call | solution.py:635
  711.5 1.3 broadcast_multiply_fusion
  712.8 1.3 broadcast_multiply_fusion.1
  714.2 4.5 fusion.30
  718.8 1.9 multiply_reduce_fusion.2
  720.7 7.3 shard_map.269
  728.1 2.1 convert.33
  730.3 4.4 subtract_convert_fusion.1
  734.8 1.4 pad_maximum_fusion.low_ref
  736.2 98.6 %shard_map.270 = (f32[128,2048]{1,0:T(8,128)}, bf16[16,64,384]{2,1,0:T(8,128)(2,1)}) custom-call(bf16[2048,384]{1,0:T(8,128)(2,1)} %pad_maximum_fusion.low_ref, bf16[2048,512]{1,0:T(8,128)(2,1)} %get-tuple-element.42.w_ref, bf16[2048,2048]{1,0:T(8,128)(2,1)} %bitcast.146), custom_call_target="tpu_custom_call" | custom-call | tf_op jit(solution)/shard_map/pallas_call | solution.py:698
  834.8 2.2 fusion.45
  837.2 13.2 %shard_map.271 = f32[32,20,64]{2,1,0:T(8,128)S(1)} custom-call(f32[32,20,64]{2,1,0:T(8,128)S(1)} %maximum_bitcast_fusion.1.in_ref), custom_call_target="tpu_custom_call" | custom-call | tf_op jit(solution)/shard_map/pallas_call | solution.py:788
  851.6 1.1 dynamic-slice_bitcast_fusion
  852.6 2.2 collective-permute-start.2
  854.9 2.4 reshape.239
  857.3 1.6 fusion.69
  859.3 1.0 copy.95
  860.5 1.0 copy.96
  861.8 1.0 copy.97
  862.8 1.3 fusion.42
  864.1 7.2 collective-permute-done.2
  871.3 10.1 %collective-permute-done.3 = f32[64,2048]{1,0:T(8,128)} collective-permute-done((f32[64,2048]{1,0:T(8,128)}, f32[64,2048]{1,0:T(8,128)}, u32[]{:S(2)}, u32[]{:S(2)}) %collective-permute-start.3) | collective-permute-done | bytes 524320 | tf_op jit(solution)/shard_map/ppermute | solution.py:1466
  881.4 1.9 add.207
  (142 shorter events, 11.7 us)
Async XLA Ops:
  7.2 601.1 %reduce-scatter.2.cloned.1.call-start = ((), (), s32[]{:S(2)}) async-start(), calls=%async_computation.1 | async-start | bytes 8912896 | tf_op jit(solution)/shard_map/reduce_scatter | solution.py:1404
  7.2 173.7 %collective-permute-start = (bf16[64,2048]{1,0:T(8,128)(2,1)}, bf16[64,2048]{1,0:T(8,128)(2,1)}, u32[]{:S(2)}, u32[]{:S(2)}) collective-permute-start(bf16[64,2048]{1,0:T(8,128)(2,1)} %param.24), channel_id=1, source_target_pairs={{0,0},{1,16},{2,1},{3,17},{4,2},{5,18},{6,3},{7,19},{8,4},{9,20},{... | collective-permute-start | bytes 786440 | tf_op jit(solution)/shard_map/ppermute | solution.py:1356
  11.7 169.2 %collective-permute-start.1 = (bf16[64,2048]{1,0:T(8,128)(2,1)}, bf16[64,2048]{1,0:T(8,128)(2,1)}, u32[]{:S(2)}, u32[]{:S(2)}) collective-permute-start(bf16[64,2048]{1,0:T(8,128)(2,1)} %param.24), channel_id=1, source_target_pairs={{0,16},{1,0},{2,17},{3,1},{4,18},{5,2},{6,19},{7,3},{8,20},{9,4},{... | collective-permute-start | bytes 786440 | tf_op jit(solution)/shard_map/ppermute | solution.py:1356
  15.8 4.6 copy-start.24
  15.8 4.7 copy-start.25
  15.8 4.8 copy-start.26
  15.9 4.9 copy-start.27
  15.9 5.0 copy-start.21
  22.3 146.0 %copy-start.30 = (s32[32]{0:T(128)S(1)}, s32[32]{0:T(128)}, u32[]{:S(2)}) copy-start(s32[32]{0:T(128)} %param.31) | copy-start | bytes 388
  22.3 147.0 %copy-start.22 = (s32[128,8]{0,1:T(8,128)S(1)}, s32[128,8]{0,1:T(8,128)}, u32[]{:S(2)}) copy-start(s32[128,8]{0,1:T(8,128)} %param.30) | copy-start | bytes 12292
  143.3 25.9 %copy-start = (f32[2048,384]{1,0:T(8,128)S(1)}, f32[2048,384]{1,0:T(8,128)}, u32[]{:S(2)}) copy-start(f32[2048,384]{1,0:T(8,128)} %get-tuple-element.39) | copy-start | bytes 9437188
  180.9 75.9 %copy-start.10 = (bf16[128,2048]{1,0:T(8,128)(2,1)S(1)}, bf16[128,2048]{1,0:T(8,128)(2,1)}, u32[]{:S(2)}) copy-start(bf16[128,2048]{1,0:T(8,128)(2,1)} %x_ref.1) | copy-start | bytes 1572868
  258.3 1.0 copy-start.2
  259.4 2.5 copy-start.8
  456.7 13.8 %slice-start.4 = ((s8[6291456]{0:T(1024)(128)(4,1)}), s8[2097152]{0:T(1024)(128)(4,1)S(1)}, s32[]{:S(2)}) async-start(s8[6291456]{0:T(1024)(128)(4,1)} %bitcast.195), calls=%async_computation.6 | async-start | bytes 4194304
  456.8 13.8 %slice-start.5 = ((s8[6291456]{0:T(1024)(128)(4,1)}), s8[4194304]{0:T(1024)(128)(4,1)S(1)}, s32[]{:S(2)}) async-start(s8[6291456]{0:T(1024)(128)(4,1)} %bitcast.195), calls=%async_computation.7 | async-start | bytes 8388608
  467.4 11.6 %copy-start.12 = (f32[2048,1024]{1,0:T(8,128)}, f32[2048,1024]{1,0:T(8,128)S(1)}, u32[]{:S(2)}) copy-start(f32[2048,1024]{1,0:T(8,128)S(1)} %fusion.74) | copy-start | bytes 25165828
  467.4 4.6 copy-start.29
  467.4 14.8 %slice-start.2 = ((s8[6291456]{0:T(1024)(128)(4,1)}), s8[4194304]{0:T(1024)(128)(4,1)S(1)}, s32[]{:S(2)}) async-start(s8[6291456]{0:T(1024)(128)(4,1)} %bitcast.193), calls=%async_computation.4 | async-start | bytes 8388608
  469.1 118.0 %collective-permute-start.5 = (bf16[1024,1024]{1,0:T(8,128)(2,1)}, bf16[1024,1024]{1,0:T(8,128)(2,1)}, u32[]{:S(2)}, u32[]{:S(2)}) collective-permute-start(bf16[1024,1024]{1,0:T(8,128)(2,1)} %fusion.4), channel_id=1, source_target_pairs={{0,16},{16,0},{1,17},{17,1},{2,18},{18,2},{3,19},{19,3},{4,20},{20... | collective-permute-start | bytes 6291464 | tf_op jit(solution)/shard_map/ppermute | solution.py:1411
  472.0 10.2 %slice-start.3 = ((s8[6291456]{0:T(1024)(128)(4,1)}), s8[2097152]{0:T(1024)(128)(4,1)S(1)}, s32[]{:S(2)}) async-start(s8[6291456]{0:T(1024)(128)(4,1)} %bitcast.193), calls=%async_computation.5 | async-start | bytes 4194304
  479.1 11.3 %copy-start.13 = (f32[2048,1024]{1,0:T(8,128)}, f32[2048,1024]{1,0:T(8,128)S(1)}, u32[]{:S(2)}) copy-start(f32[2048,1024]{1,0:T(8,128)S(1)} %fusion.73) | copy-start | bytes 25165828
  479.1 4.2 copy-start.28
  480.7 112.4 %collective-permute-start.4 = (bf16[1024,1024]{1,0:T(8,128)(2,1)}, bf16[1024,1024]{1,0:T(8,128)(2,1)}, u32[]{:S(2)}, u32[]{:S(2)}) collective-permute-start(bf16[1024,1024]{1,0:T(8,128)(2,1)} %fusion.3), channel_id=1, source_target_pairs={{0,16},{16,0},{1,17},{17,1},{2,18},{18,2},{3,19},{19,3},{4,20},{20... | collective-permute-start | bytes 6291464 | tf_op jit(solution)/shard_map/ppermute | solution.py:1411
  490.4 4.0 copy-start.14
  492.2 111.8 %collective-permute-start.6 = (bf16[512,2048]{1,0:T(8,128)(2,1)}, bf16[512,2048]{1,0:T(8,128)(2,1)}, u32[]{:S(2)}, u32[]{:S(2)}) collective-permute-start(bf16[512,2048]{1,0:T(8,128)(2,1)} %fusion.5), channel_id=1, source_target_pairs={{0,16},{16,0},{1,17},{17,1},{2,18},{18,2},{3,19},{19,3},{4,20},{20... | collective-permute-start | bytes 6291464 | tf_op jit(solution)/shard_map/ppermute | solution.py:1411
  494.3 89.4 %copy-start.9 = (bf16[128,2048]{1,0:T(8,128)(2,1)S(1)}, bf16[128,2048]{1,0:T(8,128)(2,1)}, u32[]{:S(2)}) copy-start(bf16[128,2048]{1,0:T(8,128)(2,1)} %copy-done.8) | copy-start | bytes 1572868
  494.3 90.6 %copy-start.3 = (f32[128,2048]{1,0:T(8,128)S(1)}, f32[128,2048]{1,0:T(8,128)}, u32[]{:S(2)}) copy-start(f32[128,2048]{1,0:T(8,128)} %copy-done.2) | copy-start | bytes 3145732
  587.1 16.9 %slice-start = ((s8[8388608]{0:T(1024)(128)(4,1)}), s8[4194304]{0:T(1024)(128)(4,1)S(1)}, s32[]{:S(2)}) async-start(s8[8388608]{0:T(1024)(128)(4,1)} %bitcast.153), calls=%async_computation.2 | async-start | bytes 8388608
  593.1 10.9 %slice-start.1 = ((s8[8388608]{0:T(1024)(128)(4,1)}), s8[4194304]{0:T(1024)(128)(4,1)S(1)}, s32[]{:S(2)}) async-start(s8[8388608]{0:T(1024)(128)(4,1)} %bitcast.153), calls=%async_computation.3 | async-start | bytes 8388608
  599.2 9.1 %copy-start.17 = (bf16[128,2048]{1,0:T(8,128)(2,1)S(1)}, bf16[128,2048]{1,0:T(8,128)(2,1)}, u32[]{:S(2)}) copy-start(bf16[128,2048]{1,0:T(8,128)(2,1)} %cot_ref.1) | copy-start | bytes 1572868
  714.2 4.6 copy-start.1
  718.7 1.9 copy-start.4
  718.7 1.9 copy-start.5
  718.7 1.9 copy-start.6
  718.7 2.0 copy-start.7
  730.3 4.5 copy-start.18
  736.2 98.6 %copy-start.11 = (bf16[128,2048]{1,0:T(8,128)(2,1)S(1)}, bf16[128,2048]{1,0:T(8,128)(2,1)}, u32[]{:S(2)}) copy-start(bf16[128,2048]{1,0:T(8,128)(2,1)} %x_ref.1) | copy-start | bytes 1572868
  736.2 100.9 %copy-start.20 = (f32[16,32,64]{2,0,1:T(8,128)S(1)}, f32[16,32,64]{2,0,1:T(8,128)}, u32[]{:S(2)}) copy-start(f32[16,32,64]{2,0,1:T(8,128)} %copy.79) | copy-start | bytes 393220
  834.8 16.8 %copy-start.19 = (f32[128,2048]{1,0:T(8,128)S(1)}, f32[128,2048]{1,0:T(8,128)}, u32[]{:S(2)}) copy-start(f32[128,2048]{1,0:T(8,128)} %get-tuple-element.58) | copy-start | bytes 3145732
  852.6 18.7 %collective-permute-start.2 = (f32[64,2048]{1,0:T(8,128)}, f32[64,2048]{1,0:T(8,128)S(1)}, u32[]{:S(2)}, u32[]{:S(2)}) collective-permute-start(f32[64,2048]{1,0:T(8,128)} %get-tuple-element.96), channel_id=1, source_target_pairs={{0,0},{1,2},{2,4},{3,6},{4,8},{5,10},{6,12},{7,14},{8,16},{9,18},{... | collective-permute-start | bytes 1572872 | tf_op jit(solution)/shard_map/ppermute | solution.py:1466
  854.8 26.6 %collective-permute-start.3 = (f32[64,2048]{1,0:T(8,128)}, f32[64,2048]{1,0:T(8,128)}, u32[]{:S(2)}, u32[]{:S(2)}) collective-permute-start(f32[64,2048]{1,0:T(8,128)} %get-tuple-element.95), channel_id=1, source_target_pairs={{0,1},{1,3},{2,5},{3,7},{4,9},{5,11},{6,13},{7,15},{8,17},{9,19},{... | collective-permute-start | bytes 1572872 | tf_op jit(solution)/shard_map/ppermute | solution.py:1466
  858.9 3.8 copy-start.23
  858.9 3.8 copy-start.15
  858.9 3.8 copy-start.16
Sparse Core Ops, SparseCore 0:
  456.9 123.8 reduce-scatter.1

commit v3 on v2

--- a/solution.py
+++ b/solution.py
@@ -82,76 +82,88 @@
     pl.semaphore_wait(barrier, group if n_dp == 2 else group - 1)
 
 
-def nearest(zs, z, i):
-    low = jnp.minimum(z, zs - 1 - z)
-    step = (i + 1) // 2
-    paired = jnp.where(i % 2 == 1, z - step, z + step)
-    alone = jnp.where(z > zs - 1 - z, z - (i - low), z + (i - low))
-    return jnp.where(i <= 2 * low, paired, alone)
-
-
 def gather_blocks(zs, buffers, process):
     z, x, c = spot()
     far = zs - 1
 
-    def copies(block, kind, e):
-        return [
-            pltpu.make_async_remote_copy(
-                src_ref=all_ref.at[block],
-                dst_ref=all_ref.at[block],
-                send_sem=send.at[kind, block],
-                recv_sem=recv.at[block],
-                device_id={"expert": e},
-                device_id_type=MESH,
-            )
-            for all_ref, send, recv in buffers
-        ]
-
-    def to_sibling(block):
-        return copies(block, SIB, at(z, x, 1 - c))
-
-    def to_across(block):
-        return copies(block, ACROSS, at(z, 1 - x, c))
-
-    def to_up(block):
-        return copies(block, UP, at(z + 1, x, c))
-
-    def to_down(block):
-        return copies(block, DOWN, at(z - 1, x, c))
-
-    def step(i, carry):
-        @pl.when(i < zs)
+    def copy(n, block, kind, e):
+        all_ref, send, recv = buffers[n]
+        return pltpu.make_async_remote_copy(
+            src_ref=all_ref.at[block],
+            dst_ref=all_ref.at[block],
+            send_sem=send.at[kind, block],
+            recv_sem=recv.at[block],
+            device_id={"expert": e},
+            device_id_type=MESH,
+        )
+
+    def to_sibling(n, block):
+        return copy(n, block, SIB, at(z, x, 1 - c))
+
+    def to_across(n, block):
+        return copy(n, block, ACROSS, at(z, 1 - x, c))
+
+    def to_up(n, block):
+        return copy(n, block, UP, at(z + 1, x, c))
+
+    def to_down(n, block):
+        return copy(n, block, DOWN, at(z - 1, x, c))
+
+    def sides(d, do):
+        def side(s, carry):
+            zz = jnp.where(s == 0, z - d, z + d)
+
+            @pl.when((zz >= 0) & (zz <= far) & ((d > 0) | (s == 0)))
+            def _():
+                do(zz)
+
+            return carry
+
+        lax.fori_loop(0, 2, side, 0)
+
+    def column(n, d, zz):
+        block = at(zz, x, c)
+
+        @pl.when(d > 0)
         def _():
-            zz = nearest(zs, z, i)
-            block = at(zz, x, c)
-            over = at(zz, 1 - x, c)
+            to_sibling(n, block).wait_recv()
+
+        @pl.when((zz <= z) & (z < far))
+        def _():
+            to_up(n, block).start()
+
+        @pl.when((zz >= z) & (z > 0))
+        def _():
+            to_down(n, block).start()
+
+        to_across(n, block).start()
+        to_sibling(n, block).start()
+
+    def across(n, zz):
+        over = to_sibling(n, at(zz, 1 - x, c))
+        over.wait_recv()
+        over.start()
+
+    def ready(d, zz):
+        for n in range(len(buffers)):
+            for xx in range(2):
+                to_sibling(n, at(zz, xx, 1 - c)).wait_recv()
+        process(d, zz)
+
+    def step(d, carry):
+        @pl.when(d < zs)
+        def _():
             for n in range(len(buffers)):
-
-                @pl.when(i > 0)
-                def _():
-                    to_sibling(block)[n].wait_recv()
-
-                @pl.when((zz <= z) & (z < far))
-                def _():
-                    to_up(block)[n].start()
-
-                @pl.when((zz >= z) & (z > 0))
-                def _():
-                    to_down(block)[n].start()
-
-                to_across(block)[n].start()
-                to_sibling(block)[n].start()
+                sides(d, lambda zz, n=n: column(n, d, zz))
+
+        @pl.when(d > 0)
+        def _():
+            sides(d - 1, lambda zz: ready(d - 1, zz))
+
+        @pl.when(d < zs)
+        def _():
             for n in range(len(buffers)):
-                to_sibling(over)[n].wait_recv()
-                to_sibling(over)[n].start()
-
-        @pl.when(i > 0)
-        def _():
-            zz = nearest(zs, z, i - 1)
-            for xx in range(2):
-                for copy in to_sibling(at(zz, xx, 1 - c)):
-                    copy.wait_recv()
-            process(i - 1, zz)
+                sides(d, lambda zz, n=n: across(n, zz))
 
         return carry
 
@@ -159,18 +171,18 @@
 
     def done(zz, carry):
         block = at(zz, x, c)
-        for copy in to_across(block) + to_sibling(block) + to_sibling(at(zz, 1 - x, c)):
-            copy.wait_send()
-
-        @pl.when((zz <= z) & (z < far))
-        def _():
-            for copy in to_up(block):
-                copy.wait_send()
-
-        @pl.when((zz >= z) & (z > 0))
-        def _():
-            for copy in to_down(block):
-                copy.wait_send()
+        for n in range(len(buffers)):
+            to_across(n, block).wait_send()
+            to_sibling(n, block).wait_send()
+            to_sibling(n, at(zz, 1 - x, c)).wait_send()
+
+            @pl.when((zz <= z) & (z < far))
+            def _():
+                to_up(n, block).wait_send()
+
+            @pl.when((zz >= z) & (z > 0))
+            def _():
+                to_down(n, block).wait_send()
 
         return carry
 
@@ -199,7 +211,7 @@
     return [pltpu.SemaphoreType.DMA((4, group)), pltpu.SemaphoreType.DMA((group,))]
 
 
-def scatter_blocks(zs, part_ref, out_ref, r_sib, r_x, r_z, s_x, s_z, send, recv, produce, pause=None):
+def scatter_blocks(zs, part_ref, out_ref, r_sib, r_x, r_z, s_x, s_z, send, recv, produce, pause=None, work=None):
     z, x, c = spot()
     far = zs - 1
 
@@ -239,8 +251,10 @@
     def down(zz):
         return along(zz, DOWN, at(z - 1, x, c))
 
-    def order(do):
+    def order(do, between=None):
         for d in range(far, 0, -1):
+            if between is not None:
+                between(far - d)
 
             @pl.when(z + d <= far)
             def _():
@@ -250,6 +264,8 @@
             def _():
                 do(z - d)
 
+        if between is not None:
+            between(far)
         do(z)
 
     def cross(zz):
@@ -320,7 +336,7 @@
                 down(zz).wait_recv()
                 out_ref[...] += r_z[1, zz].astype(F32)
 
-    order(finish)
+    order(finish, work)
 
     def done(zz, carry):
         to_sibling(zz, 0).wait_send()
@@ -423,67 +439,82 @@
     group, n_dp, shard,
     x_ref, w_ref, pay_ref,
     normed_ref, pre_ref, w_all, gains_ref, pay_out,
-    x_all, send, recv, local, w_send, w_recv, dp_send, dp_recv,
+    x_all, send, recv, local, w_send, w_recv, dp_send, dp_recv, pay_send, pay_recv,
 ):
     me, dp = lax.axis_index("expert"), lax.axis_index("dp")
-    mine = pltpu.make_async_copy(x_ref, x_all.at[me], local.at[0])
-    mine.start()
+    rows = x_ref.shape[0]
     half = group * shard
 
     def rows_of(d, e):
         return w_all.at[pl.ds(d * half + e * shard, shard)]
 
+    mine = pltpu.make_async_copy(x_ref, x_all.at[me], local.at[0])
     own = pltpu.make_async_copy(w_ref.at[me], rows_of(dp, me), local.at[1])
+    pay_start, pay_finish = joined(pay_ref, pay_out, local.at[2], pay_send, pay_recv)
+    mine.start()
     own.start()
     greet_all(group, n_dp)
-    start, finish_recv, finish_send = tree_swap(
-        group, lambda d, src: (w_ref.at[d], rows_of(dp, src)), w_send, w_recv
-    )
-    start()
+
+    def piece(e):
+        return over_dp(rows_of(dp, e), rows_of(dp, e), dp_send.at[e], dp_recv.at[e])
+
+    def w_copy(d, src, k):
+        return pltpu.make_async_remote_copy(
+            src_ref=w_ref.at[d],
+            dst_ref=rows_of(dp, src),
+            send_sem=w_send.at[k],
+            recv_sem=w_recv.at[src],
+            device_id={"expert": d},
+            device_id_type=MESH,
+        )
+
+    def w_start(k, carry):
+        w_copy((me + k) % group, me, k).start()
+        return carry
+
+    def w_pass(k, carry):
+        e = (me + group - k) % group
+        w_copy((me + k) % group, e, k).wait_recv()
+        piece(e).start()
+        return carry
+
+    lax.fori_loop(1, group, w_start, 0)
+    pay_start()
+    own.wait()
+    piece(me).start()
+    lax.fori_loop(1, group, w_pass, 0)
     mine.wait()
-    own.wait()
-
-    def bundle(d):
-        piece = w_all.at[pl.ds(d * half, half)]
-        return over_dp(piece, piece, dp_send.at[0], dp_recv.at[0])
-
-    pay_start, pay_finish = joined(pay_ref, pay_out, local.at[2], dp_send.at[1], dp_recv.at[1])
-
-    def compute(block):
-        rows = x_ref.shape[0]
+    pick = lax.broadcasted_iota(jnp.int32, (8, HEAD_DIM), 0)
+    lane = lax.broadcasted_iota(jnp.int32, (8, HEAD_DIM), 1)
+    pick = jnp.where(pick == lane, 1.0, 0.0).astype(BF16)
+
+    def w_done(e, carry):
+        piece(e).wait()
+        return carry
+
+    def compute(block, carry):
         values = x_all[block].astype(F32)
         scale = lax.rsqrt(jnp.mean(values * values, axis=-1, keepdims=True) + EPSILON)
         normed = (values * scale * gains_ref[0:1, :]).astype(BF16)
         normed_ref[block] = normed
         pre_ref[pl.ds(block * rows, rows), :] = mm(normed, w_all[:, : 3 * HEAD_DIM])
-
-    def weights_here():
-        finish_recv()
-        bundle(dp).start()
-        pay_start()
-
-    def weights_done():
-        bundle(1 - dp).wait_recv()
-        pick = lax.broadcasted_iota(jnp.int32, (8, HEAD_DIM), 0)
-        lane = lax.broadcasted_iota(jnp.int32, (8, HEAD_DIM), 1)
-        pick = jnp.where(pick == lane, 1.0, 0.0).astype(BF16)
-        gains_ref[...] = mm_t(pick, w_all[:, 3 * HEAD_DIM :])
-
-    def process(i, zz):
-        @pl.when(i == 0)
+        return carry
+
+    def process(d, zz):
+        @pl.when(d == 0)
         def _():
-            weights_here()
-            weights_done()
-
-        def one(j, carry):
-            compute(zz * 4 + j)
-            return carry
-
-        lax.fori_loop(0, 4, one, 0)
+            lax.fori_loop(0, group, w_done, 0)
+            gains_ref[...] = mm_t(pick, w_all[:, 3 * HEAD_DIM :])
+
+        lax.fori_loop(zz * 4, zz * 4 + 4, compute, 0)
 
     gather_blocks(group // 4, [(x_all, send, recv)], process)
-    finish_send()
-    bundle(dp).wait_send()
+
+    def w_sent(k, carry):
+        w_copy((me + k) % group, me, k).wait_send()
+        return carry
+
+    lax.fori_loop(1, group, w_sent, 0)
     pay_finish()
 
 
@@ -508,8 +539,10 @@
             DMA((3,)),
             DMA((group,)),
             DMA((group,)),
-            DMA((2,)),
-            DMA((2,)),
+            DMA((group,)),
+            DMA((group,)),
+            DMA,
+            DMA,
         ],
         compiler_params=params(cid),
     )(tokens, w_cut, payload)
@@ -573,87 +606,109 @@
 
 def attend_back_kernel(
     group, n_dp,
-    g_ref, q_ref, k_ref, v_ref, bias_ref, w_ref, attn_ref, lse_ref,
-    dq_ref, dk_ref, dv_ref, dw_ref,
-    g_all, send, recv, local,
+    g_ref, q_ref, k_ref, v_ref, bias_ref, w_ref, attn_ref, lse_ref, pay_ref, more_ref,
+    dq_ref, dk_ref, dv_ref, dw_ref, pay_out, more_out,
+    g_all, send, recv, local, dp_send, dp_recv,
 ):
     me = lax.axis_index("expert")
-    rows = g_ref.shape[0]
-    count = k_ref.shape[0]
-    chunk = min(count, 512)
+    rows, width = g_ref.shape
+    quad = 4 * rows
     mine = pltpu.make_async_copy(g_ref, g_all.at[me], local)
     mine.start()
     greet_all(group, n_dp)
     mine.wait()
+    some = more_out.shape[0]
+    payloads = [
+        over_dp(pay_ref, pay_out, dp_send.at[0], dp_recv.at[0]),
+        over_dp(more_ref.at[pl.ds(0, some)], more_out, dp_send.at[1], dp_recv.at[1]),
+    ]
+    for payload in payloads:
+        payload.start()
     dk_ref[...] = jnp.zeros_like(dk_ref)
     dv_ref[...] = jnp.zeros_like(dv_ref)
     dw_ref[...] = jnp.zeros_like(dw_ref)
-
-    def process(block):
-        first = block * rows
-        here = pl.ds(first, rows)
-        grad = g_all[block]
+    query = lax.broadcasted_iota(jnp.int32, (quad, quad), 0)
+    key = lax.broadcasted_iota(jnp.int32, (quad, quad), 1)
+
+    def process(d, zz):
+        here = pl.ds(zz * quad, quad)
+        grad = g_all[pl.ds(zz * 4, 4)].reshape(quad, width)
         attn = attn_ref[here, :]
         mixed_grad = mm_t(grad, w_ref[...]).astype(BF16)
         dw_ref[...] += t_mm(attn.astype(BF16), grad)
         delta = jnp.sum(mixed_grad.astype(F32) * attn, axis=-1, keepdims=True)
         queries = q_ref[here, :]
         lse = lse_ref[here, :][:, :1]
-        query = first + lax.broadcasted_iota(jnp.int32, (rows, chunk), 0)
 
         def turn_keys(j, dq):
-            cut = pl.ds(j * chunk, chunk)
+            cut = pl.ds(pl.multiple_of(j * quad, quad), quad)
             keys = k_ref[cut, :]
-            scores = mm_t(queries, keys) * SCALE + bias_ref[pl.ds(block, 1), cut]
-            key = j * chunk + lax.broadcasted_iota(jnp.int32, (rows, chunk), 1)
-            probs = jnp.exp(jnp.where(key <= query, scores - lse, NEGATIVE))
-            score_grad = probs * (mm_t(mixed_grad, v_ref[cut, :]) - delta)
-            score_grad = score_grad.astype(BF16)
+            bias = jnp.concatenate(
+                [
+                    jnp.broadcast_to(bias_ref[pl.ds(zz * 4 + i, 1), cut], (rows, quad))
+                    for i in range(4)
+                ]
+            )
+            scores = mm_t(queries, keys) * SCALE + bias - lse
+            seen = key + (j - zz) * quad <= query
+            probs = jnp.exp(jnp.where(seen, scores, NEGATIVE))
+            score_grad = (probs * (mm_t(mixed_grad, v_ref[cut, :]) - delta)).astype(BF16)
             dk_ref[cut, :] += t_mm(score_grad, queries)
             dv_ref[cut, :] += t_mm(probs.astype(BF16), mixed_grad)
             return dq + mm(score_grad, keys)
 
-        turns = (first + rows + chunk - 1) // chunk
-        dq = lax.fori_loop(0, turns, turn_keys, jnp.zeros((rows, HEAD_DIM), F32))
-        dq_ref[here, :] = dq
-
-    def four(i, zz):
-        def one(j, carry):
-            process(zz * 4 + j)
-            return carry
-
-        lax.fori_loop(0, 4, one, 0)
-
-    gather_blocks(group // 4, [(g_all, send, recv)], four)
-
-
-def attend_back(grad, queries, keys, values, bias, w_rows, attn, lse, n_dp, cid):
+        dq_ref[here, :] = lax.fori_loop(
+            0, zz + 1, turn_keys, jnp.zeros((quad, HEAD_DIM), F32)
+        )
+
+    gather_blocks(group // 4, [(g_all, send, recv)], process)
+    for payload in payloads:
+        payload.wait()
+
+
+def attend_back(grad, queries, keys, values, bias, w_rows, attn, lse, payload, more, n_dp, cid):
     group = bias.shape[0]
     rows, width = grad.shape
     count = queries.shape[0]
     long = jax.ShapeDtypeStruct((count, HEAD_DIM), F32)
     return pl.pallas_call(
         functools.partial(attend_back_kernel, group, n_dp),
-        out_shape=[long, long, long, jax.ShapeDtypeStruct((HEAD_DIM, width), F32)],
-        in_specs=[HBM] + [VMEM] * 7,
-        out_specs=[VMEM] * 4,
-        scratch_shapes=[pltpu.VMEM((group, rows, width), BF16), *gather_sems(group), DMA],
+        out_shape=[
+            long, long, long,
+            jax.ShapeDtypeStruct((HEAD_DIM, width), F32),
+            jax.ShapeDtypeStruct(payload.shape, payload.dtype),
+            jax.ShapeDtypeStruct((more.shape[0] // 2, more.shape[1]), more.dtype),
+        ],
+        in_specs=[HBM] + [VMEM] * 7 + [HBM] * 2,
+        out_specs=[VMEM] * 4 + [HBM] * 2,
+        scratch_shapes=[
+            pltpu.VMEM((group, rows, width), BF16),
+            *gather_sems(group),
+            DMA,
+            DMA((2,)),
+            DMA((2,)),
+        ],
         compiler_params=params(cid),
-    )(grad, queries, keys, values, bias, w_rows, attn, lse)
+    )(grad, queries, keys, values, bias, w_rows, attn, lse, payload, more)
 
 
 def unproject_kernel(
     group, n_dp, shard,
-    low_ref, w_ref, normed_ref,
-    sum_ref, got_ref,
+    low_ref, w_ref, normed_ref, more_ref,
+    sum_ref, got_ref, more_out,
     part, r_sib, r_x, r_z, s_x, s_z, send, recv,
-    mine, theirs, w_send, w_recv, dp_send, dp_recv,
+    mine, theirs, w_send, w_recv, dp_send, dp_recv, pay_send, pay_recv,
 ):
     me, dp = lax.axis_index("expert"), lax.axis_index("dp")
     rows = sum_ref.shape[0]
     half = group * shard
     greet_all(group, n_dp)
     step = min(half, 256)
+
+    some = more_out.shape[0]
+    payloads = [
+        over_dp(more_ref.at[pl.ds(some, some)], more_out, pay_send, pay_recv),
+    ]
 
     def slice_grad(d, ref):
         def one(i, carry):
@@ -676,22 +731,31 @@
 
     start, finish_recv, finish_send = tree_swap(group, make, w_send, w_recv)
 
-    def pause():
-        slice_grad(1 - dp, theirs.at[0])
-        to_dp.start()
-        slice_grad(dp, mine)
-        to_dp.wait_recv()
-        mine[...] = (mine[...].astype(F32) + theirs[1].astype(F32)).astype(BF16)
-        start()
-        got_ref[me] = mine[pl.ds(me * shard, shard), :]
-
-    scatter_blocks(group // 4, part, sum_ref, r_sib, r_x, r_z, s_x, s_z, send, recv, produce, pause)
+    def work(k):
+        if k == 0:
+            slice_grad(1 - dp, theirs.at[0])
+            to_dp.start()
+            for payload in payloads:
+                payload.start()
+        elif k == 1:
+            slice_grad(dp, mine)
+        elif k == 2:
+            to_dp.wait_recv()
+            mine[...] = (mine[...].astype(F32) + theirs[1].astype(F32)).astype(BF16)
+            start()
+            got_ref[me] = mine[pl.ds(me * shard, shard), :]
+
+    scatter_blocks(
+        group // 4, part, sum_ref, r_sib, r_x, r_z, s_x, s_z, send, recv, produce, None, work
+    )
     finish_recv()
     finish_send()
     to_dp.wait_send()
-
-
-def unproject(low, w_all, normed, rows, shard, n_dp, cid):
+    for payload in payloads:
+        payload.wait()
+
+
+def unproject(low, w_all, normed, more, rows, shard, n_dp, cid):
     count, wide = low.shape
     width = w_all.shape[0]
     group = count // rows
@@ -700,9 +764,10 @@
         out_shape=[
             jax.ShapeDtypeStruct((rows, width), F32),
             jax.ShapeDtypeStruct((group, shard, wide), BF16),
+            jax.ShapeDtypeStruct((more.shape[0] // 2, more.shape[1]), more.dtype),
         ],
-        in_specs=[VMEM] * 3,
-        out_specs=[VMEM] * 2,
+        in_specs=[VMEM] * 3 + [HBM],
+        out_specs=[VMEM] * 2 + [HBM],
         scratch_shapes=[
             pltpu.VMEM((group, rows, width), BF16),
             *scatter_scratch(group, rows, width),
@@ -712,9 +777,11 @@
             DMA((group,)),
             DMA,
             DMA,
+            DMA,
+            DMA,
         ],
         compiler_params=params(cid),
-    )(low, w_all, normed)
+    )(low, w_all, normed, more)
 
 
 def swap_kernel(axes, sizes, in_ref, out_ref, send, recv, local):
@@ -805,12 +872,12 @@
     group, n_dp, cap,
     x_ref, cot_ref, gate_ref, gate_w, up_w, down_ref,
     rows_out, grads_out, hidden_out, gate_out, up_out, sent_out, row_out, gate_grads,
-    x_all, c_all, down_w, gates, stage,
-    x_send, x_recv, c_send, c_recv, g_send, g_recv, local, dp_send, dp_recv,
+    x_all, c_all, down_w, gates, picks, taken, grads, gate_pre_s, up_pre_s, hidden_s, gate_s, up_s, stage,
+    x_send, x_recv, c_send, c_recv, g_send, g_recv, local, dp_send, dp_recv, out_sems,
 ):
     me = lax.axis_index("expert")
     rows, width = x_ref.shape
-    pair = 2 * cap
+    pair, quad = 2 * cap, 4 * cap
     own = [
         pltpu.make_async_copy(x_ref, x_all.at[me], local.at[0]),
         pltpu.make_async_copy(cot_ref, c_all.at[me], local.at[1]),
@@ -828,78 +895,119 @@
     for copy in own:
         copy.wait()
 
-    def put(kind, p):
-        ref = (sent_out, row_out)[kind]
-        return pltpu.make_async_copy(
-            stage.at[kind], ref.at[pl.ds(p * 2 * rows, 2 * rows)], local.at[3 + kind]
-        )
+    def out(n, zz):
+        src = (taken, grads, hidden_s, gate_s, up_s, stage.at[0], stage.at[1])[n]
+        dst = (rows_out, grads_out, hidden_out, gate_out, up_out, sent_out, row_out)[n]
+        size = quad if n < 5 else 4 * rows
+        return pltpu.make_async_copy(src, dst.at[pl.ds(zz * size, size)], out_sems.at[n])
 
     lane = lax.broadcasted_iota(jnp.int32, (rows, rows), 1)
     row = lax.broadcasted_iota(jnp.int32, (rows, rows), 0)
     before = jnp.where(row < lane, 1.0, 0.0).astype(BF16)
-    slot = lax.broadcasted_iota(jnp.int32, (cap, rows), 0).astype(F32)
-
-    def run(p):
-        base = p * pair
-        picks, gate_cols = [], []
-        for i in range(2):
-            segment = p * 2 + i
-            gate_row = gates[segment]
-            routed = jnp.where(gate_row > 0.0, 1.0, 0.0)
-            rank = mm(jnp.broadcast_to(routed, (16, rows)).astype(BF16), before)[0:1, :]
-            pick = jnp.where((slot == rank) & (routed > 0.5), 1.0, 0.0)
-            gate_cols.append(jnp.sum(pick * gate_row, axis=1, keepdims=True))
-            pick_low = pick.astype(BF16)
-            picks.append((pick, pick_low))
-            here = pl.ds(base + i * cap, cap)
-            rows_out[here, :] = mm(pick_low, x_all[segment]).astype(BF16)
-            grads_out[here, :] = mm(pick_low, c_all[segment]).astype(BF16)
-        here = pl.ds(base, pair)
+    pick_row = lax.broadcasted_iota(jnp.int32, (pair, 2 * rows), 0)
+    pick_lane = lax.broadcasted_iota(jnp.int32, (pair, 2 * rows), 1)
+    together = (pick_row >= cap) == (pick_lane >= rows)
+    slot = jnp.where(pick_row >= cap, pick_row - cap, pick_row).astype(F32)
+
+    def gate_row(p):
+        return jnp.concatenate([gates[p * 2], gates[p * 2 + 1]], axis=1)
+
+    def forward(d, zz):
+        @pl.when(d > 0)
+        def _():
+            out(0, zz).wait()
+
+        for j in range(2):
+            p = zz * 2 + j
+            ranks = []
+            for i in range(2):
+                routed = jnp.where(gates[p * 2 + i] > 0.0, 1.0, 0.0)
+                ranks.append(mm(jnp.broadcast_to(routed, (16, rows)).astype(BF16), before)[0:1, :])
+            rank = jnp.concatenate(ranks, axis=1)
+            hit = together & (slot == rank) & (gate_row(p) > 0.0)
+            pick = jnp.where(hit, 1.0, 0.0).astype(BF16)
+            here = slice(j * pair, (j + 1) * pair)
+            picks[here, :] = pick
+            segments = x_all[pl.ds(p * 2, 2)].reshape(2 * rows, width)
+            taken[here, :] = mm(pick, segments).astype(BF16)
+        out(0, zz).start()
+        gate_pre_s[...] = mm(taken[...], gate_w[...])
+        up_pre_s[...] = mm(taken[...], up_w[...])
+
+    def backward(d, zz):
+        @pl.when(d > 0)
+        def _():
+            for n in range(1, 7):
+                out(n, zz).wait()
+
+        gate_cols = []
+        for j in range(2):
+            p = zz * 2 + j
+            here = slice(j * pair, (j + 1) * pair)
+            pick = picks[here, :]
+            gate_cols.append(jnp.sum(pick.astype(F32) * gate_row(p), axis=1, keepdims=True))
+            segments = c_all[pl.ds(p * 2, 2)].reshape(2 * rows, width)
+            grads[here, :] = mm(pick, segments).astype(BF16)
         gate_col = jnp.concatenate(gate_cols)
-        taken = rows_out[here, :]
-        gate_pre = mm(taken, gate_w[...])
-        up_pre = mm(taken, up_w[...])
+        gate_pre, up_pre = gate_pre_s[...], up_pre_s[...]
         sig = 1.0 / (1.0 + jnp.exp(-gate_pre))
         silu = gate_pre * sig
-        hidden = (silu * up_pre).astype(BF16)
-        hidden_out[here, :] = hidden
-        result = mm(hidden, down_w[...]).astype(BF16).astype(F32)
-        cot = grads_out[here, :].astype(F32)
-        dots = jnp.sum(cot * result, axis=1, keepdims=True)
-        sent = (gate_col * result).astype(BF16)
-        grads_out[here, :] = (gate_col * cot).astype(BF16)
-        for i, (pick, pick_low) in enumerate(picks):
-            part = slice(i * cap, (i + 1) * cap)
-            gate_grads[p * 2 + i] = jnp.sum(pick * dots[part], axis=0, keepdims=True)
-            stage[0, i * rows : (i + 1) * rows, :] = t_mm(pick_low, sent[part]).astype(BF16)
-        put(0, p).start()
-        hidden_grad = mm_t(grads_out[here, :], down_w[...]).astype(BF16).astype(F32)
+        hidden_s[...] = (silu * up_pre).astype(BF16)
+        out(2, zz).start()
+        dots = jnp.zeros((quad, 1), F32)
+        half = width // 2
+        for h in range(2):
+            cols = slice(h * half, (h + 1) * half)
+            result = mm(hidden_s[...], down_w[:, cols]).astype(BF16).astype(F32)
+            cot = grads[:, cols].astype(F32)
+            dots = dots + jnp.sum(cot * result, axis=1, keepdims=True)
+            grads[:, cols] = (gate_col * cot).astype(BF16)
+            sent = (gate_col * result).astype(BF16)
+            for j in range(2):
+                here = slice(j * pair, (j + 1) * pair)
+                there = slice(j * 2 * rows, (j + 1) * 2 * rows)
+                stage[0, there, cols] = t_mm(picks[here, :], sent[here]).astype(BF16)
+        out(1, zz).start()
+        out(5, zz).start()
+        for j in range(2):
+            here = slice(j * pair, (j + 1) * pair)
+            gate_grad = jnp.sum(picks[here, :].astype(F32) * dots[here], axis=0, keepdims=True)
+            for i in range(2):
+                gate_grads[(zz * 2 + j) * 2 + i] = gate_grad[:, i * rows : (i + 1) * rows]
+        hidden_grad = mm_t(grads[...], down_w[...]).astype(BF16).astype(F32)
         slope = sig * (1.0 + gate_pre * (1.0 - sig))
-        gate_pre_grad = (hidden_grad * up_pre * slope).astype(BF16)
-        up_pre_grad = (hidden_grad * silu).astype(BF16)
-        gate_out[here, :] = gate_pre_grad
-        up_out[here, :] = up_pre_grad
-        row_grad = (mm_t(gate_pre_grad, gate_w[...]) + mm_t(up_pre_grad, up_w[...])).astype(BF16)
-        for i, (_, pick_low) in enumerate(picks):
-            part = slice(i * cap, (i + 1) * cap)
-            stage[1, i * rows : (i + 1) * rows, :] = t_mm(pick_low, row_grad[part]).astype(BF16)
-        put(1, p).start()
-        put(0, p).wait()
-        put(1, p).wait()
-
-    def process(i, zz):
-        @pl.when(i == 0)
+        gate_s[...] = (hidden_grad * up_pre * slope).astype(BF16)
+        up_s[...] = (hidden_grad * silu).astype(BF16)
+        out(3, zz).start()
+        out(4, zz).start()
+        for h in range(2):
+            cols = slice(h * half, (h + 1) * half)
+            grad = mm_t(gate_s[...], gate_w[cols, :]) + mm_t(up_s[...], up_w[cols, :])
+            grad = grad.astype(BF16)
+            for j in range(2):
+                here = slice(j * pair, (j + 1) * pair)
+                there = slice(j * 2 * rows, (j + 1) * 2 * rows)
+                stage[1, there, cols] = t_mm(picks[here, :], grad[here]).astype(BF16)
+        out(6, zz).start()
+
+    first = lax.axis_index("expert") // 4
+
+    def process(d, zz):
+        @pl.when(zz == first)
         def _():
             finish_recv()
+
+        forward(d, zz)
+
+        @pl.when(zz == first)
+        def _():
             down_finish()
 
-        def one(j, carry):
-            run(zz * 2 + j)
-            return carry
-
-        lax.fori_loop(0, 2, one, 0)
+        backward(d, zz)
 
     gather_blocks(group // 4, [(x_all, x_send, x_recv), (c_all, c_send, c_recv)], process)
+    for n in range(7):
+        out(n, first).wait()
     finish_send()
 
 
@@ -908,6 +1016,7 @@
     rows, width = x.shape
     hidden = gate_w.shape[1]
     total = group * cap
+    quad = 4 * cap
 
     def shape(*dims, dtype=BF16):
         return jax.ShapeDtypeStruct(dims, dtype)
@@ -928,58 +1037,124 @@
             shape(*gates.shape, dtype=F32),
         ],
         in_specs=[HBM, HBM, VMEM, VMEM, VMEM, HBM],
-        out_specs=[VMEM] * 5 + [HBM, HBM, VMEM],
+        out_specs=[HBM] * 7 + [VMEM],
         scratch_shapes=[
             buffer(group, rows, width),
             buffer(group, rows, width),
             buffer(n_dp * down_w.shape[0], width),
             pltpu.VMEM(gates.shape, F32),
-            buffer(2, 2 * rows, width),
+            buffer(quad, 2 * rows),
+            buffer(quad, width),
+            buffer(quad, width),
+            pltpu.VMEM((quad, hidden), F32),
+            pltpu.VMEM((quad, hidden), F32),
+            buffer(quad, hidden),
+            buffer(quad, hidden),
+            buffer(quad, hidden),
+            buffer(2, 4 * rows, width),
             *gather_sems(group),
             *gather_sems(group),
             DMA((group,)),
             DMA((group,)),
-            DMA((5,)),
+            DMA((3,)),
             DMA,
             DMA,
+            DMA((7,)),
         ],
         compiler_params=pltpu.CompilerParams(
-            collective_id=cid, has_side_effects=True, vmem_limit_bytes=63 * 2**20
+            collective_id=cid, has_side_effects=True, vmem_limit_bytes=60 * 2**20
         ),
     )(x, cot, gates, gate_w, up_w, down_w)
 
 
 def collect_kernel(
-    group, n_dp, part, gate_ref, sum_ref, gates_ref,
-    r_sib, r_x, r_z, s_x, s_z, send, recv, g_send, g_recv,
+    group, n_dp,
+    part, gate_ref, taken, grads, hidden, gate_grad, up_grad,
+    sum_ref, gates_ref, gate_own, up_own, down_own, gate_dp, up_dp, down_dp, gate_in,
+    r_sib, r_x, r_z, s_x, s_z, send, recv, g_send, g_recv, tile, tile_low, sems, dp_send, dp_recv,
 ):
-    me = lax.axis_index("expert")
+    me, dp = lax.axis_index("expert"), lax.axis_index("dp")
     greet_all(group, n_dp)
     start, finish_recv, finish_send = tree_swap(
         group, lambda d, src: (gate_ref.at[d], gates_ref.at[src]), g_send, g_recv
     )
     start()
     gates_ref[me] = gate_ref[me]
+    step, wide = tile.shape
+
+    def product(left, right, own_out, dp_out, cols):
+        half = own_out.shape[0]
+        pieces = half // step
+
+        def one(i, carry):
+            there = pl.ds(i * step, step)
+            for whose, buffer, ref, sem in (
+                (1 - dp, tile_low, dp_out, sems.at[0]),
+                (dp, tile, own_out, sems.at[1]),
+            ):
+                rows = pl.ds(pl.multiple_of(whose * half + i * step, step), step)
+                buffer[...] = t_mm(left[:, rows], right[:, cols]).astype(buffer.dtype)
+                put = pltpu.make_async_copy(buffer, ref.at[there, cols], sem)
+                put.start()
+                put.wait()
+            return carry
+
+        lax.fori_loop(0, pieces, one, 0)
+
+    exchange = over_dp(gate_dp, gate_in, dp_send, dp_recv)
+
+    def work(k):
+        if k == 0:
+            product(taken, gate_grad, gate_own, gate_dp, slice(0, wide))
+            exchange.start()
+        elif k == 1:
+            product(taken, up_grad, up_own, up_dp, slice(0, wide))
+        elif k == 2:
+            for h in range(grads.shape[1] // wide):
+                product(hidden, grads, down_own, down_dp, slice(h * wide, (h + 1) * wide))
+
     scatter_blocks(
-        group // 4, part, sum_ref, r_sib, r_x, r_z, s_x, s_z, send, recv, lambda block: None
+        group // 4, part, sum_ref, r_sib, r_x, r_z, s_x, s_z, send, recv,
+        lambda block: None, None, work,
     )
     finish_recv()
     finish_send()
-
-
-def collect(parts, gates, n_dp, cid):
+    exchange.wait()
+
+
+def collect(parts, gates, taken, grads, hidden, gate_grad, up_grad, n_dp, cid):
     group, rows, width = parts.shape
+    narrow = hidden.shape[1]
+
+    def halves(a, b):
+        return a.shape[1] // n_dp, b.shape[1]
+
+    shapes = [halves(taken, gate_grad), halves(taken, up_grad), halves(hidden, grads)]
     return pl.pallas_call(
         functools.partial(collect_kernel, group, n_dp),
         out_shape=[
             jax.ShapeDtypeStruct((rows, width), F32),
             jax.ShapeDtypeStruct(gates.shape, gates.dtype),
+            *(jax.ShapeDtypeStruct(s, F32) for s in shapes),
+            *(jax.ShapeDtypeStruct(s, BF16) for s in shapes),
+            jax.ShapeDtypeStruct(shapes[0], BF16),
         ],
-        in_specs=[VMEM, VMEM],
-        out_specs=[VMEM, VMEM],
-        scratch_shapes=[*scatter_scratch(group, rows, width), DMA((group,)), DMA((group,))],
-        compiler_params=params(cid),
-    )(parts, gates)
+        in_specs=[VMEM] * 7,
+        out_specs=[VMEM, VMEM] + [HBM] * 7,
+        scratch_shapes=[
+            *scatter_scratch(group, rows, width),
+            DMA((group,)),
+            DMA((group,)),
+            pltpu.VMEM((256, narrow), F32),
+            pltpu.VMEM((256, narrow), BF16),
+            DMA((2,)),
+            DMA,
+            DMA,
+        ],
+        compiler_params=pltpu.CompilerParams(
+            collective_id=cid, has_side_effects=True, vmem_limit_bytes=60 * 2**20
+        ),
+    )(parts, gates, taken, grads, hidden, gate_grad, up_grad)
 
 
 def attention(queries, mask, keys, values):
@@ -1392,26 +1567,12 @@
     taken, taken_grad, hidden, gate_pre_grad, up_pre_grad, sent_out, row_grad, gate_grad = expert(
         normed_two, cotangent, gates_own.T[:, None], gate_w, up_w, w_down[0], n_dp, cap, 3
     )
-    expert_grad, gate_grad_own = collect(
-        row_grad.reshape(group, rows, width), gate_grad, n_dp, 4
-    )
-    sums = (
-        t_mm(taken, gate_pre_grad),
-        t_mm(taken, up_pre_grad),
-        t_mm(hidden, taken_grad),
+    expert_grad, gate_grad_own, gate_own, up_own, down_own, _, up_dp, down_dp, gate_in = collect(
+        row_grad.reshape(group, rows, width),
+        gate_grad, taken, taken_grad, hidden, gate_pre_grad, up_pre_grad, n_dp, 4,
     )
     gate_grad_own = gate_grad_own.reshape(group, rows).T
     combined = lax.psum_scatter(sent_out, "expert", scatter_dimension=0, tiled=True)
-    output = (residual + combined.astype(F32)).astype(BF16)
-
-    def dp_sum(total):
-        halves = total.reshape(n_dp, total.shape[0] // n_dp, -1)
-        theirs = lax.dynamic_index_in_dim(halves, 1 - dp, 0, keepdims=False).astype(BF16)
-        ours = lax.dynamic_index_in_dim(halves, dp, 0, keepdims=False)
-        theirs = lax.ppermute(theirs, "dp", [(d, 1 - d) for d in range(n_dp)])
-        return (ours + theirs.astype(F32))[None]
-
-    grad_gate, grad_up, grad_down = (dp_sum(s) for s in sums)
 
     prob_grad = jnp.where(routed, gate_grad_own, 0.0)
     logit_grad = (
@@ -1428,8 +1589,8 @@
     )
     proj_grad = residual_grad.astype(BF16)
 
-    query_grad, key_grad, value_grad, out_w_grad = attend_back(
-        proj_grad, queries, keys, values, bias, out_head, attn, lse, n_dp, 5
+    query_grad, key_grad, value_grad, out_w_grad, up_in, down_first = attend_back(
+        proj_grad, queries, keys, values, bias, out_head, attn, lse, up_dp, down_dp, n_dp, 5
     )
     query_turned = turn(query_grad * SCALE, cosine, -sine)
     key_turned = turn(key_grad * SCALE, cosine, -sine)
@@ -1439,11 +1600,16 @@
     query_low = query_scale * my_query_g * query_turned - query_pre * query_scale**3 * query_mean
     key_low = key_scale * my_key_g * key_turned - key_pre * key_scale**3 * key_mean
     low = jnp.concatenate([query_low, key_low, value_grad], axis=1).astype(BF16)
+    combined, low = lax.optimization_barrier((combined, low))
+    output = (residual + combined.astype(F32)).astype(BF16)
     query_gain_grad = jnp.sum(query_turned * query_pre * query_scale, axis=0)
     key_gain_grad = jnp.sum(key_turned * key_pre * key_scale, axis=0)
-    normed_grad, got = unproject(
-        low, w_all, normed_all.reshape(count, width), rows, shard, n_dp, 7
-    )
+    normed_grad, got, down_second = unproject(
+        low, w_all, normed_all.reshape(count, width), down_dp, rows, shard, n_dp, 7
+    )
+    grad_gate = (gate_own + gate_in.astype(F32))[None]
+    grad_up = (up_own + up_in.astype(F32))[None]
+    grad_down = (down_own + jnp.concatenate([down_first, down_second]).astype(F32))[None]
     attn_scale = inverse_rms(token_f)
     attn_gain_grad = jnp.sum(normed_grad * token_f * attn_scale, axis=0)
     weighted = normed_grad * attn_g

time: 900 us -> 763 us (0.85)
  Pallas kernels: 719 us -> 631 us
  matrix products: 29.5 us -> 5.04 us
  waiting for transfers between devices: 22.2 us -> 3.85 us
    pallas_call x1, Pallas kernels: 195 us -> 130 us  [expert(): pl.pallas_call(functools.partial(expert_kernel, group, n_dp, cap), out_sh...]
    dot_general x4 -> x1, matrix products: 24.8 us -> 1.23 us  [t_mm(): lax.dot_general(a, b, (((0,), (0,)), ((), ())), preferred_element_type=F32)]
    pallas_call x1, Pallas kernels: 98.6 us -> 76.4 us  [unproject(): pl.pallas_call(functools.partial(unproject_kernel, group, n_dp, shard), o...]
    pallas_call x1, Pallas kernels: 88 us -> 104 us  [collect(): pl.pallas_call(functools.partial(collect_kernel, group, n_dp), out_shape=...]
    ppermute x2, waiting for transfers between devices: 17.3 us -> 3.82 us  [per_head(): grad_out = grad_out + lax.ppermute(block, BOTH, pairs)]
    pallas_call x1, Pallas kernels: 100 us -> 89.5 us  [attend_back(): pl.pallas_call(functools.partial(attend_back_kernel, group, n_dp), out_sh...]
    pallas_call x1, Pallas kernels: 121 us -> 112 us  [project(): pl.pallas_call(functools.partial(project_kernel, group, n_dp, shard), out...]
  transfers between devices with their start and end apart: 8 -> 5, of which waited for: 3 -> 1; matrix products, arithmetic and copies ran while one was open for 10% -> 9% of each run, Pallas kernels for 26% -> 44%
where the time goes in v3:
time: 763 us; the launch traced here: 753 us
  Pallas kernels  631 us (83%)
  other arithmetic  56.9 us (7%)
  local copies, waits for them, and re-layouts  29.3 us (4%)
  between operations  15 us (2%)
  starting transfers between devices  12 us (2%)
    pallas_call x1, Pallas kernels, expert(): pl.pallas_call(functools.partial(expert_kernel, group, n_dp, cap), out_sh...  130 us
    pallas_call x1, Pallas kernels, project(): pl.pallas_call(functools.partial(project_kernel, group, n_dp, shard), out...  112 us
    pallas_call x1, Pallas kernels, collect(): pl.pallas_call(functools.partial(collect_kernel, group, n_dp), out_shape=...  104 us
    pallas_call x1, Pallas kernels, attend_back(): pl.pallas_call(functools.partial(attend_back_kernel, group, n_dp), out_sh...  89.5 us
    pallas_call x1, Pallas kernels, unproject(): pl.pallas_call(functools.partial(unproject_kernel, group, n_dp, shard), o...  76.4 us
    pallas_call x1, Pallas kernels, attend(): pl.pallas_call(functools.partial(attend_kernel, group, n_dp), out_shape=[...  74 us
    pallas_call x3, Pallas kernels, swap(): pl.pallas_call(functools.partial(swap_kernel, axes, sizes), out_shape=jax...  45.4 us
  transfers between devices with their start and end apart: 5, of which 1 were waited for; matrix products, arithmetic and copies ran while one was open for 9% of the time, Pallas kernels for 44%

profile of v3, /device:TPU:4, one launch (start us, length us, event | category | flops | bytes accessed | tf_op | source)
XLA Modules:
  0.0 752.7 jit_solution(15497861160509709677)
XLA Ops:
  7.2 4.4 collective-permute-start
  11.7 1.6 collective-permute-start.1
  13.3 0.8 copy.73
  14.1 0.8 copy.74
  14.8 0.8 copy.75
  15.6 0.8 copy.76
  16.4 0.8 copy.77
  17.2 1.0 copy.86
  18.7 1.0 copy.85
  20.2 1.0 copy.84
  21.7 1.8 maximum_bitcast_fusion
  23.5 0.7 reshape.216
  24.4 1.1 pad_maximum_fusion.1.w_ref
  25.5 111.8 %shard_map.263 = (bf16[16,128,2048]{2,1,0:T(8,128)(2,1)}, f32[2048,384]{1,0:T(8,128)}, bf16[2048,512]{1,0:T(8,128)(2,1)}, f32[8,2048]{1,0:T(8,128)}, bf16[2048,1024]{1,0:T(8,128)(2,1)}) custom-call(bf16[128,2048]{1,0:T(8,128)(2,1)} %x_ref.1, bf16[16,64,512]{2,1,0:T(8,128)(2,1)} %pad_maximum_fusion.1.w_ref, bf16[1024,1024]{1,0:T(8,128)(2,1)} %bitcast.122), custom_call_target="tpu_custom_call" | custom-call | tf_op jit(solution)/shard_map/pallas_call | solution.py:525
  137.3 1.7 fusion.64
  139.0 2.2 multiply_reduce_fusion.8
  141.2 12.5 %shard_map.264 = f32[16,32,128]{2,1,0:T(8,128)S(1)} custom-call(f32[1,32,128]{2,1,0:T(8,128)S(1)} %reshape.217.in_ref), custom_call_target="tpu_custom_call" | custom-call | tf_op jit(solution)/shard_map/pallas_call | solution.py:855
  154.9 0.7 multiply_multiply_fusion
  155.6 5.8 fusion.31
  161.3 1.1 pad_maximum_fusion.4.q_ref
  162.5 0.8 slice.201.v_ref
  163.4 0.7 copy.98
  164.1 2.3 pad_maximum_fusion.5.k_ref
  166.4 1.3 fusion.46
  167.7 0.8 pad_maximum_fusion.6.w_ref
  168.6 74.0 %shard_map.265 = (f32[2048,128]{1,0:T(8,128)}, f32[2048,128]{1,0:T(8,128)}, f32[128,2048]{1,0:T(8,128)}, bf16[2048,1024]{1,0:T(8,128)(2,1)}) custom-call(bf16[2048,128]{1,0:T(8,128)(2,1)} %pad_maximum_fusion.4.q_ref, bf16[2048,128]{1,0:T(8,128)(2,1)} %pad_maximum_fusion.5.k_ref, bf16[2048,128]{1,0:T(8,128)(2,1)} %slice.201.v_ref, f32[16,2048]{1,0:T(8,128)} %bitcast.127, ...), custom_call_target="tpu_custom_call" | custom-call | tf_op jit(solution)/shard_map/pallas_call | solution.py:586
  242.6 1.7 multiply_reduce_fusion.6
  245.1 0.6 broadcast_select_fusion.1
  245.7 130.0 %shard_map.266 = (bf16[1536,2048]{1,0:T(8,128)(2,1)}, bf16[1536,2048]{1,0:T(8,128)(2,1)}, bf16[1536,1024]{1,0:T(8,128)(2,1)}, bf16[1536,1024]{1,0:T(8,128)(2,1)}...) custom-call(bf16[128,2048]{1,0:T(8,128)(2,1)} %copy-done.6, ...), custom_call_target="tpu_custom_call" | custom-call | tf_op jit(solution)/shard_map/pallas_call | solution.py:1027
  376.4 103.6 %shard_map.267 = (f32[128,2048]{1,0:T(8,128)}, f32[16,1,128]{2,1,0:T(1,128)}, f32[1024,1024]{1,0:T(8,128)}, f32[1024,1024]{1,0:T(8,128)}, f32[512,2048]{1,0:T(8,...) custom-call(bf16[16,128,2048]{2,1,0:T(8,128)(2,1)} %bitcast.119, ...), custom_call_target="tpu_custom_call" | custom-call | tf_op jit(solution)/shard_map/pallas_call | solution.py:1133
  480.0 0.8 multiply_reduce_fusion.9
  480.8 0.7 multiply_convert_fusion.1
  481.5 2.5 multiply_reduce_fusion
  484.0 1.5 fusion.62
  485.5 89.5 %shard_map.268 = (f32[2048,128]{1,0:T(8,128)}, f32[2048,128]{1,0:T(8,128)}, f32[2048,128]{1,0:T(8,128)}, f32[128,2048]{1,0:T(8,128)}, bf16[1024,1024]{1,0:T(8,128)(2,1)}, /*index=5*/bf16[256,2048]{1,0:T(8,128)(2,1)}) custom-call(bf16[128,2048]{1,0:T(8,128)(2,1)} %get-tuple-element.98.g_ref, bf16[2048,128]{1,0:T(8,128)(2,1)} %pad_maximum_fusion.4.q_ref, ...), custom_call_target="tpu_custom_call" | custom-call | tf_op jit(solution)/shard_map/pallas_call | solution.py:674
  575.0 2.2 convert.33
  577.2 1.3 broadcast_multiply_fusion
  578.6 4.5 fusion.24
  583.2 2.4 multiply_reduce_fusion.2
  585.6 11.6 %shard_map.269 = f32[16,32,128]{2,1,0:T(8,128)S(1)} custom-call(f32[1,32,128]{2,1,0:T(8,128)S(1)} %reshape.221.in_ref), custom_call_target="tpu_custom_call" | custom-call | tf_op jit(solution)/shard_map/pallas_call | solution.py:855
  597.3 2.4 dynamic-slice_bitcast_fusion
  599.7 2.3 collective-permute-start.2
  602.1 3.6 collective-permute-start.3
  606.2 1.2 fusion.66
  607.5 4.4 subtract_convert_fusion.1
  611.9 1.3 pad_maximum_fusion.low_ref
  613.2 0.8 copy-done.14
  614.0 2.7 add_bitcast_fusion.2
  617.0 0.6 copy.80
  617.7 0.9 copy.79
  618.6 5.3 add_bitcast_fusion.1
  623.9 3.8 collective-permute-done.3
  627.7 2.0 add.194
  629.8 76.4 %shard_map.270 = (f32[128,2048]{1,0:T(8,128)}, bf16[16,64,384]{2,1,0:T(8,128)(2,1)}, bf16[256,2048]{1,0:T(8,128)(2,1)}) custom-call(bf16[2048,384]{1,0:T(8,128)(2,1)} %pad_maximum_fusion.low_ref, bf16[2048,512]{1,0:T(8,128)(2,1)} %get-tuple-element.53.w_ref, bf16[2048,2048]{1,0:T(8,128)(2,1)} %bitcast.118, bf16[512,2048]{1,0:T(8,128)(2,1)} %get-tuple-element.69.more_ref), custom_call_target="tpu_custom_call" | custom-call | tf_op jit(solution)/shard_map/pallas_call | solution.py:762
  706.2 1.6 fusion.39
  708.0 21.3 %shard_map.271 = f32[32,20,64]{2,1,0:T(8,128)S(1)} custom-call(f32[32,20,64]{2,1,0:T(8,128)S(1)} %maximum_bitcast_fusion.1.in_ref), custom_call_target="tpu_custom_call" | custom-call | tf_op jit(solution)/shard_map/pallas_call | solution.py:855
  730.5 0.9 add_convert_fusion
  731.4 1.6 reshape.224
  733.0 4.6 fusion.63
  737.9 1.0 copy.97
  739.2 1.0 copy.96
  740.4 1.0 copy.95
  741.4 1.3 fusion.36
  743.1 2.6 add_bitcast_fusion
  (126 shorter events, 8.2 us)
Async XLA Ops:
  7.2 622.6 %reduce-scatter.2.cloned.1.call-start = ((), (), s32[]{:S(2)}) async-start(), calls=%async_computation.1 | async-start | bytes 8912896 | tf_op jit(solution)/shard_map/reduce_scatter | solution.py:1575
  7.2 159.2 %collective-permute-start = (bf16[64,2048]{1,0:T(8,128)(2,1)}, bf16[64,2048]{1,0:T(8,128)(2,1)}, u32[]{:S(2)}, u32[]{:S(2)}) collective-permute-start(bf16[64,2048]{1,0:T(8,128)(2,1)} %param.24), channel_id=1, source_target_pairs={{0,0},{1,16},{2,1},{3,17},{4,2},{5,18},{6,3},{7,19},{8,4},{9,20},{... | collective-permute-start | bytes 786440 | tf_op jit(solution)/shard_map/ppermute | solution.py:1531
  11.7 154.8 %collective-permute-start.1 = (bf16[64,2048]{1,0:T(8,128)(2,1)}, bf16[64,2048]{1,0:T(8,128)(2,1)}, u32[]{:S(2)}, u32[]{:S(2)}) collective-permute-start(bf16[64,2048]{1,0:T(8,128)(2,1)} %param.24), channel_id=1, source_target_pairs={{0,16},{1,0},{2,17},{3,1},{4,18},{5,2},{6,19},{7,3},{8,20},{9,4},{... | collective-permute-start | bytes 786440 | tf_op jit(solution)/shard_map/ppermute | solution.py:1531
  25.5 128.3 %copy-start.35 = (s32[32]{0:T(128)S(1)}, s32[32]{0:T(128)}, u32[]{:S(2)}) copy-start(s32[32]{0:T(128)} %param.31) | copy-start | bytes 388
  25.5 129.3 %copy-start.30 = (s32[128,8]{0,1:T(8,128)S(1)}, s32[128,8]{0,1:T(8,128)}, u32[]{:S(2)}) copy-start(s32[128,8]{0,1:T(8,128)} %param.30) | copy-start | bytes 12292
  137.3 17.6 %copy-start = (f32[2048,384]{1,0:T(8,128)S(1)}, f32[2048,384]{1,0:T(8,128)}, u32[]{:S(2)}) copy-start(f32[2048,384]{1,0:T(8,128)} %get-tuple-element.50) | copy-start | bytes 9437188
  154.8 428.3 %copy-start.28 = (f32[128]{0:T(128)}, f32[128]{0:T(128)S(1)}, u32[]{:S(2)}) copy-start(f32[128]{0:T(128)S(1)} %get-tuple-element.147) | copy-start | bytes 1540
  154.8 428.3 %copy-start.29 = (f32[128]{0:T(128)}, f32[128]{0:T(128)S(1)}, u32[]{:S(2)}) copy-start(f32[128]{0:T(128)S(1)} %get-tuple-element.148) | copy-start | bytes 1540
  166.4 76.1 %copy-start.7 = (bf16[128,2048]{1,0:T(8,128)(2,1)S(1)}, bf16[128,2048]{1,0:T(8,128)(2,1)}, u32[]{:S(2)}) copy-start(bf16[128,2048]{1,0:T(8,128)(2,1)} %x_ref.1) | copy-start | bytes 1572868
  242.6 1.9 copy-start.9
  244.4 1.3 copy-start.6
  480.0 4.0 copy-start.16
  481.5 4.0 copy-start.26
  575.0 3.5 copy-start.20
  578.6 4.6 copy-start.1
  583.1 2.4 copy-start.2
  583.1 2.4 copy-start.4
  597.3 10.2 %copy-start.3 = (f32[2048,64]{1,0:T(8,128)S(1)}, f32[2048,64]{1,0:T(8,128)}, u32[]{:S(2)}) copy-start(f32[2048,64]{1,0:T(8,128)} %copy-done.2) | copy-start | bytes 1572868
  597.3 10.2 %copy-start.5 = (f32[2048,64]{1,0:T(8,128)S(1)}, f32[2048,64]{1,0:T(8,128)}, u32[]{:S(2)}) copy-start(f32[2048,64]{1,0:T(8,128)} %copy-done.4) | copy-start | bytes 1572868
  599.7 24.1 %collective-permute-start.2 = (f32[64,2048]{1,0:T(8,128)}, f32[64,2048]{1,0:T(8,128)}, u32[]{:S(2)}, u32[]{:S(2)}) collective-permute-start(f32[64,2048]{1,0:T(8,128)} %get-tuple-element.118), channel_id=1, source_target_pairs={{0,0},{1,2},{2,4},{3,6},{4,8},{5,10},{6,12},{7,14},{8,16},{9,18},{... | collective-permute-start | bytes 1572872 | tf_op jit(solution)/shard_map/ppermute | solution.py:1632
  602.1 25.6 %collective-permute-start.3 = (f32[64,2048]{1,0:T(8,128)}, f32[64,2048]{1,0:T(8,128)}, u32[]{:S(2)}, u32[]{:S(2)}) collective-permute-start(f32[64,2048]{1,0:T(8,128)} %get-tuple-element.117), channel_id=1, source_target_pairs={{0,1},{1,3},{2,5},{3,7},{4,9},{5,11},{6,13},{7,15},{8,17},{9,19},{... | collective-permute-start | bytes 1572872 | tf_op jit(solution)/shard_map/ppermute | solution.py:1632
  607.5 4.4 copy-start.17
  607.5 5.7 copy-start.13
  611.8 2.2 copy-start.14
  614.0 2.8 copy-start.32
  614.0 2.8 copy-start.33
  614.0 2.8 copy-start.27
  614.0 4.6 copy-start.15
  629.7 76.4 %copy-start.8 = (bf16[128,2048]{1,0:T(8,128)(2,1)S(1)}, bf16[128,2048]{1,0:T(8,128)(2,1)}, u32[]{:S(2)}) copy-start(bf16[128,2048]{1,0:T(8,128)(2,1)} %x_ref.1) | copy-start | bytes 1572868
  629.7 76.4 %copy-start.25 = (f32[1,2048]{1,0:T(1,128)S(1)}, f32[1,2048]{1,0:T(1,128)}, u32[]{:S(2)}) copy-start(f32[1,2048]{1,0:T(1,128)} %get-tuple-element.122) | copy-start | bytes 24580
  629.7 76.5 %copy-start.31 = (f32[128]{0:T(128)S(1)}, f32[128]{0:T(128)}, u32[]{:S(2)}) copy-start(f32[128]{0:T(128)} %get-tuple-element.141) | copy-start | bytes 1540
  629.7 78.1 %copy-start.21 = (f32[16,32,64]{2,0,1:T(8,128)S(1)}, f32[16,32,64]{2,0,1:T(8,128)}, u32[]{:S(2)}) copy-start(f32[16,32,64]{2,0,1:T(8,128)} %copy.79) | copy-start | bytes 393220
  629.8 78.1 %copy-start.24 = (f32[2,32,64]{2,0,1:T(2,128)S(1)}, f32[2,32,64]{2,0,1:T(2,128)}, u32[]{:S(2)}) copy-start(f32[2,32,64]{2,0,1:T(2,128)} %copy.80) | copy-start | bytes 49156
  706.1 24.3 %copy-start.23 = (bf16[128,2048]{1,0:T(8,128)(2,1)S(1)}, bf16[128,2048]{1,0:T(8,128)(2,1)}, u32[]{:S(2)}) copy-start(bf16[128,2048]{1,0:T(8,128)(2,1)} %reduce-scatter.2.cloned.1.call-done) | copy-start | bytes 1572868
  706.2 25.2 %copy-start.22 = (bf16[16,64,384]{2,1,0:T(8,128)(2,1)S(1)}, bf16[16,64,384]{2,1,0:T(8,128)(2,1)}, u32[]{:S(2)}) copy-start(bf16[16,64,384]{2,1,0:T(8,128)(2,1)} %get-tuple-element.77) | copy-start | bytes 2359300
  737.5 3.8 copy-start.10
  737.6 3.8 copy-start.11
  737.6 3.8 copy-start.34
  739.2 3.6 copy-start.19
  740.1 2.6 copy-start.12
  740.1 2.9 copy-start.18
Sparse Core Ops, SparseCore 0:
  375.9 147.2 reduce-scatter.1

commit v4 on v3

--- a/solution.py
+++ b/solution.py
@@ -695,8 +695,8 @@
 def unproject_kernel(
     group, n_dp, shard,
     low_ref, w_ref, normed_ref, more_ref,
-    sum_ref, got_ref, more_out,
-    part, r_sib, r_x, r_z, s_x, s_z, send, recv,
+    sum_ref, wq_ref, wk_ref, wv_ref, more_out,
+    got_ref, part, r_sib, r_x, r_z, s_x, s_z, send, recv,
     mine, theirs, w_send, w_recv, dp_send, dp_recv, pay_send, pay_recv,
 ):
     me, dp = lax.axis_index("expert"), lax.axis_index("dp")
@@ -749,6 +749,10 @@
         group // 4, part, sum_ref, r_sib, r_x, r_z, s_x, s_z, send, recv, produce, None, work
     )
     finish_recv()
+    for e in range(group):
+        for n, ref in enumerate((wq_ref, wk_ref, wv_ref)):
+            cols = slice(n * HEAD_DIM, (n + 1) * HEAD_DIM)
+            ref[:, e * HEAD_DIM : (e + 1) * HEAD_DIM] = got_ref[e, :, cols].astype(F32)
     finish_send()
     to_dp.wait_send()
     for payload in payloads:
@@ -763,12 +767,13 @@
         functools.partial(unproject_kernel, group, n_dp, shard),
         out_shape=[
             jax.ShapeDtypeStruct((rows, width), F32),
-            jax.ShapeDtypeStruct((group, shard, wide), BF16),
+            *(jax.ShapeDtypeStruct((shard, width), F32) for _ in range(3)),
             jax.ShapeDtypeStruct((more.shape[0] // 2, more.shape[1]), more.dtype),
         ],
         in_specs=[VMEM] * 3 + [HBM],
-        out_specs=[VMEM] * 2 + [HBM],
+        out_specs=[VMEM] * 4 + [HBM],
         scratch_shapes=[
+            pltpu.VMEM((group, shard, wide), BF16),
             pltpu.VMEM((group, rows, width), BF16),
             *scatter_scratch(group, rows, width),
             pltpu.VMEM((group * shard, wide), BF16),
@@ -1604,7 +1609,7 @@
     output = (residual + combined.astype(F32)).astype(BF16)
     query_gain_grad = jnp.sum(query_turned * query_pre * query_scale, axis=0)
     key_gain_grad = jnp.sum(key_turned * key_pre * key_scale, axis=0)
-    normed_grad, got, down_second = unproject(
+    normed_grad, grad_query, grad_key, grad_value, down_second = unproject(
         low, w_all, normed_all.reshape(count, width), down_dp, rows, shard, n_dp, 7
     )
     grad_gate = (gate_own + gate_in.astype(F32))[None]
@@ -1619,8 +1624,6 @@
         - token_f * attn_scale**3 * jnp.mean(weighted * token_f, axis=-1, keepdims=True)
     )
 
-    got = got.reshape(group, shard, 3, HEAD_DIM).transpose(2, 1, 0, 3).reshape(3, shard, width)
-    got = got.astype(F32)
     grad_out = jnp.zeros((shard, width), F32)
     halves = out_w_grad.reshape(n_dp, shard, width)
     for r in range(n_dp):
@@ -1644,9 +1647,9 @@
         small[experts],
         small[experts + 1],
         small[experts + 2],
-        got[0],
-        got[1],
-        got[2],
+        grad_query,
+        grad_key,
+        grad_value,
         grad_out,
         small[:experts].T,
         grad_gate,

time: 763 us -> 762 us (level)
  no operation moved by 1% of the time
where the time goes in v4:
time: 762 us; the launch traced here: 751 us
  Pallas kernels  631 us (83%)
  other arithmetic  61.2 us (8%)
  local copies, waits for them, and re-layouts  23.7 us (3%)
  between operations  15.2 us (2%)
  starting transfers between devices  12 us (2%)
    pallas_call x1, Pallas kernels, expert(): pl.pallas_call(functools.partial(expert_kernel, group, n_dp, cap), out_sh...  130 us
    pallas_call x1, Pallas kernels, project(): pl.pallas_call(functools.partial(project_kernel, group, n_dp, shard), out...  112 us
    pallas_call x1, Pallas kernels, collect(): pl.pallas_call(functools.partial(collect_kernel, group, n_dp), out_shape=...  104 us
    pallas_call x1, Pallas kernels, attend_back(): pl.pallas_call(functools.partial(attend_back_kernel, group, n_dp), out_sh...  89.5 us
    pallas_call x1, Pallas kernels, unproject(): pl.pallas_call(functools.partial(unproject_kernel, group, n_dp, shard), o...  76.6 us
    pallas_call x1, Pallas kernels, attend(): pl.pallas_call(functools.partial(attend_kernel, group, n_dp), out_shape=[...  73.9 us
    pallas_call x3, Pallas kernels, swap(): pl.pallas_call(functools.partial(swap_kernel, axes, sizes), out_shape=jax...  45.5 us
  transfers between devices with their start and end apart: 5, of which 1 were waited for; matrix products, arithmetic and copies ran while one was open for 9% of the time, Pallas kernels for 44%

profile of v4, /device:TPU:4, one launch (start us, length us, event | category | flops | bytes accessed | tf_op | source)
XLA Modules:
  0.0 751.5 jit_solution(3249838365224645503)
XLA Ops:
  7.2 4.4 collective-permute-start
  11.7 1.6 collective-permute-start.1
  13.3 0.8 copy.55
  14.1 0.8 copy.56
  14.8 0.8 copy.57
  15.6 0.8 copy.58
  16.4 0.8 copy.59
  17.2 1.0 copy.65
  18.7 1.0 copy.64
  20.2 1.0 copy.63
  21.7 1.8 maximum_bitcast_fusion
  23.5 0.7 reshape.205
  24.4 1.1 pad_maximum_fusion.1.w_ref
  25.5 111.8 %shard_map.263 = (bf16[16,128,2048]{2,1,0:T(8,128)(2,1)}, f32[2048,384]{1,0:T(8,128)}, bf16[2048,512]{1,0:T(8,128)(2,1)}, f32[8,2048]{1,0:T(8,128)}, bf16[2048,1024]{1,0:T(8,128)(2,1)}) custom-call(bf16[128,2048]{1,0:T(8,128)(2,1)} %x_ref.1, bf16[16,64,512]{2,1,0:T(8,128)(2,1)} %pad_maximum_fusion.1.w_ref, bf16[1024,1024]{1,0:T(8,128)(2,1)} %bitcast.105), custom_call_target="tpu_custom_call" | custom-call | tf_op jit(solution)/shard_map/pallas_call | solution.py:525
  137.3 1.7 fusion.63
  139.0 2.2 multiply_reduce_fusion.8
  141.2 12.5 %shard_map.264 = f32[16,32,128]{2,1,0:T(8,128)S(1)} custom-call(f32[1,32,128]{2,1,0:T(8,128)S(1)} %reshape.206.in_ref), custom_call_target="tpu_custom_call" | custom-call | tf_op jit(solution)/shard_map/pallas_call | solution.py:860
  154.9 0.7 multiply_multiply_fusion
  155.6 5.8 fusion.31
  161.4 1.1 pad_maximum_fusion.4.q_ref
  162.6 0.8 slice.183.v_ref
  163.5 0.7 copy.68
  164.2 2.3 pad_maximum_fusion.5.k_ref
  166.5 1.3 fusion.46
  167.8 0.8 pad_maximum_fusion.6.w_ref
  168.6 73.9 %shard_map.265 = (f32[2048,128]{1,0:T(8,128)}, f32[2048,128]{1,0:T(8,128)}, f32[128,2048]{1,0:T(8,128)}, bf16[2048,1024]{1,0:T(8,128)(2,1)}) custom-call(bf16[2048,128]{1,0:T(8,128)(2,1)} %pad_maximum_fusion.4.q_ref, bf16[2048,128]{1,0:T(8,128)(2,1)} %pad_maximum_fusion.5.k_ref, bf16[2048,128]{1,0:T(8,128)(2,1)} %slice.183.v_ref, f32[16,2048]{1,0:T(8,128)} %bitcast.107, ...), custom_call_target="tpu_custom_call" | custom-call | tf_op jit(solution)/shard_map/pallas_call | solution.py:586
  242.6 1.7 multiply_reduce_fusion.6
  245.7 130.1 %shard_map.266 = (bf16[1536,2048]{1,0:T(8,128)(2,1)}, bf16[1536,2048]{1,0:T(8,128)(2,1)}, bf16[1536,1024]{1,0:T(8,128)(2,1)}, bf16[1536,1024]{1,0:T(8,128)(2,1)}...) custom-call(bf16[128,2048]{1,0:T(8,128)(2,1)} %copy-done.6, ...), custom_call_target="tpu_custom_call" | custom-call | tf_op jit(solution)/shard_map/pallas_call | solution.py:1032
  376.4 103.6 %shard_map.267 = (f32[128,2048]{1,0:T(8,128)}, f32[16,1,128]{2,1,0:T(1,128)}, f32[1024,1024]{1,0:T(8,128)}, f32[1024,1024]{1,0:T(8,128)}, f32[512,2048]{1,0:T(8,...) custom-call(bf16[16,128,2048]{2,1,0:T(8,128)(2,1)} %bitcast.103, ...), custom_call_target="tpu_custom_call" | custom-call | tf_op jit(solution)/shard_map/pallas_call | solution.py:1138
  480.0 0.8 multiply_reduce_fusion.9
  480.8 0.7 multiply_convert_fusion.1
  481.5 2.5 multiply_reduce_fusion
  484.0 1.5 fusion.62
  485.5 89.5 %shard_map.268 = (f32[2048,128]{1,0:T(8,128)}, f32[2048,128]{1,0:T(8,128)}, f32[2048,128]{1,0:T(8,128)}, f32[128,2048]{1,0:T(8,128)}, bf16[1024,1024]{1,0:T(8,128)(2,1)}, /*index=5*/bf16[256,2048]{1,0:T(8,128)(2,1)}) custom-call(bf16[128,2048]{1,0:T(8,128)(2,1)} %get-tuple-element.102.g_ref, bf16[2048,128]{1,0:T(8,128)(2,1)} %pad_maximum_fusion.4.q_ref, ...), custom_call_target="tpu_custom_call" | custom-call | tf_op jit(solution)/shard_map/pallas_call | solution.py:674
  575.1 2.2 convert.31
  577.2 1.3 broadcast_multiply_fusion
  578.7 4.5 fusion.24
  583.3 2.4 multiply_reduce_fusion.2
  585.7 11.7 %shard_map.269 = f32[16,32,128]{2,1,0:T(8,128)S(1)} custom-call(f32[1,32,128]{2,1,0:T(8,128)S(1)} %reshape.210.in_ref), custom_call_target="tpu_custom_call" | custom-call | tf_op jit(solution)/shard_map/pallas_call | solution.py:860
  597.4 2.4 dynamic-slice_bitcast_fusion
  599.8 2.3 collective-permute-start.2
  602.1 3.6 collective-permute-start.3
  606.3 1.2 fusion.65
  607.5 4.4 subtract_convert_fusion.1
  611.9 1.3 pad_maximum_fusion.low_ref
  613.3 0.8 copy-done.13
  614.1 2.7 add_bitcast_fusion.2
  616.9 0.7 concatenate.53
  618.4 0.9 copy.61
  619.2 5.3 add_bitcast_fusion.1
  624.5 3.3 collective-permute-done.3
  627.8 2.0 add.194
  629.9 76.6 %shard_map.270 = (f32[128,2048]{1,0:T(8,128)}, f32[64,2048]{1,0:T(8,128)}, f32[64,2048]{1,0:T(8,128)}, f32[64,2048]{1,0:T(8,128)}, bf16[256,2048]{1,0:T(8,128)(2,1)}) custom-call(bf16[2048,384]{1,0:T(8,128)(2,1)} %pad_maximum_fusion.low_ref, bf16[2048,512]{1,0:T(8,128)(2,1)} %get-tuple-element.55.w_ref, bf16[2048,2048]{1,0:T(8,128)(2,1)} %bitcast.102, ...), custom_call_target="tpu_custom_call" | custom-call | tf_op jit(solution)/shard_map/pallas_call | solution.py:766
  706.5 2.1 fusion.39
  708.8 21.3 %shard_map.271 = f32[32,20,64]{2,1,0:T(8,128)S(1)} custom-call(f32[32,20,64]{2,1,0:T(8,128)S(1)} %maximum_bitcast_fusion.1.in_ref), custom_call_target="tpu_custom_call" | custom-call | tf_op jit(solution)/shard_map/pallas_call | solution.py:860
  730.7 1.4 slice_bitcast_fusion.1
  732.2 1.5 slice_bitcast_fusion
  733.7 0.9 add_convert_fusion
  734.6 0.7 broadcast_multiply_fusion.2
  735.2 2.5 fusion.36
  737.8 4.0 add_bitcast_fusion
  741.8 0.8 copy.73
  742.6 0.8 copy.74
  743.4 0.8 copy.75
  (123 shorter events, 7.5 us)
Async XLA Ops:
  7.2 622.6 %reduce-scatter.2.cloned.1.call-start = ((), (), s32[]{:S(2)}) async-start(), calls=%async_computation.1 | async-start | bytes 8912896 | tf_op jit(solution)/shard_map/reduce_scatter | solution.py:1580
  7.2 159.3 %collective-permute-start = (bf16[64,2048]{1,0:T(8,128)(2,1)}, bf16[64,2048]{1,0:T(8,128)(2,1)}, u32[]{:S(2)}, u32[]{:S(2)}) collective-permute-start(bf16[64,2048]{1,0:T(8,128)(2,1)} %param.24), channel_id=1, source_target_pairs={{0,0},{1,16},{2,1},{3,17},{4,2},{5,18},{6,3},{7,19},{8,4},{9,20},{... | collective-permute-start | bytes 786440 | tf_op jit(solution)/shard_map/ppermute | solution.py:1536
  11.7 154.8 %collective-permute-start.1 = (bf16[64,2048]{1,0:T(8,128)(2,1)}, bf16[64,2048]{1,0:T(8,128)(2,1)}, u32[]{:S(2)}, u32[]{:S(2)}) collective-permute-start(bf16[64,2048]{1,0:T(8,128)(2,1)} %param.24), channel_id=1, source_target_pairs={{0,16},{1,0},{2,17},{3,1},{4,18},{5,2},{6,19},{7,3},{8,20},{9,4},{... | collective-permute-start | bytes 786440 | tf_op jit(solution)/shard_map/ppermute | solution.py:1536
  25.5 128.4 %copy-start.36 = (s32[32]{0:T(128)S(1)}, s32[32]{0:T(128)}, u32[]{:S(2)}) copy-start(s32[32]{0:T(128)} %param.31) | copy-start | bytes 388
  25.5 129.4 %copy-start.31 = (s32[128,8]{0,1:T(8,128)S(1)}, s32[128,8]{0,1:T(8,128)}, u32[]{:S(2)}) copy-start(s32[128,8]{0,1:T(8,128)} %param.30) | copy-start | bytes 12292
  137.3 17.6 %copy-start = (f32[2048,384]{1,0:T(8,128)S(1)}, f32[2048,384]{1,0:T(8,128)}, u32[]{:S(2)}) copy-start(f32[2048,384]{1,0:T(8,128)} %get-tuple-element.52) | copy-start | bytes 9437188
  154.9 428.3 %copy-start.29 = (f32[128]{0:T(128)}, f32[128]{0:T(128)S(1)}, u32[]{:S(2)}) copy-start(f32[128]{0:T(128)S(1)} %get-tuple-element.148) | copy-start | bytes 1540
  154.9 428.3 %copy-start.30 = (f32[128]{0:T(128)}, f32[128]{0:T(128)S(1)}, u32[]{:S(2)}) copy-start(f32[128]{0:T(128)S(1)} %get-tuple-element.149) | copy-start | bytes 1540
  166.5 76.1 %copy-start.7 = (bf16[128,2048]{1,0:T(8,128)(2,1)S(1)}, bf16[128,2048]{1,0:T(8,128)(2,1)}, u32[]{:S(2)}) copy-start(bf16[128,2048]{1,0:T(8,128)(2,1)} %x_ref.1) | copy-start | bytes 1572868
  242.5 1.9 copy-start.9
  244.4 1.3 copy-start.6
  480.0 4.0 copy-start.15
  481.5 4.0 copy-start.27
  575.1 3.5 copy-start.18
  578.7 4.6 copy-start.1
  583.2 2.4 copy-start.2
  583.2 2.4 copy-start.4
  597.4 10.1 %copy-start.3 = (f32[2048,64]{1,0:T(8,128)S(1)}, f32[2048,64]{1,0:T(8,128)}, u32[]{:S(2)}) copy-start(f32[2048,64]{1,0:T(8,128)} %copy-done.2) | copy-start | bytes 1572868
  597.4 10.1 %copy-start.5 = (f32[2048,64]{1,0:T(8,128)S(1)}, f32[2048,64]{1,0:T(8,128)}, u32[]{:S(2)}) copy-start(f32[2048,64]{1,0:T(8,128)} %copy-done.4) | copy-start | bytes 1572868
  599.8 24.7 %collective-permute-start.2 = (f32[64,2048]{1,0:T(8,128)}, f32[64,2048]{1,0:T(8,128)}, u32[]{:S(2)}, u32[]{:S(2)}) collective-permute-start(f32[64,2048]{1,0:T(8,128)} %get-tuple-element.119), channel_id=1, source_target_pairs={{0,0},{1,2},{2,4},{3,6},{4,8},{5,10},{6,12},{7,14},{8,16},{9,18},{... | collective-permute-start | bytes 1572872 | tf_op jit(solution)/shard_map/ppermute | solution.py:1635
  602.1 25.6 %collective-permute-start.3 = (f32[64,2048]{1,0:T(8,128)}, f32[64,2048]{1,0:T(8,128)}, u32[]{:S(2)}, u32[]{:S(2)}) collective-permute-start(f32[64,2048]{1,0:T(8,128)} %get-tuple-element.118), channel_id=1, source_target_pairs={{0,1},{1,3},{2,5},{3,7},{4,9},{5,11},{6,13},{7,15},{8,17},{9,19},{... | collective-permute-start | bytes 1572872 | tf_op jit(solution)/shard_map/ppermute | solution.py:1635
  607.5 4.4 copy-start.16
  607.5 5.7 copy-start.12
  611.9 2.2 copy-start.13
  614.1 2.8 copy-start.33
  614.1 2.8 copy-start.34
  614.1 2.8 copy-start.28
  614.1 5.2 copy-start.14
  629.8 76.7 %copy-start.8 = (bf16[128,2048]{1,0:T(8,128)(2,1)S(1)}, bf16[128,2048]{1,0:T(8,128)(2,1)}, u32[]{:S(2)}) copy-start(bf16[128,2048]{1,0:T(8,128)(2,1)} %x_ref.1) | copy-start | bytes 1572868
  629.8 76.7 %copy-start.25 = (f32[1,2048]{1,0:T(1,128)S(1)}, f32[1,2048]{1,0:T(1,128)}, u32[]{:S(2)}) copy-start(f32[1,2048]{1,0:T(1,128)} %get-tuple-element.123) | copy-start | bytes 24580
  629.8 76.7 %copy-start.32 = (f32[128]{0:T(128)S(1)}, f32[128]{0:T(128)}, u32[]{:S(2)}) copy-start(f32[128]{0:T(128)} %get-tuple-element.142) | copy-start | bytes 1540
  629.8 78.9 %copy-start.19 = (f32[16,32,64]{2,0,1:T(8,128)S(1)}, f32[16,32,64]{2,0,1:T(8,128)}, u32[]{:S(2)}) copy-start(f32[16,32,64]{2,0,1:T(8,128)} %copy.61) | copy-start | bytes 393220
  629.8 78.9 %copy-start.24 = (f32[2,32,64]{2,0,1:T(2,128)S(1)}, f32[2,32,64]{2,0,1:T(2,128)}, u32[]{:S(2)}) copy-start(f32[2,32,64]{2,0,1:T(2,128)} %copy.62) | copy-start | bytes 49156
  629.8 78.9 %copy-start.26 = (f32[1,32,64]{2,0,1:T(1,128)S(1)}, f32[1,32,64]{2,0,1:T(1,128)}, u32[]{:S(2)}) copy-start(f32[1,32,64]{2,0,1:T(1,128)} %concatenate.53) | copy-start | bytes 24580
  706.5 27.2 %copy-start.23 = (bf16[128,2048]{1,0:T(8,128)(2,1)S(1)}, bf16[128,2048]{1,0:T(8,128)(2,1)}, u32[]{:S(2)}) copy-start(bf16[128,2048]{1,0:T(8,128)(2,1)} %reduce-scatter.2.cloned.1.call-done) | copy-start | bytes 1572868
  706.5 28.8 %copy-start.10 = (f32[128,2048]{1,0:T(8,128)S(1)}, f32[128,2048]{1,0:T(8,128)}, u32[]{:S(2)}) copy-start(f32[128,2048]{1,0:T(8,128)} %get-tuple-element.103) | copy-start | bytes 3145732
  706.5 28.8 %copy-start.35 = (f32[128]{0:T(128)S(1)}, f32[128]{0:T(128)}, u32[]{:S(2)}) copy-start(f32[128]{0:T(128)} %get-tuple-element.141) | copy-start | bytes 1540
  730.7 7.0 copy-start.11
  730.7 7.0 copy-start.17
  737.8 4.0 copy-start.22
  737.8 4.8 copy-start.21
  737.8 5.6 copy-start.20
Sparse Core Ops, SparseCore 0:
  375.9 147.2 reduce-scatter.1
